TPU v7x, 512 devices: a whole 4x4x16 slice. The times are simulated.
512 devices in a mesh: grp: 16 (over y, x_hi, core), blk: 32 (over x_lo, z).
Axes of the slice: x: 4 (x_hi: 2, x_lo: 2; x = x_hi * 2 + x_lo), y: 4, z: 16, core: 2. Of those that a mesh axis runs over, the one named last changes fastest.
Arguments:
- queries: bfloat16 [16384, 5120], P(('grp', 'blk')), may hold values from -8 to 8
- page_table: int32 [16384, 4], P(('grp', 'blk')), may hold values from 0 to 24575, as said below
- suffix_len: int32 [16384], P(('grp', 'blk')), may hold values from 0 to 64
- place: int32 [24576], P('grp'), may hold values from 0 to 24575, as said below
- suffix_keys: bfloat16 [24576, 16, 1024], P(('grp', 'blk')), may hold values from -6 to 6
- suffix_values: bfloat16 [24576, 16, 1024], P(('grp', 'blk')), may hold values from -5 to 5
- prefix_keys: bfloat16 [1024, 1024], P('blk'), may hold values from -5 to 5
- prefix_values: bfloat16 [1024, 1024], P('blk'), may hold values from -5 to 5
Outputs:
- attention: bfloat16 [16384, 5120], P(('grp', 'blk'))
Inputs may be any that keep to these rules, and one draw needn't show every extreme that they name: `page_table`: only the first ceil(suffix_len[r] / 16) entries of row r are used, and used entries name distinct pages. The requests and pool rows held on one index of grp form a group; every entry of a request names a page number whose pool row place puts in its own group. Among the used entries of one device's requests, at most 2 name pages whose rows lie on any one other device of the group; in every draw some device has exactly 2 such pages on every other device of its group. `place`: A permutation of the page numbers that maps each group's page numbers onto that group's pool rows.
All inputs are finite; a program needn't handle non-finite values.
Results may differ from a plain program's by a relative error of at most 0.02.
Values may be sent and summed in bfloat16 or wider, within the bound.
No kernel may reach another device: no remote copies, remote signals or barrier semaphores. Data moves between devices by JAX's collectives and lax.ppermute only.
A program may use at most 128 MiB of HBM per device.

v0:
```python
import jax
import jax.numpy as jnp
from jax import lax
from jax.sharding import PartitionSpec as P

QH = 40
KVH = 8
HD = 128
CAP = 2


very_low = -1e30


def absorb(carry, scores, values, form):
    run_max, run_sum, run_acc = carry
    new_max = jnp.maximum(run_max, jnp.max(scores, axis=-1))
    weights = jnp.exp(scores - new_max[..., None])
    rescale = jnp.exp(run_max - new_max)
    run_sum = run_sum * rescale + jnp.sum(weights, axis=-1)
    product = jnp.einsum(
        form, weights.astype(jnp.bfloat16), values, preferred_element_type=jnp.float32
    )
    run_acc = run_acc * rescale[..., None] + product
    return (new_max, run_sum, run_acc)


def prefix_attend(head_rows, all_keys, all_values, scale):
    kv_heads = head_rows.shape[0]
    rows = head_rows.shape[1]
    length = all_keys.shape[0]
    carry = (
        jnp.full((kv_heads, rows), very_low, jnp.float32),
        jnp.zeros((kv_heads, rows), jnp.float32),
        jnp.zeros((kv_heads, rows, head_rows.shape[2]), jnp.float32),
    )
    for begin in range(0, length, 512):
        finish = min(length, begin + 512)
        key_block = all_keys[begin:finish].reshape(finish - begin, kv_heads, -1)
        value_block = all_values[begin:finish].reshape(finish - begin, kv_heads, -1)
        scores = (
            jnp.einsum("kmd,nkd->kmn", head_rows, key_block, preferred_element_type=jnp.float32)
            * scale
        )
        carry = absorb(carry, scores, value_block, "kmn,nkd->kmd")
    return carry


def body(
    queries, page_table, suffix_len, place, suffix_keys, suffix_values, prefix_keys, prefix_values
):
    requests = queries.shape[0]
    depth = page_table.shape[1]
    pool = suffix_keys.shape[0]
    page = suffix_keys.shape[1]
    width = suffix_keys.shape[2]
    group = QH // KVH
    scale = HD ** (-0.5)
    heads = queries.reshape(requests, KVH, group, HD)
    head_rows = heads.transpose(1, 0, 2, 3).reshape(KVH, requests * group, HD)
    all_keys, all_values = (
        lax.all_gather(prefix_keys, "blk", axis=0, tiled=True),
        lax.all_gather(prefix_values, "blk", axis=0, tiled=True),
    )
    pre_max, pre_sum, pre_acc = prefix_attend(head_rows, all_keys, all_values, scale)
    carry = (
        pre_max.reshape(KVH, requests, group).transpose(1, 0, 2),
        pre_sum.reshape(KVH, requests, group).transpose(1, 0, 2),
        pre_acc.reshape(KVH, requests, group, HD).transpose(1, 0, 2, 3),
    )
    devices = lax.axis_size("blk")
    mine = lax.axis_index("blk")
    base = lax.axis_index("grp") * devices * pool
    physical = place[page_table - base] - base
    holder = physical // pool
    slot = physical % pool
    entry = jnp.arange(depth, dtype=jnp.int32)
    used_pages = (suffix_len + page - 1) // page
    live = entry[None, :] < used_pages[:, None]
    remote = live & (holder != mine)
    local = live & (holder == mine)
    positions = jnp.arange(depth * page, dtype=jnp.int32)
    token_valid = positions[None, :] < suffix_len[:, None]
    entries = requests * depth
    flat_remote = remote.reshape(entries)
    flat_holder = jnp.where(flat_remote, holder.reshape(entries), devices)
    member = (flat_holder[:, None] == jnp.arange(devices, dtype=jnp.int32)[None, :]).astype(
        jnp.int32
    )
    rank = jnp.sum((jnp.cumsum(member, axis=0) - member) * member, axis=1)
    cells = devices * CAP
    target = jnp.where(flat_remote, flat_holder * CAP + rank, cells)
    select = (target[:, None] == jnp.arange(cells, dtype=jnp.int32)[None, :]).astype(jnp.int32)
    send_slot = jnp.sum(select * slot.reshape(entries)[:, None], axis=0).reshape(devices, CAP)
    asked = lax.all_to_all(send_slot, "blk", split_axis=0, concat_axis=0, tiled=True)
    got_keys = lax.all_to_all(suffix_keys[asked], "blk", split_axis=0, concat_axis=0, tiled=True)
    got_values = lax.all_to_all(
        suffix_values[asked], "blk", split_axis=0, concat_axis=0, tiled=True
    )
    pool_keys = jnp.concatenate([suffix_keys, got_keys.reshape(cells, page, width)], axis=0)
    pool_values = jnp.concatenate([suffix_values, got_values.reshape(cells, page, width)], axis=0)
    index = jnp.where(remote, pool + target.reshape(requests, depth), jnp.where(local, slot, 0))
    entry_keys = pool_keys[index].reshape(requests, depth * page, KVH, HD)
    entry_values = pool_values[index].reshape(requests, depth * page, KVH, HD)
    scores = (
        jnp.einsum("rkgd,rnkd->rkgn", heads, entry_keys, preferred_element_type=jnp.float32) * scale
    )
    scores = jnp.where(token_valid[:, None, None, :], scores, very_low)
    carry = absorb(carry, scores, entry_values, "rkgn,rnkd->rkgd")
    run_max, run_sum, run_acc = carry
    return (run_acc / run_sum[..., None]).astype(jnp.bfloat16).reshape(requests, QH * HD)


def solution(mesh):
    return jax.shard_map(
        body,
        mesh=mesh,
        in_specs=(
            P(("grp", "blk"), None),
            P(("grp", "blk"), None),
            P(("grp", "blk")),
            P("grp"),
            P(("grp", "blk"), None, None),
            P(("grp", "blk"), None, None),
            P("blk", None),
            P("blk", None),
        ),
        out_specs=P(("grp", "blk"), None),
        check_vma=False,
    )
```

profile of v0, /device:TPU:4, one launch (start us, length us, event | category | flops | bytes accessed | tf_op | source)
XLA Modules:
  0.0 434.6 jit_solution(12021402378725835866)
XLA Ops:
  8.3 1.1 gather_fusion
  10.2 29.2 %all_to_all.22 = s32[32,1,2]{2,1,0:T(1,128)S(1)} all-to-all(s32[32,1,2]{2,1,0:T(1,128)S(1)} %bitcast.66), channel_id=1, replica_groups=mesh['grp'=16,'blk'=32] {'blk'}, dimensions={0} | all-to-all | bytes 512 | tf_op jit(solution)/shard_map/all_to_all | solution.py:95
  39.7 2.0 gather_fusion.3
  41.8 4.9 %all-to-all-start.2 = ((bf16[32,2,16,1024]{3,2,1,0:T(8,128)(2,1)}), bf16[32,2,16,1024]{3,2,1,0:T(8,128)(2,1)}, u32[]{:S(2)}, u32[]{:S(2)}) async-start(bf16[32,2,16,1024]{3,2,1,0:T(8,128)(2,1)} %bitcast.55), calls=%async_computation.2 | async-start | bytes 4194304 | tf_op jit(solution)/shard_map/all_to_all | solution.py:97
  47.4 2.0 gather_fusion.1
  49.5 102.9 %all-to-all-done.2 = bf16[32,2,16,1024]{3,2,1,0:T(8,128)(2,1)} async-done(((bf16[32,2,16,1024]{3,2,1,0:T(8,128)(2,1)}), bf16[32,2,16,1024]{3,2,1,0:T(8,128)(2,1)}, u32[]{:S(2)}, u32[]{:S(2)}) %all-to-all-start.2) | async-done | bytes 2097184 | tf_op jit(solution)/shard_map/all_to_all | solution.py:97
  152.4 8.7 %all-to-all-start.1 = ((bf16[32,2,16,1024]{3,2,1,0:T(8,128)(2,1)}), bf16[32,2,16,1024]{3,2,1,0:T(8,128)(2,1)}, u32[]{:S(2)}, u32[]{:S(2)}) async-start(bf16[32,2,16,1024]{3,2,1,0:T(8,128)(2,1)} %bitcast.54), calls=%async_computation.1 | async-start | bytes 4194304 | tf_op jit(solution)/shard_map/all_to_all | solution.py:96
  161.2 0.7 all-gather.5.cloned.1.call-update
  163.7 67.6 %all-gather.3.cloned.1.call-done = bf16[1024,1024]{1,0:T(8,128)(2,1)} async-done(((bf16[32,1024]{1,0:T(8,128)(2,1)}), bf16[1024,1024]{1,0:T(8,128)(2,1)}) %all-gather.3.cloned.1.call-update) | async-done | bytes 2097168 | tf_op jit(solution)/shard_map/all_gather | solution.py:62
  231.3 1.7 fusion.62
  233.0 1.4 copy.122
  234.3 137.2 %all-gather.5.cloned.1.call-done = bf16[1024,1024]{1,0:T(8,128)(2,1)} async-done(((bf16[32,1024]{1,0:T(8,128)(2,1)}), bf16[1024,1024]{1,0:T(8,128)(2,1)}) %all-gather.5.cloned.1.call-update) | async-done | bytes 2097168 | tf_op jit(solution)/shard_map/all_gather | solution.py:63
  371.5 1.7 fusion.61
  373.2 1.3 copy.123
  374.6 1.3 copy.121
  375.9 1.3 copy.120
  377.2 1.8 multiply_reduce_fusion
  379.0 0.8 reduce_max.31
  379.8 3.2 multiply_reduce_fusion.1
  383.2 2.9 fusion.28
  387.9 3.0 fusion.4
  390.9 0.8 reduce_sum.55
  392.1 0.8 reduce_sum.57
  393.1 4.2 pad_maximum_fusion.1
  397.3 4.8 %gather_fusion.4 = bf16[128,16,1024]{2,1,0:T(8,128)(2,1)} fusion(bf16[112,16,1024]{2,1,0:T(8,128)(2,1)} %pad_maximum_fusion.1, s32[1024]{0:T(1024)S(1)} %pad_clamp_fusion), kind=kCustom, calls=%fused_computation.4 | custom fusion | bytes 8389120 | tf_op jit(solution)/shard_map/gather | solution.py:104
  402.1 5.3 %copy.125 = bf16[256,8,8,128]{3,2,1,0:T(8,128)(2,1)} copy(bf16[256,8,8,128]{3,1,2,0:T(8,128)(2,1)} %bitcast.53) | data formatting | bytes 8388608
  407.4 3.7 pad_maximum_fusion
  411.2 4.8 %gather_fusion.2 = bf16[128,16,1024]{2,1,0:T(8,128)(2,1)} fusion(bf16[112,16,1024]{2,1,0:T(8,128)(2,1)} %pad_maximum_fusion, s32[1024]{0:T(1024)S(1)} %pad_clamp_fusion), kind=kCustom, calls=%fused_computation.2 | custom fusion | bytes 8389120 | tf_op jit(solution)/shard_map/gather | solution.py:103
  416.0 3.3 copy.124
  419.4 2.4 fusion.63
  423.1 3.5 fusion.40
  426.6 1.1 reshape.332
  (75 shorter events, 9.0 us)
Async XLA Ops:
  6.5 1.8 copy-start
  8.3 31.4 %copy-start.2 = (bf16[48,16,1024]{2,1,0:T(8,128)(2,1)S(1)}, bf16[48,16,1024]{2,1,0:T(8,128)(2,1)}, u32[]{:S(2)}) copy-start(bf16[48,16,1024]{2,1,0:T(8,128)(2,1)} %param.13) | copy-start | bytes 4718596
  41.8 5.7 %copy-start.3 = (bf16[48,16,1024]{2,1,0:T(8,128)(2,1)S(1)}, bf16[48,16,1024]{2,1,0:T(8,128)(2,1)}, u32[]{:S(2)}) copy-start(bf16[48,16,1024]{2,1,0:T(8,128)(2,1)} %param.12) | copy-start | bytes 4718596
  41.8 110.6 %all-to-all-start.2 = ((bf16[32,2,16,1024]{3,2,1,0:T(8,128)(2,1)}), bf16[32,2,16,1024]{3,2,1,0:T(8,128)(2,1)}, u32[]{:S(2)}, u32[]{:S(2)}) async-start(bf16[32,2,16,1024]{3,2,1,0:T(8,128)(2,1)} %bitcast.55), calls=%async_computation.2 | async-start | bytes 4194304 | tf_op jit(solution)/shard_map/all_to_all | solution.py:97
  46.7 184.6 %all-gather.3.cloned.1.call-start = ((), (), s32[]{:S(2)}) async-start(), calls=%async_computation.3 | async-start | bytes 2162688 | tf_op jit(solution)/shard_map/all_gather | solution.py:62
  49.5 113.0 %copy-start.9 = (bf16[32,5120]{1,0:T(8,128)(2,1)S(1)}, bf16[32,5120]{1,0:T(8,128)(2,1)}, u32[]{:S(2)}) copy-start(bf16[32,5120]{1,0:T(8,128)(2,1)} %param.8) | copy-start | bytes 983044
  152.4 10.6 %copy-start.12 = (s32[32]{0:T(128)S(1)}, s32[32]{0:T(128)}, u32[]{:S(2)}) copy-start(s32[32]{0:T(128)} %param.10) | copy-start | bytes 388
  152.4 255.1 %all-to-all-start.1 = ((bf16[32,2,16,1024]{3,2,1,0:T(8,128)(2,1)}), bf16[32,2,16,1024]{3,2,1,0:T(8,128)(2,1)}, u32[]{:S(2)}, u32[]{:S(2)}) async-start(bf16[32,2,16,1024]{3,2,1,0:T(8,128)(2,1)} %bitcast.54), calls=%async_computation.1 | async-start | bytes 4194304 | tf_op jit(solution)/shard_map/all_to_all | solution.py:96
  161.1 210.4 %all-gather.5.cloned.1.call-start = ((), (), s32[]{:S(2)}) async-start(), calls=%async_computation.4 | async-start | bytes 2162688 | tf_op jit(solution)/shard_map/all_gather | solution.py:63
  162.9 0.8 copy-start.6
  383.0 3.1 copy-start.10
  383.1 3.1 copy-start.11
  383.2 3.0 copy-start.5
  386.2 1.7 copy-start.1
  387.9 4.1 copy-start.8
  402.1 5.3 %copy-start.4 = (bf16[48,16,1024]{2,1,0:T(8,128)(2,1)S(1)}, bf16[48,16,1024]{2,1,0:T(8,128)(2,1)}, u32[]{:S(2)}) copy-start(bf16[48,16,1024]{2,1,0:T(8,128)(2,1)} %param.12) | copy-start | bytes 4718596
  416.0 3.3 copy-start.7
Sparse Core Ops, SparseCore 0:
  49.6 181.5 all-gather.2
  233.3 138.1 all-gather.4
where the time goes:
time: 435 us
  waiting for transfers between devices  309 us (71%)
  local copies, waits for them, and re-layouts  40.5 us (9%)
  blocking collectives  29.2 us (7%)
  matrix products  14.4 us (3%)
  other arithmetic  13.8 us (3%)
  between operations  13.8 us (3%)
  starting transfers between devices  13.7 us (3%)
    all_gather x1, waiting for transfers between devices, body(): lax.all_gather(prefix_values, 'blk', axis=0, tiled=True)  137 us
    all_to_all x1, waiting for transfers between devices, body(): lax.all_to_all(suffix_values[asked], 'blk', split_axis=0, concat_axis=0,...  103 us
    all_gather x1, waiting for transfers between devices, body(): lax.all_gather(prefix_keys, 'blk', axis=0, tiled=True)  67.6 us
    all_to_all x1, blocking collectives, body(): lax.all_to_all(send_slot, 'blk', split_axis=0, concat_axis=0, tiled=True)  29.2 us
    unnamed x32, local copies, waits for them, and re-layouts  15.3 us
    all_to_all x1, starting transfers between devices, body(): lax.all_to_all(suffix_keys[asked], 'blk', split_axis=0, concat_axis=0, ti...  8.74 us
  transfers between devices with their start and end apart: 4, of which 3 were waited for; matrix products, arithmetic and copies ran while one was open for 10% of the time, Pallas kernels for 0%

commit v1 on v0

v1 whole, which is shorter than its diff:
```python
import functools

import jax
import jax.numpy as jnp
from jax import lax
from jax.experimental import pallas as pl
from jax.experimental.pallas import tpu as pltpu
from jax.sharding import PartitionSpec as P

QH = 40
KVH = 8
HD = 128
PAGE = 16
MAXP = 4
CAP = 2
GROUP = QH // KVH
QCOLS = QH * HD
SIDE = 128
ROW = QCOLS + SIDE
SHARE = 4
HEADS = QH // SHARE
BLOCK = HEADS * HD
KV = KVH // SHARE * HD
SCALE = HD ** (-0.5)
VERY_LOW = -1e30
F32 = jnp.float32
BF16 = jnp.bfloat16
MIB = 1 << 20


def iota(shape, axis):
    return lax.broadcasted_iota(jnp.int32, shape, axis)


def dot(a, b):
    return lax.dot_general(a, b, (((1,), (0,)), ((), ())), preferred_element_type=F32)


def dot_t(a, b):
    return lax.dot_general(a, b, (((1,), (1,)), ((), ())), preferred_element_type=F32)


def three_parts(x):
    hi = x.astype(BF16).astype(F32)
    mid = (x - hi).astype(BF16).astype(F32)
    lo = (x - hi - mid).astype(BF16).astype(F32)
    return hi, mid, lo


def route_kernel(
    pool, q_ref, table_ref, len_ref, place_ref, pk_ref, pv_ref,
    send_ref, local_ref, where_ref, *share_refs,
):
    requests = q_ref.shape[0]
    entries = requests * MAXP
    cells = send_ref.shape[0]
    devices = cells // CAP
    mine = lax.axis_index("blk")
    group = lax.axis_index("grp")
    base = group * (devices * pool)
    table = table_ref[...] - base
    page = jnp.concatenate([table[:, j : j + 1] for j in range(MAXP)], axis=0)
    place = (place_ref[...] - base).astype(F32)
    lane = iota((entries, 128), 1)
    found = jnp.zeros((entries, 128), F32)
    for k in range(place.shape[0]):
        found = found + jnp.where(page == lane + 128 * k, place[k : k + 1, :], 0.0)
    physical = jnp.sum(found, axis=1, keepdims=True)
    holder = jnp.floor((physical + 0.5) * (1.0 / pool))
    slot = physical - holder * pool
    row = jnp.broadcast_to(len_ref[...], (requests, requests)).astype(F32)
    square = iota((requests, requests), 0) == iota((requests, requests), 1)
    length = jnp.sum(jnp.where(square, row, 0.0), axis=1, keepdims=True)
    tokens = jnp.concatenate(
        [jnp.clip(length - PAGE * j, 0.0, PAGE) for j in range(MAXP)], axis=0
    )
    used = tokens > 0.0
    at_home = holder == mine.astype(F32)
    remote = jnp.where(used & jnp.logical_not(at_home), 1.0, 0.0)
    lane_f = lane.astype(F32)
    member = jnp.where(holder == lane_f, remote, 0.0)
    below = jnp.where(iota((entries, entries), 1) < iota((entries, entries), 0), 1.0, 0.0)
    before = dot(below.astype(BF16), member.astype(BF16))
    rank = jnp.sum(before * member, axis=1, keepdims=True)
    where = jnp.where(remote > 0.0, holder * CAP + rank, cells + slot)
    where = jnp.where(used, where, -1.0)
    where_ref[...] = jnp.broadcast_to(where, where_ref.shape)
    pick = jnp.where(where == lane_f, 1.0, 0.0).T
    picked = functools.reduce(
        jnp.add, [pick[:, requests * j : requests * (j + 1)] for j in range(MAXP)]
    ).astype(BF16)
    facts = jnp.where(lane == 0, slot, jnp.where(lane == 1, tokens, 0.0))
    side = dot(pick.astype(BF16), facts.astype(BF16)).astype(BF16)
    send_ref[:, QCOLS:ROW] = side[:cells]
    local_ref[:, QCOLS:ROW] = side[cells : cells + pool]
    for k in range(KVH):
        cols = slice(k * GROUP * HD, (k + 1) * GROUP * HD)
        rows = dot(picked, q_ref[:, cols]).astype(BF16)
        send_ref[:, cols] = rows[:cells]
        local_ref[:, cols] = rows[cells : cells + pool]
    turn, part = lax.rem(group, SHARE), lax.div(group, SHARE)
    kv_at = pl.ds(pl.multiple_of(turn * KV, KV), KV)
    prefix = jnp.concatenate([pk_ref[:, kv_at], pv_ref[:, kv_at]], axis=1)
    depth = prefix.shape[0] // (lax.axis_size("grp") // SHARE) // CAP
    at = iota((cells, prefix.shape[0]), 1)
    want = part * (CAP * depth) + depth * lax.rem(iota((cells, prefix.shape[0]), 0), CAP)
    for p in range(depth):
        one = jnp.where(at == want + p, 1.0, 0.0).astype(BF16)
        send_ref[:, ROW + 2 * KV * p : ROW + 2 * KV * (p + 1)] = dot(one, prefix).astype(BF16)
    for o, share_ref in enumerate(share_refs):
        turned = turn ^ o
        share_ref[...] = q_ref[:, pl.ds(pl.multiple_of(turned * BLOCK, 128), BLOCK)]


def pages_kernel(got_ref, local_ref, k_ref, v_ref, answer_ref, own_ref):
    cells = got_ref.shape[0]
    pool = k_ref.shape[0]
    step = 16
    facts = got_ref[:, QCOLS:ROW].astype(F32)
    lane = iota((cells, 128), 1).astype(F32)
    pick = jnp.where((facts[:, 0:1] == lane) & (facts[:, 1:2] > 0.0), 1.0, 0.0)
    fetch = pick.T[:pool].astype(BF16)
    pick = pick[:, :pool].astype(BF16)
    tokens = (dot(fetch, got_ref[:, QCOLS:ROW]) + local_ref[:, QCOLS:ROW].astype(F32))[:, 1:2]
    wide = (step, step * PAGE)
    column = iota(wide, 1)
    sums = [jnp.zeros((step, SIDE), F32) for _ in range(pool // step)]
    side_lane = iota((step, SIDE), 1)
    masks = []
    for g in range(pool // step):
        ok = (lax.div(column, PAGE) == iota(wide, 0)) & (
            lax.rem(column, PAGE).astype(F32) < tokens[step * g : step * (g + 1)]
        )
        bias = jnp.where(ok, 0.0, VERY_LOW)
        masks.append(jnp.concatenate([bias] * GROUP, axis=0))
    for k in range(KVH):
        base = k * GROUP * HD
        cols = slice(base, base + GROUP * HD)
        rows = (dot(fetch, got_ref[:, cols]) + local_ref[:, cols].astype(F32)).astype(BF16)
        for g in range(pool // step):
            span = slice(step * g, step * (g + 1))
            heads = jnp.concatenate(
                [rows[span, i * HD : (i + 1) * HD] for i in range(GROUP)], axis=0
            )
            keys = k_ref[span, :, k * HD : (k + 1) * HD].reshape(step * PAGE, HD)
            values = v_ref[span, :, k * HD : (k + 1) * HD].reshape(step * PAGE, HD)
            scores = dot_t(heads, keys) * SCALE + masks[g]
            top = jnp.max(scores, axis=1, keepdims=True)
            weights = jnp.exp(scores - top)
            total = jnp.sum(weights, axis=1, keepdims=True)
            mixture = (dot(weights.astype(BF16), values) / total).astype(BF16)
            log_sum = top + jnp.log(total)
            for i in range(GROUP):
                own_ref[span, base + i * HD : base + (i + 1) * HD] = mixture[step * i : step * (i + 1)]
                here = lax.rem(side_lane, QH) == k * GROUP + i
                sums[g] = jnp.where(here, log_sum[step * i : step * (i + 1)], sums[g])
    for g in range(pool // step):
        hi, mid, lo = three_parts(sums[g])
        side = jnp.where(side_lane < QH, hi, jnp.where(side_lane < 2 * QH, mid, lo))
        own_ref[step * g : step * (g + 1), QCOLS:ROW] = side.astype(BF16)
    for k in range(KVH):
        cols = slice(k * GROUP * HD, (k + 1) * GROUP * HD)
        answer_ref[:, cols] = dot(pick, own_ref[:, cols]).astype(BF16)
    answer_ref[:, QCOLS:ROW] = dot(pick, own_ref[:, QCOLS:ROW]).astype(BF16)


def prefix_kernel(q0, q1, q2, q3, kv_ref, o0, o1, o2, o3):
    requests = q0.shape[0]
    rows = requests * SHARE
    chunks = kv_ref.shape[1] // (2 * KV)
    lane = iota((rows, SIDE), 1)
    sums = jnp.zeros((rows, SIDE), F32)
    outs = (o0, o1, o2, o3)
    for h in range(HEADS):
        head = h // GROUP
        cols = slice(h * HD, (h + 1) * HD)
        heads = jnp.concatenate([q[:, cols] for q in (q0, q1, q2, q3)], axis=0)
        scores = [
            dot_t(heads, kv_ref[:, 2 * KV * p + head * HD : 2 * KV * p + (head + 1) * HD]) * SCALE
            for p in range(chunks)
        ]
        top = functools.reduce(jnp.maximum, scores)
        top = jnp.max(top, axis=1, keepdims=True)
        weights = [jnp.exp(s - top) for s in scores]
        total = jnp.sum(functools.reduce(jnp.add, weights), axis=1, keepdims=True)
        mixture = functools.reduce(
            jnp.add,
            [
                dot(
                    w.astype(BF16),
                    kv_ref[:, 2 * KV * p + KV + head * HD : 2 * KV * p + KV + (head + 1) * HD],
                )
                for p, w in enumerate(weights)
            ],
        )
        mixture = (mixture / total).astype(BF16)
        sums = jnp.where(lax.rem(lane, HEADS) == h, top + jnp.log(total), sums)
        for o, out in enumerate(outs):
            out[:, cols] = mixture[requests * o : requests * (o + 1)]
    hi, mid, lo = three_parts(sums)
    side = jnp.where(lane < HEADS, hi, jnp.where(lane < 2 * HEADS, mid, lo)).astype(BF16)
    for o, out in enumerate(outs):
        out[:, BLOCK:] = side[requests * o : requests * (o + 1)]


def join_kernel(got_ref, own_ref, where_ref, p0, p1, p2, p3, out_ref):
    entries = where_ref.shape[0]
    requests = p0.shape[0]
    cells = got_ref.shape[0]
    pool = own_ref.shape[0]
    lane = iota((entries, 128), 1)
    where = where_ref[...]
    pick = jnp.where(where == lane.astype(F32), 1.0, 0.0).astype(BF16)
    far, near = pick[:, :cells], pick[:, cells : cells + pool]
    side = dot(far, got_ref[:, QCOLS:ROW]) + dot(near, own_ref[:, QCOLS:ROW])
    sums = side + pltpu.roll(side, SIDE - QH, 1) + pltpu.roll(side, SIDE - 2 * QH, 1)
    sums = jnp.where(where >= 0.0, sums, VERY_LOW)
    turn = lax.rem(lax.axis_index("grp"), SHARE)
    for o, p_ref in enumerate((p0, p1, p2, p3)):
        turned = turn ^ o
        at = pl.multiple_of(turned * BLOCK, 128)
        cols = pl.ds(at, BLOCK)
        rows = dot(far, got_ref[:, cols]) + dot(near, own_ref[:, cols])
        moved = pltpu.roll(sums, lax.rem(SIDE - turned * HEADS, SIDE), 1)
        pre = p_ref[:, BLOCK:].astype(F32)
        pre = pre + pltpu.roll(pre, SIDE - HEADS, 1) + pltpu.roll(pre, SIDE - 2 * HEADS, 1)
        logs = [moved[requests * j : requests * (j + 1)] for j in range(MAXP)]
        top = functools.reduce(jnp.maximum, logs, pre)
        parts = [jnp.exp(x - top) for x in logs]
        part = jnp.exp(pre - top)
        total = functools.reduce(jnp.add, parts, part)
        parts = [x / total for x in parts]
        part = part / total
        for h in range(HEADS):
            here = slice(h * HD, (h + 1) * HD)
            mixture = part[:, h : h + 1] * p_ref[:, here].astype(F32)
            for j in range(MAXP):
                mixture = mixture + parts[j][:, h : h + 1] * rows[requests * j : requests * (j + 1), here]
            out_ref[:, pl.ds(pl.multiple_of(at + h * HD, 128), HD)] = mixture.astype(BF16)


def call(kernel, out_shape, flops, *args):
    return pl.pallas_call(
        kernel,
        out_shape=[jax.ShapeDtypeStruct(s, d) for s, d in out_shape],
        compiler_params=pltpu.CompilerParams(vmem_limit_bytes=40 * MIB),
        cost_estimate=pl.CostEstimate(flops=flops, bytes_accessed=4 * MIB, transcendentals=0),
    )(*args)


def body(
    queries, page_table, suffix_len, place, suffix_keys, suffix_values, prefix_keys, prefix_values
):
    requests = queries.shape[0]
    pool = suffix_keys.shape[0]
    devices = lax.axis_size("blk")
    group = lax.axis_size("grp")
    cells = devices * CAP
    rest = 2 * prefix_keys.shape[0] * KV // (group // SHARE) // CAP
    send, local, where, *shares = call(
        functools.partial(route_kernel, pool),
        [((cells, ROW + rest), BF16), ((pool, ROW), BF16), ((requests * MAXP, 128), F32)]
        + [((requests, BLOCK), BF16)] * SHARE,
        10**8,
        queries,
        page_table,
        suffix_len.reshape(1, requests),
        place.reshape(-1, 128),
        prefix_keys,
        prefix_values,
    )
    swap = lambda x, o: lax.ppermute(x, "grp", [(i, i ^ o) for i in range(group)]) if o else x
    got = lax.all_to_all(send, "blk", split_axis=0, concat_axis=0, tiled=True)
    strips = [[SHARE * y + t for y in range(group // SHARE)] for t in range(SHARE)]
    kv = lax.all_gather(got[:, ROW:], "grp", axis=0, tiled=True, axis_index_groups=strips)
    asked = [swap(x, o) for o, x in enumerate(shares)]
    answer, own = call(
        pages_kernel,
        [((cells, ROW), BF16), ((pool, ROW), BF16)],
        10**9,
        got,
        local,
        suffix_keys,
        suffix_values,
    )
    back = lax.all_to_all(answer, "blk", split_axis=0, concat_axis=0, tiled=True)
    served = call(
        prefix_kernel, [((requests, BLOCK + SIDE), BF16)] * SHARE, 10**9, *asked, kv
    )
    served = [swap(x, o) for o, x in enumerate(served)]
    (out,) = call(
        join_kernel, [((requests, QCOLS), BF16)], 10**8, back, own, where, *served
    )
    return out


def solution(mesh):
    return jax.shard_map(
        body,
        mesh=mesh,
        in_specs=(
            P(("grp", "blk"), None),
            P(("grp", "blk"), None),
            P(("grp", "blk")),
            P("grp"),
            P(("grp", "blk"), None, None),
            P(("grp", "blk"), None, None),
            P("blk", None),
            P("blk", None),
        ),
        out_specs=P(("grp", "blk"), None),
        check_vma=False,
    )
```

time: 435 us -> 165 us (0.38)
  the two profiles are of different devices: /device:TPU:4 before, /device:TPU:1 now
where the time goes in v1:
time: 165 us
  blocking collectives  62.4 us (38%)
  waiting for transfers between devices  29.6 us (18%)
  starting transfers between devices  29.2 us (18%)
  local copies, waits for them, and re-layouts  16.5 us (10%)
  between operations  13.6 us (8%)
  Pallas kernels  13.3 us (8%)
    all_to_all x1, blocking collectives, body(): got = lax.all_to_all(send, 'blk', split_axis=0, concat_axis=0, tiled=True)  62.4 us
    ppermute x6, starting transfers between devices, body(): lax.ppermute(x, 'grp', [(i, i ^ o) for i in range(group)])  20.4 us
    all_gather x1, waiting for transfers between devices, body(): lax.all_gather(got[:, ROW:], 'grp', axis=0, tiled=True, axis_index_groups...  18.3 us
    pallas_call x4, Pallas kernels, call(): pl.pallas_call(kernel, out_shape=[jax.ShapeDtypeStruct(s, d) for s, d in...  13.3 us
    ppermute x6, waiting for transfers between devices, body(): lax.ppermute(x, 'grp', [(i, i ^ o) for i in range(group)])  11.3 us
    unnamed x29, local copies, waits for them, and re-layouts  10.6 us
    all_to_all x1, starting transfers between devices, body(): lax.all_to_all(answer, 'blk', split_axis=0, concat_axis=0, tiled=True)  8.77 us
    all_to_all x2, local copies, waits for them, and re-layouts, body(): got = lax.all_to_all(send, 'blk', split_axis=0, concat_axis=0, tiled=True)  3.8 us
  transfers between devices with their start and end apart: 8, of which 5 were waited for; matrix products, arithmetic and copies ran while one was open for 0% of the time, Pallas kernels for 2%

profile of v1, /device:TPU:1, one launch (start us, length us, event | category | flops | bytes accessed | tf_op | source)
XLA Modules:
  0.0 164.6 jit_solution(17710135919409467766)
XLA Ops:
  6.5 0.8 copy.9.table_ref
  7.3 1.0 copy-done.6
  8.3 0.8 copy-done.7
  9.1 0.8 copy-done.8
  10.0 0.7 copy-done.9
  10.6 0.7 copy-done.10
  11.3 1.3 shard_map.82
  12.6 0.8 copy-done.2
  13.4 0.6 copy-done.12
  14.0 1.3 all_to_all.14
  15.4 62.4 %all_to_all.22 = bf16[32,2,7296]{2,1,0:T(2,128)(2,1)} all-to-all(bf16[32,2,7296]{2,1,0:T(2,128)(2,1)} %all_to_all.14), channel_id=1, replica_groups=mesh['grp'=16,'blk'=32] {'blk'}, dimensions={0} | all-to-all | bytes 1867776 | tf_op jit(solution)/shard_map/all_to_all | solution.py:273
  77.8 2.5 %all_to_all.16.got_ref = bf16[64,7296]{1,0:T(8,128)(2,1)S(1)} reshape(bf16[32,2,7296]{2,1,0:T(2,128)(2,1)} %all_to_all.22) | data formatting | bytes 1867776 | tf_op jit(solution)/shard_map/all_to_all | solution.py:273
  80.3 1.4 copy-done.1
  81.7 1.0 copy-done.3
  82.7 5.5 %shard_map.83 = (bf16[64,5248]{1,0:T(8,128)(2,1)S(1)}, bf16[48,5248]{1,0:T(8,128)(2,1)S(1)}) custom-call(bf16[64,7296]{1,0:T(8,128)(2,1)S(1)} %all_to_all.16.got_ref, bf16[48,5248]{1,0:T(8,128)(2,1)S(1)} %copy-done.3, bf16[48,16,1024]{2,1,0:T(8,128)(2,1)S(1)} %copy-done, bf16[48,16,1024]{2,1,0:T(8,128)(2,1)S(1)} %copy-done.1), custom_call_target="tpu_custom_call" | custom-call | flops 1000000000 | bytes 4194304 | tf_op jit(solution)/shard_map/pallas_call | solution.py:243
  88.2 0.8 copy-done.4
  89.0 1.1 all_to_all.17
  90.1 8.8 %all-to-all-start.1 = ((bf16[32,2,5248]{2,1,0:T(2,128)(2,1)}), bf16[32,2,5248]{2,1,0:T(2,128)(2,1)S(1)}, u32[]{:S(2)}, u32[]{:S(2)}) async-start(bf16[32,2,5248]{2,1,0:T(2,128)(2,1)} %all_to_all.17), calls=%async_computation.1 | async-start | bytes 1343488 | tf_op jit(solution)/shard_map/all_to_all | solution.py:286
  98.9 0.7 slice.4
  99.7 2.8 %collective-permute-start = (bf16[32,1280]{1,0:T(8,128)(2,1)S(1)}, bf16[32,1280]{1,0:T(8,128)(2,1)S(1)}, u32[]{:S(2)}, u32[]{:S(2)}) collective-permute-start(bf16[32,1280]{1,0:T(8,128)(2,1)S(1)} %copy-done.13), channel_id=1, source_target_pairs={{0,32},{32,0},{64,96},{96,64},{128,160},{160,128},{192,224},{224,1... | collective-permute-start | bytes 245768 | tf_op jit(solution)/shard_map/ppermute | solution.py:272
  102.5 4.4 %collective-permute-start.1 = (bf16[32,1280]{1,0:T(8,128)(2,1)S(1)}, bf16[32,1280]{1,0:T(8,128)(2,1)S(1)}, u32[]{:S(2)}, u32[]{:S(2)}) collective-permute-start(bf16[32,1280]{1,0:T(8,128)(2,1)S(1)} %get-tuple-element.25), channel_id=1, source_target_pairs={{0,64},{32,96},{64,0},{96,32},{128,192},{160,224},{192,128},{224,1... | collective-permute-start | bytes 245768 | tf_op jit(solution)/shard_map/ppermute | solution.py:272
  106.9 2.6 %collective-permute-start.2 = (bf16[32,1280]{1,0:T(8,128)(2,1)S(1)}, bf16[32,1280]{1,0:T(8,128)(2,1)S(1)}, u32[]{:S(2)}, u32[]{:S(2)}) collective-permute-start(bf16[32,1280]{1,0:T(8,128)(2,1)S(1)} %get-tuple-element.26), channel_id=1, source_target_pairs={{0,96},{32,64},{64,32},{96,0},{128,224},{160,192},{192,160},{224,1... | collective-permute-start | bytes 245768 | tf_op jit(solution)/shard_map/ppermute | solution.py:272
  109.5 1.2 collective-permute-done.1.q2
  110.7 4.8 %collective-permute-done.2.q3 = bf16[32,1280]{1,0:T(8,128)(2,1)S(1)} collective-permute-done((bf16[32,1280]{1,0:T(8,128)(2,1)S(1)}, bf16[32,1280]{1,0:T(8,128)(2,1)S(1)}, u32[]{:S(2)}, u32[]{:S(2)}) %collective-permute-start.2) | collective-permute-done | bytes 81952 | tf_op jit(solution)/shard_map/ppermute | solution.py:272
  115.5 18.3 %all-gather.2.cloned.1.call-done.kv_ref = bf16[256,2048]{1,0:T(8,128)(2,1)} async-done(((bf16[64,2048]{1,0:T(8,128)(2,1)}), bf16[256,2048]{1,0:T(8,128)(2,1)}) %all-gather.2.cloned.1.call-update) | async-done | bytes 1048592 | tf_op jit(solution)/shard_map/all_gather | solution.py:275
  133.8 1.2 copy-done.11
  135.0 3.7 %shard_map.84 = (bf16[32,1408]{1,0:T(8,128)(2,1)S(1)}, bf16[32,1408]{1,0:T(8,128)(2,1)S(1)}, bf16[32,1408]{1,0:T(8,128)(2,1)S(1)}, bf16[32,1408]{1,0:T(8,128)(2,1)S(1)}) custom-call(bf16[32,1280]{1,0:T(8,128)(2,1)S(1)} %get-tuple-element.23.q0, bf16[32,1280]{1,0:T(8,128)(2,1)S(1)} %collective-permute-done.q1, ...), custom_call_target="tpu_custom_call" | custom-call | flops 1000000000 | bytes 4194304 | tf_op jit(solution)/shard_map/pallas_call | solution.py:243
  138.7 3.6 %collective-permute-start.3 = (bf16[32,1408]{1,0:T(8,128)(2,1)S(1)}, bf16[32,1408]{1,0:T(8,128)(2,1)S(1)}, u32[]{:S(2)}, u32[]{:S(2)}) collective-permute-start(bf16[32,1408]{1,0:T(8,128)(2,1)S(1)} %get-tuple-element.28), channel_id=1, source_target_pairs={{0,32},{32,0},{64,96},{96,64},{128,160},{160,128},{192,224},{224,1... | collective-permute-start | bytes 270344 | tf_op jit(solution)/shard_map/ppermute | solution.py:272
  142.4 4.6 %collective-permute-start.4 = (bf16[32,1408]{1,0:T(8,128)(2,1)S(1)}, bf16[32,1408]{1,0:T(8,128)(2,1)S(1)}, u32[]{:S(2)}, u32[]{:S(2)}) collective-permute-start(bf16[32,1408]{1,0:T(8,128)(2,1)S(1)} %get-tuple-element.29), channel_id=1, source_target_pairs={{0,64},{32,96},{64,0},{96,32},{128,192},{160,224},{192,128},{224,1... | collective-permute-start | bytes 270344 | tf_op jit(solution)/shard_map/ppermute | solution.py:272
  147.0 2.4 %collective-permute-start.5 = (bf16[32,1408]{1,0:T(8,128)(2,1)S(1)}, bf16[32,1408]{1,0:T(8,128)(2,1)S(1)}, u32[]{:S(2)}, u32[]{:S(2)}) collective-permute-start(bf16[32,1408]{1,0:T(8,128)(2,1)S(1)} %get-tuple-element.30), channel_id=1, source_target_pairs={{0,96},{32,64},{64,32},{96,0},{128,224},{160,192},{192,160},{224,1... | collective-permute-start | bytes 270344 | tf_op jit(solution)/shard_map/ppermute | solution.py:272
  150.0 4.9 %collective-permute-done.5.p3 = bf16[32,1408]{1,0:T(8,128)(2,1)S(1)} collective-permute-done((bf16[32,1408]{1,0:T(8,128)(2,1)S(1)}, bf16[32,1408]{1,0:T(8,128)(2,1)S(1)}, u32[]{:S(2)}, u32[]{:S(2)}) %collective-permute-start.5) | collective-permute-done | bytes 90144 | tf_op jit(solution)/shard_map/ppermute | solution.py:272
  154.9 2.8 %shard_map.85 = bf16[32,5120]{1,0:T(8,128)(2,1)} custom-call(bf16[64,5248]{1,0:T(8,128)(2,1)S(1)} %all_to_all.19.got_ref, bf16[48,5248]{1,0:T(8,128)(2,1)S(1)} %copy-done.5, f32[128,128]{1,0:T(8,128)S(1)} %get-tuple-element.22.where_ref, bf16[32,1408]{1,0:T(8,128)(2,1)S(1)} %get-tuple-element.27.p0, bf16[32,1408]{1,0:T(8,128)(2,1)S(1)} %collective-permute-done.3.p1, ...), custom_call_target="tpu_custom_call" | custom-call | flops 100000000 | bytes 4194304 | tf_op jit(solution)/shard_map/pallas_call | solution.py:243
  (24 shorter events, 0.7 us)
Async XLA Ops:
  7.3 1.0 copy-start.6
  8.3 0.8 copy-start.7
  9.1 0.8 copy-start.8
  9.9 0.7 copy-start.9
  10.6 0.7 copy-start.10
  12.6 0.8 copy-start.2
  13.4 0.6 copy-start.12
  15.4 64.9 %copy-start = (bf16[48,16,1024]{2,1,0:T(8,128)(2,1)S(1)}, bf16[48,16,1024]{2,1,0:T(8,128)(2,1)}, u32[]{:S(2)}) copy-start(bf16[48,16,1024]{2,1,0:T(8,128)(2,1)} %k_ref.1) | copy-start | bytes 4718596
  80.3 1.4 copy-start.1
  81.7 1.0 copy-start.3
  88.2 0.8 copy-start.4
  89.0 10.7 %copy-start.13 = (bf16[32,1280]{1,0:T(8,128)(2,1)S(1)}, bf16[32,1280]{1,0:T(8,128)(2,1)}, u32[]{:S(2)}) copy-start(bf16[32,1280]{1,0:T(8,128)(2,1)} %copy-done.12) | copy-start | bytes 245764
  90.1 59.3 %all-to-all-start.1 = ((bf16[32,2,5248]{2,1,0:T(2,128)(2,1)}), bf16[32,2,5248]{2,1,0:T(2,128)(2,1)S(1)}, u32[]{:S(2)}, u32[]{:S(2)}) async-start(bf16[32,2,5248]{2,1,0:T(2,128)(2,1)} %all_to_all.17), calls=%async_computation.1 | async-start | bytes 1343488 | tf_op jit(solution)/shard_map/all_to_all | solution.py:286
  98.9 34.9 %all-gather.2.cloned.1.call-start = ((), (), s32[]{:S(2)}) async-start(), calls=%async_computation.2 | async-start | bytes 1310720 | tf_op jit(solution)/shard_map/all_gather | solution.py:275
  99.7 9.8 %collective-permute-start = (bf16[32,1280]{1,0:T(8,128)(2,1)S(1)}, bf16[32,1280]{1,0:T(8,128)(2,1)S(1)}, u32[]{:S(2)}, u32[]{:S(2)}) collective-permute-start(bf16[32,1280]{1,0:T(8,128)(2,1)S(1)} %copy-done.13), channel_id=1, source_target_pairs={{0,32},{32,0},{64,96},{96,64},{128,160},{160,128},{192,224},{224,1... | collective-permute-start | bytes 245768 | tf_op jit(solution)/shard_map/ppermute | solution.py:272
  102.5 8.2 %collective-permute-start.1 = (bf16[32,1280]{1,0:T(8,128)(2,1)S(1)}, bf16[32,1280]{1,0:T(8,128)(2,1)S(1)}, u32[]{:S(2)}, u32[]{:S(2)}) collective-permute-start(bf16[32,1280]{1,0:T(8,128)(2,1)S(1)} %get-tuple-element.25), channel_id=1, source_target_pairs={{0,64},{32,96},{64,0},{96,32},{128,192},{160,224},{192,128},{224,1... | collective-permute-start | bytes 245768 | tf_op jit(solution)/shard_map/ppermute | solution.py:272
  106.9 8.6 %collective-permute-start.2 = (bf16[32,1280]{1,0:T(8,128)(2,1)S(1)}, bf16[32,1280]{1,0:T(8,128)(2,1)S(1)}, u32[]{:S(2)}, u32[]{:S(2)}) collective-permute-start(bf16[32,1280]{1,0:T(8,128)(2,1)S(1)} %get-tuple-element.26), channel_id=1, source_target_pairs={{0,96},{32,64},{64,32},{96,0},{128,224},{160,192},{192,160},{224,1... | collective-permute-start | bytes 245768 | tf_op jit(solution)/shard_map/ppermute | solution.py:272
  133.8 1.2 copy-start.11
  138.7 16.2 %copy-start.5 = (bf16[48,5248]{1,0:T(8,128)(2,1)S(1)}, bf16[48,5248]{1,0:T(8,128)(2,1)}, u32[]{:S(2)}) copy-start(bf16[48,5248]{1,0:T(8,128)(2,1)} %copy-done.4) | copy-start | bytes 1511428
  138.7 10.9 %collective-permute-start.3 = (bf16[32,1408]{1,0:T(8,128)(2,1)S(1)}, bf16[32,1408]{1,0:T(8,128)(2,1)S(1)}, u32[]{:S(2)}, u32[]{:S(2)}) collective-permute-start(bf16[32,1408]{1,0:T(8,128)(2,1)S(1)} %get-tuple-element.28), channel_id=1, source_target_pairs={{0,32},{32,0},{64,96},{96,64},{128,160},{160,128},{192,224},{224,1... | collective-permute-start | bytes 270344 | tf_op jit(solution)/shard_map/ppermute | solution.py:272
  142.4 7.6 %collective-permute-start.4 = (bf16[32,1408]{1,0:T(8,128)(2,1)S(1)}, bf16[32,1408]{1,0:T(8,128)(2,1)S(1)}, u32[]{:S(2)}, u32[]{:S(2)}) collective-permute-start(bf16[32,1408]{1,0:T(8,128)(2,1)S(1)} %get-tuple-element.29), channel_id=1, source_target_pairs={{0,64},{32,96},{64,0},{96,32},{128,192},{160,224},{192,128},{224,1... | collective-permute-start | bytes 270344 | tf_op jit(solution)/shard_map/ppermute | solution.py:272
  147.0 7.9 %collective-permute-start.5 = (bf16[32,1408]{1,0:T(8,128)(2,1)S(1)}, bf16[32,1408]{1,0:T(8,128)(2,1)S(1)}, u32[]{:S(2)}, u32[]{:S(2)}) collective-permute-start(bf16[32,1408]{1,0:T(8,128)(2,1)S(1)} %get-tuple-element.30), channel_id=1, source_target_pairs={{0,96},{32,64},{64,32},{96,0},{128,224},{160,192},{192,160},{224,1... | collective-permute-start | bytes 270344 | tf_op jit(solution)/shard_map/ppermute | solution.py:272
Sparse Core Ops, SparseCore 0:
  101.8 31.9 all-gather.1

commit v2 on v1

v2 whole, which is shorter than its diff:
```python
import functools

import jax
import jax.numpy as jnp
from jax import lax
from jax.experimental import pallas as pl
from jax.experimental.pallas import tpu as pltpu
from jax.sharding import PartitionSpec as P

QH = 40
KVH = 8
HD = 128
PAGE = 16
MAXP = 4
CAP = 2
GROUP = QH // KVH
QCOLS = QH * HD
SIDE = 128
ROW = QCOLS + SIDE
SHARE = 2
HEADS = QH // SHARE
BLOCK = HEADS * HD
KV = KVH // SHARE * HD
SCALE = HD ** (-0.5)
VERY_LOW = -1e30
F32 = jnp.float32
BF16 = jnp.bfloat16


def iota(shape, axis):
    return lax.broadcasted_iota(jnp.int32, shape, axis)


def dot(a, b):
    return lax.dot_general(a, b, (((1,), (0,)), ((), ())), preferred_element_type=F32)


def dot_t(a, b):
    return lax.dot_general(a, b, (((1,), (1,)), ((), ())), preferred_element_type=F32)


def three_parts(x):
    hi = x.astype(BF16).astype(F32)
    mid = (x - hi).astype(BF16).astype(F32)
    lo = (x - hi - mid).astype(BF16).astype(F32)
    return hi, mid, lo


def load(refs, scratch, sems):
    copies = [
        pltpu.make_async_copy(ref, buf, sems.at[i])
        for i, (ref, buf) in enumerate(zip(refs, scratch, strict=True))
    ]
    for copy in copies:
        copy.start()
    return copies


def my_turn():
    return lax.rem(lax.div(lax.axis_index("grp"), 2), SHARE)


def share_kernel(pk_hbm, pv_hbm, q_hbm, prefix_ref, mine_ref, away_ref, rows, q_ref, sems):
    group = lax.axis_index("grp")
    turn, part, core = my_turn(), lax.div(group, 2 * SHARE), lax.rem(group, 2)
    kv_at = pl.ds(pl.multiple_of(turn * KV, KV), KV)
    fetch_q = pltpu.make_async_copy(q_hbm, q_ref, sems.at[0])
    fetch_q.start()

    def fetch_rows(source):
        copy = pltpu.make_async_copy(source.at[:, kv_at], rows, sems.at[1])
        copy.start()
        copy.wait()

    @pl.when(core == 0)
    def _():
        fetch_rows(pk_hbm)

    @pl.when(core == 1)
    def _():
        fetch_rows(pv_hbm)

    shape = (prefix_ref.shape[0], rows.shape[0])
    each = rows.shape[0] // (lax.axis_size("grp") // (2 * SHARE))
    one = iota(shape, 1) == part * each + lax.rem(iota(shape, 0), each)
    prefix_ref[...] = dot(jnp.where(one, 1.0, 0.0).astype(BF16), rows[...]).astype(BF16)
    fetch_q.wait()
    for o, ref in enumerate((mine_ref, away_ref)):
        at = pl.multiple_of((turn ^ o) * BLOCK, BLOCK)
        ref[...] = q_ref[:, pl.ds(at, BLOCK)]


def route_kernel(
    pool, q_hbm, table_hbm, len_hbm, place_hbm, send_ref, local_ref, where_ref,
    q_ref, table_ref, len_ref, place_ref, sems,
):
    copies = load(
        (place_hbm, table_hbm, len_hbm, q_hbm), (place_ref, table_ref, len_ref, q_ref), sems
    )
    requests = q_ref.shape[0]
    entries = requests * MAXP
    devices = send_ref.shape[0]
    cells = devices * CAP
    mine = lax.axis_index("blk")
    group = lax.axis_index("grp")
    base = group * (devices * pool)
    square = iota((requests, requests), 0) == iota((requests, requests), 1)

    def column(row):
        row = jnp.broadcast_to(row, (requests, requests)).astype(F32)
        return jnp.sum(jnp.where(square, row, 0.0), axis=1, keepdims=True)

    for copy in copies[:3]:
        copy.wait()
    table = table_ref[...] - base
    page = jnp.concatenate([column(table[j : j + 1]) for j in range(MAXP)], axis=0)
    place = (place_ref[...] - base).astype(F32)
    lane = iota((entries, 128), 1).astype(F32)
    found = jnp.zeros((entries, 128), F32)
    for k in range(place.shape[0]):
        found = found + jnp.where(page == lane + 128.0 * k, place[k : k + 1, :], 0.0)
    physical = jnp.sum(found, axis=1, keepdims=True)
    holder = jnp.floor((physical + 0.5) * (1.0 / pool))
    slot = physical - holder * pool
    length = column(len_ref[...])
    tokens = jnp.concatenate(
        [jnp.clip(length - PAGE * j, 0.0, PAGE) for j in range(MAXP)], axis=0
    )
    used = tokens > 0.0
    at_home = holder == mine.astype(F32)
    remote = jnp.where(used & jnp.logical_not(at_home), 1.0, 0.0)
    member = jnp.where(holder == lane, remote, 0.0)
    below = jnp.where(iota((entries, entries), 1) < iota((entries, entries), 0), 1.0, 0.0)
    before = dot(below.astype(BF16), member.astype(BF16))
    rank = jnp.sum(before * member, axis=1, keepdims=True)
    where = jnp.where(remote > 0.0, holder * CAP + rank, cells + slot)
    where = jnp.where(used, where, -1.0)
    where_ref[...] = jnp.broadcast_to(where, where_ref.shape)
    pick = jnp.where(where == lane, 1.0, 0.0).T
    picked = functools.reduce(
        jnp.add, [pick[:, requests * j : requests * (j + 1)] for j in range(MAXP)]
    ).astype(BF16)
    facts = jnp.where(lane == 0.0, slot, jnp.where(lane == 1.0, tokens, 0.0))
    side = dot(pick.astype(BF16), facts.astype(BF16)).astype(BF16)
    send_ref[:, :, QCOLS:ROW] = side[:cells].reshape(devices, CAP, SIDE)
    local_ref[:, QCOLS:ROW] = side[cells : cells + pool]
    copies[3].wait()
    for k in range(KVH):
        cols = slice(k * GROUP * HD, (k + 1) * GROUP * HD)
        rows = dot(picked, q_ref[:, cols]).astype(BF16)
        send_ref[:, :, cols] = rows[:cells].reshape(devices, CAP, GROUP * HD)
        local_ref[:, cols] = rows[cells : cells + pool]


def pages_kernel(
    got_hbm, local_hbm, k_hbm, v_hbm, answer_ref, own_ref, got_ref, local_ref, k_ref, v_ref, sems
):
    devices = got_ref.shape[0]
    first = load((got_hbm, local_hbm), (got_ref, local_ref), sems.at[pl.ds(KVH, 2)])
    cells = devices * CAP
    pool = k_ref.shape[0]
    step = 16
    pair = 2 * HD
    copies = []
    for c in range(KVH // 2):
        at = (slice(None), slice(None), pl.ds(c * pair, pair))
        for i, (hbm, ref) in enumerate(((k_hbm, k_ref), (v_hbm, v_ref))):
            copy = pltpu.make_async_copy(hbm.at[at], ref.at[at], sems.at[2 * c + i])
            copy.start()
            copies.append(copy)
    for copy in first:
        copy.wait()
    facts = got_ref[:, :, QCOLS:ROW].reshape(cells, SIDE)
    plain = facts
    facts = facts.astype(F32)
    lane = iota((cells, 128), 1).astype(F32)
    pick = jnp.where((facts[:, 0:1] == lane) & (facts[:, 1:2] > 0.0), 1.0, 0.0)
    fetch = pick.T[:pool].astype(BF16)
    pick = pick[:, :pool].astype(BF16)
    tokens = (dot(fetch, plain) + local_ref[:, QCOLS:ROW].astype(F32))[:, 1:2]
    wide = (step, step * PAGE)
    column = iota(wide, 1)
    sums = [jnp.zeros((step, SIDE), F32) for _ in range(pool // step)]
    side_lane = iota((step, SIDE), 1)
    masks = []
    for g in range(pool // step):
        ok = (lax.div(column, PAGE) == iota(wide, 0)) & (
            lax.rem(column, PAGE).astype(F32) < tokens[step * g : step * (g + 1)]
        )
        bias = jnp.where(ok, 0.0, VERY_LOW)
        masks.append(jnp.concatenate([bias] * GROUP, axis=0))
    for k in range(KVH):
        base = k * GROUP * HD
        cols = slice(base, base + GROUP * HD)
        asked = got_ref[:, :, cols].reshape(cells, GROUP * HD)
        rows = (dot(fetch, asked) + local_ref[:, cols].astype(F32)).astype(BF16)
        if k % 2 == 0:
            copies[k].wait()
            copies[k + 1].wait()
        for g in range(pool // step):
            span = slice(step * g, step * (g + 1))
            heads = jnp.concatenate(
                [rows[span, i * HD : (i + 1) * HD] for i in range(GROUP)], axis=0
            )
            keys = k_ref[span, :, k * HD : (k + 1) * HD].reshape(step * PAGE, HD)
            values = v_ref[span, :, k * HD : (k + 1) * HD].reshape(step * PAGE, HD)
            scores = dot_t(heads, keys) * SCALE + masks[g]
            top = jnp.max(scores, axis=1, keepdims=True)
            weights = jnp.exp(scores - top)
            total = jnp.sum(weights, axis=1, keepdims=True)
            mixture = (dot(weights.astype(BF16), values) / total).astype(BF16)
            log_sum = top + jnp.log(total)
            for i in range(GROUP):
                own_ref[span, base + i * HD : base + (i + 1) * HD] = mixture[step * i : step * (i + 1)]
                here = lax.rem(side_lane, QH) == k * GROUP + i
                sums[g] = jnp.where(here, log_sum[step * i : step * (i + 1)], sums[g])
    for g in range(pool // step):
        hi, mid, lo = three_parts(sums[g])
        side = jnp.where(side_lane < QH, hi, jnp.where(side_lane < 2 * QH, mid, lo))
        own_ref[step * g : step * (g + 1), QCOLS:ROW] = side.astype(BF16)
    for k in range(KVH):
        cols = slice(k * GROUP * HD, (k + 1) * GROUP * HD)
        rows = dot(pick, own_ref[:, cols]).astype(BF16)
        answer_ref[:, :, cols] = rows.reshape(devices, CAP, GROUP * HD)
    rows = dot(pick, own_ref[:, QCOLS:ROW]).astype(BF16)
    answer_ref[:, :, QCOLS:ROW] = rows.reshape(devices, CAP, SIDE)


def prefix_kernel(q0, q1, kv_mine, kv_other, o0, o1):
    requests = q0.shape[0]
    rows = requests * SHARE
    step = 256
    chunks = [slice(c, c + step) for c in range(0, kv_mine.shape[0], step)]
    core = lax.rem(lax.axis_index("grp"), 2)
    lane = iota((rows, SIDE), 1)
    outs = (o0, o1)

    def attend(k_ref, v_ref):
        sums = jnp.zeros((rows, SIDE), F32)
        for k in range(KVH // SHARE):
            kv = slice(k * HD, (k + 1) * HD)
            heads = jnp.concatenate(
                [
                    q[:, (k * GROUP + i) * HD : (k * GROUP + i + 1) * HD]
                    for i in range(GROUP)
                    for q in (q0, q1)
                ],
                axis=0,
            )
            scores = [dot_t(heads, k_ref[c, kv]) * SCALE for c in chunks]
            top = jnp.max(functools.reduce(jnp.maximum, scores), axis=1, keepdims=True)
            weights = [jnp.exp(s - top) for s in scores]
            total = jnp.sum(functools.reduce(jnp.add, weights), axis=1, keepdims=True)
            mixture = functools.reduce(
                jnp.add, [dot(w.astype(BF16), v_ref[c, kv]) for c, w in zip(chunks, weights)]
            )
            mixture = (mixture / total).astype(BF16)
            log_sum = top + jnp.log(total)
            for i in range(GROUP):
                h = k * GROUP + i
                here = lax.rem(lane, HEADS) == h
                sums = jnp.where(here, log_sum[rows * i : rows * (i + 1)], sums)
                for o, out in enumerate(outs):
                    at = rows * i + requests * o
                    out[:, h * HD : (h + 1) * HD] = mixture[at : at + requests]
        hi, mid, lo = three_parts(sums)
        side = jnp.where(lane < HEADS, hi, jnp.where(lane < 2 * HEADS, mid, lo)).astype(BF16)
        for o, out in enumerate(outs):
            out[:, BLOCK:] = side[requests * o : requests * (o + 1)]

    @pl.when(core == 0)
    def _():
        attend(kv_mine, kv_other)

    @pl.when(core == 1)
    def _():
        attend(kv_other, kv_mine)


def join_kernel(
    got_hbm, own_hbm, where_hbm, p0_hbm, p1_hbm, out_ref, got_ref, own_ref, where_ref, p0, p1, sems
):
    hbm, vmem = (got_hbm, own_hbm, where_hbm, p0_hbm, p1_hbm), (got_ref, own_ref, where_ref, p0, p1)
    for copy in load(hbm, vmem, sems):
        copy.wait()
    entries = where_ref.shape[0]
    requests = p0.shape[0]
    cells = got_ref.shape[0] * CAP
    pool = own_ref.shape[0]
    lane = iota((entries, 128), 1)
    where = where_ref[...]
    pick = jnp.where(where == lane.astype(F32), 1.0, 0.0).astype(BF16)
    far, near = pick[:, :cells], pick[:, cells : cells + pool]
    side = dot(far, got_ref[:, :, QCOLS:ROW].reshape(cells, SIDE)) + dot(near, own_ref[:, QCOLS:ROW])
    sums = side + pltpu.roll(side, SIDE - QH, 1) + pltpu.roll(side, SIDE - 2 * QH, 1)
    sums = jnp.where(where >= 0.0, sums, VERY_LOW)
    turn = my_turn()
    for o, p_ref in enumerate((p0, p1)):
        turned = turn ^ o
        at = pl.multiple_of(turned * BLOCK, 128)
        cols = pl.ds(at, BLOCK)
        got = got_ref[:, :, cols].reshape(cells, BLOCK)
        rows = dot(far, got) + dot(near, own_ref[:, cols])
        moved = pltpu.roll(sums, lax.rem(SIDE - turned * HEADS, SIDE), 1)
        pre = p_ref[:, BLOCK:].astype(F32)
        pre = pre + pltpu.roll(pre, SIDE - HEADS, 1) + pltpu.roll(pre, SIDE - 2 * HEADS, 1)
        logs = [moved[requests * j : requests * (j + 1)] for j in range(MAXP)]
        top = functools.reduce(jnp.maximum, logs, pre)
        parts = [jnp.exp(x - top) for x in logs]
        part = jnp.exp(pre - top)
        total = functools.reduce(jnp.add, parts, part)
        parts = [x / total for x in parts]
        part = part / total
        for h in range(HEADS):
            here = slice(h * HD, (h + 1) * HD)
            mixture = part[:, h : h + 1] * p_ref[:, here].astype(F32)
            for j in range(MAXP):
                mixture = mixture + parts[j][:, h : h + 1] * rows[requests * j : requests * (j + 1), here]
            out_ref[:, pl.ds(pl.multiple_of(at + h * HD, 128), HD)] = mixture.astype(BF16)


def call(kernel, out_shape, flops, *args, in_hbm=(), scratch=(), room=62_150_000):
    specs = [
        pl.BlockSpec(memory_space=pl.ANY if i in in_hbm else pltpu.VMEM) for i in range(len(args))
    ]
    return pl.pallas_call(
        kernel,
        out_shape=[jax.ShapeDtypeStruct(s, d) for s, d in out_shape],
        in_specs=specs,
        scratch_shapes=list(scratch),
        compiler_params=pltpu.CompilerParams(vmem_limit_bytes=room),
        cost_estimate=pl.CostEstimate(flops=flops, bytes_accessed=1 << 22, transcendentals=0),
    )(*args)


def like(x):
    return pltpu.VMEM(x.shape, x.dtype)


def body(
    queries, page_table, suffix_len, place, suffix_keys, suffix_values, prefix_keys, prefix_values
):
    requests = queries.shape[0]
    pool = suffix_keys.shape[0]
    devices = lax.axis_size("blk")
    group = lax.axis_size("grp")
    depth = prefix_keys.shape[0]
    each = depth // (group // (2 * SHARE))
    share, mine, away = call(
        share_kernel,
        [((devices * each, KV), BF16), ((requests, BLOCK), BF16), ((requests, BLOCK), BF16)],
        10**7,
        prefix_keys,
        prefix_values,
        queries,
        in_hbm=range(3),
        scratch=(pltpu.VMEM((depth, KV), BF16), like(queries), pltpu.SemaphoreType.DMA((2,))),
    )
    swap = lambda x: lax.ppermute(x, "grp", [(i, i ^ 2) for i in range(group)])
    exchange = lambda x: lax.all_to_all(x, "blk", split_axis=0, concat_axis=0, tiled=True)
    part = exchange(share.reshape(devices, each, KV)).reshape(devices * each, KV)
    tables, lengths, places = (
        page_table.T, suffix_len.reshape(1, requests), place.reshape(-1, 128)
    )
    send, local, where = call(
        functools.partial(route_kernel, pool),
        [((devices, CAP, ROW), BF16), ((pool, ROW), BF16), ((requests * MAXP, 128), F32)],
        10**8,
        queries,
        tables,
        lengths,
        places,
        in_hbm=range(4),
        scratch=(*map(like, (queries, tables, lengths, places)), pltpu.SemaphoreType.DMA((4,))),
    )
    send, part = lax.optimization_barrier((send, part))
    got = exchange(send)
    around = [
        lax.ppermute(part, "grp", [(i, (i + 2 * SHARE * y) % group) for i in range(group)])
        for y in range(1, group // (2 * SHARE))
    ]
    kv_mine = jnp.concatenate([part, *around], axis=0)
    kv_other = lax.ppermute(kv_mine, "grp", [(i, i ^ 1) for i in range(group)])
    asked = swap(away)
    local, kv_mine, kv_other, asked = lax.optimization_barrier((local, kv_mine, kv_other, asked))
    served, away = call(
        prefix_kernel,
        [((requests, BLOCK + SIDE), BF16)] * SHARE,
        10**9,
        mine,
        asked,
        kv_mine,
        kv_other,
        room=40 << 20,
    )
    away = swap(away)
    answer, own = call(
        pages_kernel,
        [((devices, CAP, ROW), BF16), ((pool, ROW), BF16)],
        10**9,
        got,
        local,
        suffix_keys,
        suffix_values,
        in_hbm=range(4),
        scratch=(
            *map(like, (got, local, suffix_keys, suffix_values)),
            pltpu.SemaphoreType.DMA((KVH + 2,)),
        ),
    )
    back = exchange(answer)
    last = (back, own, where, served, away)
    (out,) = call(
        join_kernel,
        [((requests, QCOLS), BF16)],
        10**8,
        *last,
        in_hbm=range(5),
        scratch=(*map(like, last), pltpu.SemaphoreType.DMA((5,))),
        room=32 << 20,
    )
    return out


def solution(mesh):
    return jax.shard_map(
        body,
        mesh=mesh,
        in_specs=(
            P(("grp", "blk"), None),
            P(("grp", "blk"), None),
            P(("grp", "blk")),
            P("grp"),
            P(("grp", "blk"), None, None),
            P(("grp", "blk"), None, None),
            P("blk", None),
            P("blk", None),
        ),
        out_specs=P(("grp", "blk"), None),
        check_vma=False,
    )
```

time: 165 us -> 140 us (0.85)
  blocking collectives: 62.4 us -> 0 us
  waiting for transfers between devices: 29.6 us -> 59.8 us
  starting transfers between devices: 29.2 us -> 55.4 us
  between operations: 13.6 us -> 0.16 us
  local copies, waits for them, and re-layouts: 16.5 us -> 3.43 us
  Pallas kernels: 13.3 us -> 19.1 us
    all_to_all x1 -> x0, blocking collectives: 62.4 us -> none  [body(): got = lax.all_to_all(send, 'blk', split_axis=0, concat_axis=0, tiled=True)]
    all_to_all x1 -> x3, waiting for transfers between devices: 0.01 us -> 41.5 us  [body(): lax.all_to_all(x, 'blk', split_axis=0, concat_axis=0, tiled=True)]
    all_to_all x1 -> x3, starting transfers between devices: 8.77 us -> 32.6 us  [body(): lax.all_to_all(x, 'blk', split_axis=0, concat_axis=0, tiled=True)]
    all_gather x1 -> x0, waiting for transfers between devices: 18.3 us -> none  [body(): lax.all_gather(got[:, ROW:], 'grp', axis=0, tiled=True, axis_index_groups...]
    unnamed x29 -> x17, local copies, waits for them, and re-layouts: 10.6 us -> 3.41 us
    ppermute x6, waiting for transfers between devices: 11.3 us -> 18.4 us  [the longest x2 11.2 us: body(): swap = lambda x: lax.ppermute(x, 'grp', [(i, i ^ 2) for i in range(group)])]
    pallas_call x4 -> x5, Pallas kernels: 13.3 us -> 19.1 us  [call(): pl.pallas_call(kernel, out_shape=[jax.ShapeDtypeStruct(s, d) for s, d in...]
    all_to_all x4 -> x0, local copies, waits for them, and re-layouts: 5.15 us -> none  [the longest x2 3.8 us: body(): got = lax.all_to_all(send, 'blk', split_axis=0, concat_axis=0, tiled=True)]
  transfers between devices with their start and end apart: 8 -> 9, of which waited for: 5 -> 7; matrix products, arithmetic and copies ran while one was open for 0% -> 0% of each run, Pallas kernels for 2% -> 4%
where the time goes in v2:
time: 140 us; the launch traced here: 138 us
  waiting for transfers between devices  59.8 us (43%)
  starting transfers between devices  55.4 us (40%)
  Pallas kernels  19.1 us (14%)
  local copies, waits for them, and re-layouts  3.43 us (2%)
    all_to_all x3, waiting for transfers between devices, body(): lax.all_to_all(x, 'blk', split_axis=0, concat_axis=0, tiled=True)  41.5 us
    all_to_all x3, starting transfers between devices, body(): lax.all_to_all(x, 'blk', split_axis=0, concat_axis=0, tiled=True)  32.6 us
    pallas_call x5, Pallas kernels, call(): pl.pallas_call(kernel, out_shape=[jax.ShapeDtypeStruct(s, d) for s, d in...  19.1 us
    ppermute x2, waiting for transfers between devices, body(): swap = lambda x: lax.ppermute(x, 'grp', [(i, i ^ 2) for i in range(group)])  11.2 us
    ppermute x3, starting transfers between devices, body(): lax.ppermute(part, 'grp', [(i, (i + 2 * SHARE * y) % group) for i in rang...  10.7 us
    ppermute x2, starting transfers between devices, body(): swap = lambda x: lax.ppermute(x, 'grp', [(i, i ^ 2) for i in range(group)])  8.17 us
    ppermute x3, waiting for transfers between devices, body(): lax.ppermute(part, 'grp', [(i, (i + 2 * SHARE * y) % group) for i in rang...  7.18 us
    ppermute x1, starting transfers between devices, body(): kv_other = lax.ppermute(kv_mine, 'grp', [(i, i ^ 1) for i in range(group)])  3.92 us
  transfers between devices with their start and end apart: 9, of which 7 were waited for; matrix products, arithmetic and copies ran while one was open for 0% of the time, Pallas kernels for 4%

profile of v2, /device:TPU:1, one launch (start us, length us, event | category | flops | bytes accessed | tf_op | source)
XLA Modules:
  0.0 138.0 jit_solution(17491558813671652213)
XLA Ops:
  0.0 1.9 %shard_map.83 = (bf16[256,512]{1,0:T(8,128)(2,1)}, bf16[32,2560]{1,0:T(8,128)(2,1)}, bf16[32,2560]{1,0:T(8,128)(2,1)}) custom-call(bf16[32,1024]{1,0:T(8,128)(2,1)} %pk_hbm.1, bf16[32,1024]{1,0:T(8,128)(2,1)} %pv_hbm.1, bf16[32,5120]{1,0:T(8,128)(2,1)} %q_hbm.3), custom_call_target="tpu_custom_call" | custom-call | flops 10000000 | bytes 4194304 | tf_op jit(solution)/shard_map/pallas_call | solution.py:326
  1.9 17.0 %all-to-all-start = ((bf16[32,8,512]{2,1,0:T(8,128)(2,1)}), bf16[32,8,512]{2,1,0:T(8,128)(2,1)S(1)}, u32[]{:S(2)}, u32[]{:S(2)}) async-start(bf16[32,8,512]{2,1,0:T(8,128)(2,1)} %bitcast.9), calls=%async_computation | async-start | bytes 524288 | tf_op jit(solution)/shard_map/all_to_all | solution.py:360
  18.9 3.2 %shard_map.82 = (bf16[32,2,5248]{2,1,0:T(2,128)(2,1)}, bf16[48,5248]{1,0:T(8,128)(2,1)}, f32[128,128]{1,0:T(8,128)}) custom-call(bf16[32,5120]{1,0:T(8,128)(2,1)} %q_hbm.3, s32[4,32]{1,0:T(4,128)} %bitcast.11, s32[1,32]{1,0:T(1,128)} %bitcast.12, s32[12,128]{1,0:T(8,128)} %bitcast.10), custom_call_target="tpu_custom_call" | custom-call | flops 100000000 | bytes 4194304 | tf_op jit(solution)/shard_map/pallas_call | solution.py:326
  22.1 16.8 %all-to-all-done = bf16[32,8,512]{2,1,0:T(8,128)(2,1)S(1)} async-done(((bf16[32,8,512]{2,1,0:T(8,128)(2,1)}), bf16[32,8,512]{2,1,0:T(8,128)(2,1)S(1)}, u32[]{:S(2)}, u32[]{:S(2)}) %all-to-all-start) | async-done | bytes 262176 | tf_op jit(solution)/shard_map/all_to_all | solution.py:360
  38.9 0.0 copy-start.6
  38.9 5.2 %all-to-all-start.1 = ((bf16[32,2,5248]{2,1,0:T(2,128)(2,1)}), bf16[32,2,5248]{2,1,0:T(2,128)(2,1)S(1)}, u32[]{:S(2)}, u32[]{:S(2)}) async-start(bf16[32,2,5248]{2,1,0:T(2,128)(2,1)} %get-tuple-element.23), calls=%async_computation.1 | async-start | bytes 1343488 | tf_op jit(solution)/shard_map/all_to_all | solution.py:360
  44.1 3.2 %collective-permute-start = (bf16[256,512]{1,0:T(8,128)(2,1)S(1)}, bf16[256,512]{1,0:T(8,128)(2,1)S(1)}, u32[]{:S(2)}, u32[]{:S(2)}) collective-permute-start(bf16[256,512]{1,0:T(8,128)(2,1)S(1)} %bitcast.5), channel_id=1, source_target_pairs={{0,128},{32,160},{64,192},{96,224},{128,256},{160,288},{192,320},{... | collective-permute-start | bytes 786440 | tf_op jit(solution)/shard_map/ppermute | solution.py:379
  47.3 4.5 %collective-permute-start.1 = (bf16[256,512]{1,0:T(8,128)(2,1)S(1)}, bf16[256,512]{1,0:T(8,128)(2,1)S(1)}, u32[]{:S(2)}, u32[]{:S(2)}) collective-permute-start(bf16[256,512]{1,0:T(8,128)(2,1)S(1)} %bitcast.6), channel_id=1, source_target_pairs={{0,256},{32,288},{64,320},{96,352},{128,384},{160,416},{192,448},{... | collective-permute-start | bytes 786440 | tf_op jit(solution)/shard_map/ppermute | solution.py:379
  51.8 3.0 %collective-permute-start.2 = (bf16[256,512]{1,0:T(8,128)(2,1)S(1)}, bf16[256,512]{1,0:T(8,128)(2,1)S(1)}, u32[]{:S(2)}, u32[]{:S(2)}) collective-permute-start(bf16[256,512]{1,0:T(8,128)(2,1)S(1)} %bitcast.7), channel_id=1, source_target_pairs={{0,384},{32,416},{64,448},{96,480},{128,0},{160,32},{192,64},{224,... | collective-permute-start | bytes 786440 | tf_op jit(solution)/shard_map/ppermute | solution.py:379
  54.8 0.0 collective-permute-done
  54.9 4.9 %collective-permute-done.1 = bf16[256,512]{1,0:T(8,128)(2,1)S(1)} collective-permute-done((bf16[256,512]{1,0:T(8,128)(2,1)S(1)}, bf16[256,512]{1,0:T(8,128)(2,1)S(1)}, u32[]{:S(2)}, u32[]{:S(2)}) %collective-permute-start.1) | collective-permute-done | bytes 262176 | tf_op jit(solution)/shard_map/ppermute | solution.py:379
  59.8 2.3 %collective-permute-done.2 = bf16[256,512]{1,0:T(8,128)(2,1)S(1)} collective-permute-done((bf16[256,512]{1,0:T(8,128)(2,1)S(1)}, bf16[256,512]{1,0:T(8,128)(2,1)S(1)}, u32[]{:S(2)}, u32[]{:S(2)}) %collective-permute-start.2) | collective-permute-done | bytes 262176 | tf_op jit(solution)/shard_map/ppermute | solution.py:379
  62.1 3.9 %collective-permute-start.3 = (bf16[1024,512]{1,0:T(8,128)(2,1)S(1)}, bf16[1024,512]{1,0:T(8,128)(2,1)S(1)}, u32[]{:S(2)}, u32[]{:S(2)}) collective-permute-start(bf16[1024,512]{1,0:T(8,128)(2,1)S(1)} %constant_dynamic-update-slice_fusion.kv_mine), channel_id=1, source_target_pairs={{0,32},{32,0},{64,96},{96,64},{128,160},{160,128},{192,224},{224,1... | collective-permute-start | bytes 3145736 | tf_op jit(solution)/shard_map/ppermute | solution.py:383
  66.0 0.0 copy-done.6
  66.0 4.4 %collective-permute-start.4 = (bf16[32,2560]{1,0:T(8,128)(2,1)S(1)}, bf16[32,2560]{1,0:T(8,128)(2,1)S(1)}, u32[]{:S(2)}, u32[]{:S(2)}) collective-permute-start(bf16[32,2560]{1,0:T(8,128)(2,1)S(1)} %copy-done.6), channel_id=1, source_target_pairs={{0,64},{32,96},{64,0},{96,32},{128,192},{160,224},{192,128},{224,1... | collective-permute-start | bytes 491528 | tf_op jit(solution)/shard_map/ppermute | solution.py:359
  70.4 5.6 %collective-permute-done.4.q1 = bf16[32,2560]{1,0:T(8,128)(2,1)S(1)} collective-permute-done((bf16[32,2560]{1,0:T(8,128)(2,1)S(1)}, bf16[32,2560]{1,0:T(8,128)(2,1)S(1)}, u32[]{:S(2)}, u32[]{:S(2)}) %collective-permute-start.4) | collective-permute-done | bytes 163872 | tf_op jit(solution)/shard_map/ppermute | solution.py:359
  76.0 0.7 copy-done.3
  76.6 0.0 collective-permute-done.3.kv_other
  76.6 2.5 %all-to-all-done.1.got_hbm = bf16[32,2,5248]{2,1,0:T(2,128)(2,1)S(1)} async-done(((bf16[32,2,5248]{2,1,0:T(2,128)(2,1)}), bf16[32,2,5248]{2,1,0:T(2,128)(2,1)S(1)}, u32[]{:S(2)}, u32[]{:S(2)}) %all-to-all-start.1) | async-done | bytes 671776 | tf_op jit(solution)/shard_map/all_to_all | solution.py:360
  79.1 0.9 copy-done.5
  80.0 8.0 %shard_map.84 = (bf16[32,2,5248]{2,1,0:T(2,128)(2,1)}, bf16[48,5248]{1,0:T(8,128)(2,1)}) custom-call(bf16[32,2,5248]{2,1,0:T(2,128)(2,1)} %copy-done.5, bf16[48,5248]{1,0:T(8,128)(2,1)} %get-tuple-element.27.local_hbm, bf16[48,16,1024]{2,1,0:T(8,128)(2,1)} %k_hbm.1, bf16[48,16,1024]{2,1,0:T(8,128)(2,1)} %v_hbm.1), custom_call_target="tpu_custom_call" | custom-call | flops 1000000000 | bytes 4194304 | tf_op jit(solution)/shard_map/pallas_call | solution.py:326
  88.0 10.5 %all-to-all-start.2 = ((bf16[32,2,5248]{2,1,0:T(2,128)(2,1)}), bf16[32,2,5248]{2,1,0:T(2,128)(2,1)S(1)}, u32[]{:S(2)}, u32[]{:S(2)}) async-start(bf16[32,2,5248]{2,1,0:T(2,128)(2,1)} %get-tuple-element.28), calls=%async_computation.2 | async-start | bytes 1343488 | tf_op jit(solution)/shard_map/all_to_all | solution.py:360
  98.4 0.0 copy-start.2
  98.5 0.9 copy-done.2
  99.4 0.9 copy-done.4
  100.3 2.4 %shard_map.85 = (bf16[32,2688]{1,0:T(8,128)(2,1)S(1)}, bf16[32,2688]{1,0:T(8,128)(2,1)S(1)}) custom-call(bf16[32,2560]{1,0:T(8,128)(2,1)S(1)} %copy-done.2, bf16[32,2560]{1,0:T(8,128)(2,1)S(1)} %copy-done.4, bf16[1024,512]{1,0:T(8,128)(2,1)S(1)} %constant_dynamic-update-slice_fusion.kv_mine, bf16[1024,512]{1,0:T(8,128)(2,1)S(1)} %collective-permute-done.3.kv_other), custom_call_target="tpu_custom_call" | custom-call | flops 1000000000 | bytes 4194304 | tf_op jit(solution)/shard_map/pallas_call | solution.py:326
  102.7 3.8 %collective-permute-start.5 = (bf16[32,2688]{1,0:T(8,128)(2,1)S(1)}, bf16[32,2688]{1,0:T(8,128)(2,1)S(1)}, u32[]{:S(2)}, u32[]{:S(2)}) collective-permute-start(bf16[32,2688]{1,0:T(8,128)(2,1)S(1)} %get-tuple-element.36), channel_id=1, source_target_pairs={{0,64},{32,96},{64,0},{96,32},{128,192},{160,224},{192,128},{224,1... | collective-permute-start | bytes 516104 | tf_op jit(solution)/shard_map/ppermute | solution.py:359
  106.5 5.6 %collective-permute-done.5.p1_hbm = bf16[32,2688]{1,0:T(8,128)(2,1)S(1)} collective-permute-done((bf16[32,2688]{1,0:T(8,128)(2,1)S(1)}, bf16[32,2688]{1,0:T(8,128)(2,1)S(1)}, u32[]{:S(2)}, u32[]{:S(2)}) %collective-permute-start.5) | collective-permute-done | bytes 172064 | tf_op jit(solution)/shard_map/ppermute | solution.py:359
  112.1 22.2 %all-to-all-done.2.got_hbm = bf16[32,2,5248]{2,1,0:T(2,128)(2,1)S(1)} async-done(((bf16[32,2,5248]{2,1,0:T(2,128)(2,1)}), bf16[32,2,5248]{2,1,0:T(2,128)(2,1)S(1)}, u32[]{:S(2)}, u32[]{:S(2)}) %all-to-all-start.2) | async-done | bytes 671776 | tf_op jit(solution)/shard_map/all_to_all | solution.py:360
  134.3 0.0 copy-done
  134.3 0.0 copy-done.1
  134.3 3.7 %shard_map.86 = bf16[32,5120]{1,0:T(8,128)(2,1)} custom-call(bf16[32,2,5248]{2,1,0:T(2,128)(2,1)S(1)} %all-to-all-done.2.got_hbm, bf16[48,5248]{1,0:T(8,128)(2,1)S(1)} %copy-done, f32[128,128]{1,0:T(8,128)S(1)} %copy-done.1, bf16[32,2688]{1,0:T(8,128)(2,1)S(1)} %get-tuple-element.35.p0_hbm, bf16[32,2688]{1,0:T(8,128)(2,1)S(1)} %collective-permute-done.5.p1_hbm), custom_call_target="tpu_custom_call" | custom-call | flops 100000000 | bytes 4194304 | tf_op jit(solution)/shard_map/pallas_call | solution.py:326
  (9 shorter events, 0.1 us)
Async XLA Ops:
  1.9 37.0 %all-to-all-start = ((bf16[32,8,512]{2,1,0:T(8,128)(2,1)}), bf16[32,8,512]{2,1,0:T(8,128)(2,1)S(1)}, u32[]{:S(2)}, u32[]{:S(2)}) async-start(bf16[32,8,512]{2,1,0:T(8,128)(2,1)} %bitcast.9), calls=%async_computation | async-start | bytes 524288 | tf_op jit(solution)/shard_map/all_to_all | solution.py:360
  38.9 27.1 %copy-start.6 = (bf16[32,2560]{1,0:T(8,128)(2,1)S(1)}, bf16[32,2560]{1,0:T(8,128)(2,1)}, u32[]{:S(2)}) copy-start(bf16[32,2560]{1,0:T(8,128)(2,1)} %get-tuple-element.26) | copy-start | bytes 491524
  38.9 40.2 %all-to-all-start.1 = ((bf16[32,2,5248]{2,1,0:T(2,128)(2,1)}), bf16[32,2,5248]{2,1,0:T(2,128)(2,1)S(1)}, u32[]{:S(2)}, u32[]{:S(2)}) async-start(bf16[32,2,5248]{2,1,0:T(2,128)(2,1)} %get-tuple-element.23), calls=%async_computation.1 | async-start | bytes 1343488 | tf_op jit(solution)/shard_map/all_to_all | solution.py:360
  44.1 10.8 %collective-permute-start = (bf16[256,512]{1,0:T(8,128)(2,1)S(1)}, bf16[256,512]{1,0:T(8,128)(2,1)S(1)}, u32[]{:S(2)}, u32[]{:S(2)}) collective-permute-start(bf16[256,512]{1,0:T(8,128)(2,1)S(1)} %bitcast.5), channel_id=1, source_target_pairs={{0,128},{32,160},{64,192},{96,224},{128,256},{160,288},{192,320},{... | collective-permute-start | bytes 786440 | tf_op jit(solution)/shard_map/ppermute | solution.py:379
  47.3 12.5 %collective-permute-start.1 = (bf16[256,512]{1,0:T(8,128)(2,1)S(1)}, bf16[256,512]{1,0:T(8,128)(2,1)S(1)}, u32[]{:S(2)}, u32[]{:S(2)}) collective-permute-start(bf16[256,512]{1,0:T(8,128)(2,1)S(1)} %bitcast.6), channel_id=1, source_target_pairs={{0,256},{32,288},{64,320},{96,352},{128,384},{160,416},{192,448},{... | collective-permute-start | bytes 786440 | tf_op jit(solution)/shard_map/ppermute | solution.py:379
  51.8 10.2 %collective-permute-start.2 = (bf16[256,512]{1,0:T(8,128)(2,1)S(1)}, bf16[256,512]{1,0:T(8,128)(2,1)S(1)}, u32[]{:S(2)}, u32[]{:S(2)}) collective-permute-start(bf16[256,512]{1,0:T(8,128)(2,1)S(1)} %bitcast.7), channel_id=1, source_target_pairs={{0,384},{32,416},{64,448},{96,480},{128,0},{160,32},{192,64},{224,... | collective-permute-start | bytes 786440 | tf_op jit(solution)/shard_map/ppermute | solution.py:379
  62.1 14.6 %collective-permute-start.3 = (bf16[1024,512]{1,0:T(8,128)(2,1)S(1)}, bf16[1024,512]{1,0:T(8,128)(2,1)S(1)}, u32[]{:S(2)}, u32[]{:S(2)}) collective-permute-start(bf16[1024,512]{1,0:T(8,128)(2,1)S(1)} %constant_dynamic-update-slice_fusion.kv_mine), channel_id=1, source_target_pairs={{0,32},{32,0},{64,96},{96,64},{128,160},{160,128},{192,224},{224,1... | collective-permute-start | bytes 3145736 | tf_op jit(solution)/shard_map/ppermute | solution.py:383
  66.0 9.9 %collective-permute-start.4 = (bf16[32,2560]{1,0:T(8,128)(2,1)S(1)}, bf16[32,2560]{1,0:T(8,128)(2,1)S(1)}, u32[]{:S(2)}, u32[]{:S(2)}) collective-permute-start(bf16[32,2560]{1,0:T(8,128)(2,1)S(1)} %copy-done.6), channel_id=1, source_target_pairs={{0,64},{32,96},{64,0},{96,32},{128,192},{160,224},{192,128},{224,1... | collective-permute-start | bytes 491528 | tf_op jit(solution)/shard_map/ppermute | solution.py:359
  76.0 0.7 copy-start.3
  79.1 0.9 copy-start.5
  88.0 46.3 %all-to-all-start.2 = ((bf16[32,2,5248]{2,1,0:T(2,128)(2,1)}), bf16[32,2,5248]{2,1,0:T(2,128)(2,1)S(1)}, u32[]{:S(2)}, u32[]{:S(2)}) async-start(bf16[32,2,5248]{2,1,0:T(2,128)(2,1)} %get-tuple-element.28), calls=%async_computation.2 | async-start | bytes 1343488 | tf_op jit(solution)/shard_map/all_to_all | solution.py:360
  98.4 0.9 copy-start.2
  99.4 0.9 copy-start.4
  100.3 34.0 %copy-start = (bf16[48,5248]{1,0:T(8,128)(2,1)S(1)}, bf16[48,5248]{1,0:T(8,128)(2,1)}, u32[]{:S(2)}) copy-start(bf16[48,5248]{1,0:T(8,128)(2,1)} %get-tuple-element.29.own_hbm) | copy-start | bytes 1511428
  100.3 34.0 %copy-start.1 = (f32[128,128]{1,0:T(8,128)S(1)}, f32[128,128]{1,0:T(8,128)}, u32[]{:S(2)}) copy-start(f32[128,128]{1,0:T(8,128)} %get-tuple-element.30.where_hbm) | copy-start | bytes 196612
  102.7 9.4 %collective-permute-start.5 = (bf16[32,2688]{1,0:T(8,128)(2,1)S(1)}, bf16[32,2688]{1,0:T(8,128)(2,1)S(1)}, u32[]{:S(2)}, u32[]{:S(2)}) collective-permute-start(bf16[32,2688]{1,0:T(8,128)(2,1)S(1)} %get-tuple-element.36), channel_id=1, source_target_pairs={{0,64},{32,96},{64,0},{96,32},{128,192},{160,224},{192,128},{224,1... | collective-permute-start | bytes 516104 | tf_op jit(solution)/shard_map/ppermute | solution.py:359

commit v3 on v2

--- a/solution.py
+++ b/solution.py
@@ -17,7 +17,7 @@
 QCOLS = QH * HD
 SIDE = 128
 ROW = QCOLS + SIDE
-SHARE = 2
+SHARE = 4
 HEADS = QH // SHARE
 BLOCK = HEADS * HD
 KV = KVH // SHARE * HD
@@ -57,52 +57,38 @@
 
 
 def my_turn():
-    return lax.rem(lax.div(lax.axis_index("grp"), 2), SHARE)
-
-
-def share_kernel(pk_hbm, pv_hbm, q_hbm, prefix_ref, mine_ref, away_ref, rows, q_ref, sems):
     group = lax.axis_index("grp")
-    turn, part, core = my_turn(), lax.div(group, 2 * SHARE), lax.rem(group, 2)
-    kv_at = pl.ds(pl.multiple_of(turn * KV, KV), KV)
-    fetch_q = pltpu.make_async_copy(q_hbm, q_ref, sems.at[0])
-    fetch_q.start()
-
-    def fetch_rows(source):
-        copy = pltpu.make_async_copy(source.at[:, kv_at], rows, sems.at[1])
-        copy.start()
-        copy.wait()
-
-    @pl.when(core == 0)
-    def _():
-        fetch_rows(pk_hbm)
-
-    @pl.when(core == 1)
-    def _():
-        fetch_rows(pv_hbm)
-
-    shape = (prefix_ref.shape[0], rows.shape[0])
-    each = rows.shape[0] // (lax.axis_size("grp") // (2 * SHARE))
-    one = iota(shape, 1) == part * each + lax.rem(iota(shape, 0), each)
-    prefix_ref[...] = dot(jnp.where(one, 1.0, 0.0).astype(BF16), rows[...]).astype(BF16)
-    fetch_q.wait()
-    for o, ref in enumerate((mine_ref, away_ref)):
-        at = pl.multiple_of((turn ^ o) * BLOCK, BLOCK)
-        ref[...] = q_ref[:, pl.ds(at, BLOCK)]
+    return lax.rem(lax.div(group, 2), 2) + 2 * lax.div(group, 8)
 
 
 def route_kernel(
-    pool, q_hbm, table_hbm, len_hbm, place_hbm, send_ref, local_ref, where_ref,
-    q_ref, table_ref, len_ref, place_ref, sems,
+    pool, q_hbm, table_hbm, len_hbm, place_hbm, pk_hbm, pv_hbm,
+    send_ref, local_ref, where_ref, s0, s1, s2, s3,
+    q_ref, table_ref, len_ref, place_ref, rows_ref, sems,
 ):
-    copies = load(
-        (place_hbm, table_hbm, len_hbm, q_hbm), (place_ref, table_ref, len_ref, q_ref), sems
-    )
     requests = q_ref.shape[0]
     entries = requests * MAXP
     devices = send_ref.shape[0]
     cells = devices * CAP
     mine = lax.axis_index("blk")
     group = lax.axis_index("grp")
+    turn = my_turn()
+    copies = load(
+        (place_hbm, table_hbm, len_hbm, q_hbm), (place_ref, table_ref, len_ref, q_ref), sems
+    )
+    kv_at = pl.ds(pl.multiple_of(turn * KV, KV), KV)
+
+    def fetch_rows(source):
+        return pltpu.make_async_copy(source.at[:, kv_at], rows_ref, sems.at[4])
+
+    @pl.when(lax.rem(group, 2) == 0)
+    def _():
+        fetch_rows(pk_hbm).start()
+
+    @pl.when(lax.rem(group, 2) == 1)
+    def _():
+        fetch_rows(pv_hbm).start()
+
     base = group * (devices * pool)
     square = iota((requests, requests), 0) == iota((requests, requests), 1)
 
@@ -150,13 +136,25 @@
         rows = dot(picked, q_ref[:, cols]).astype(BF16)
         send_ref[:, :, cols] = rows[:cells].reshape(devices, CAP, GROUP * HD)
         local_ref[:, cols] = rows[cells : cells + pool]
+    for o, ref in enumerate((s0, s1, s2, s3)):
+        at = pl.multiple_of((turn ^ o) * BLOCK, BLOCK)
+        ref[...] = q_ref[:, pl.ds(at, BLOCK)]
+    fetch_rows(pk_hbm).wait()
+    shape = (cells, rows_ref.shape[0])
+    deep = rows_ref.shape[0] // 2
+    half = deep * lax.rem(lax.div(group, 4), 2)
+    for p in range(deep // CAP):
+        one = iota(shape, 1) == half + deep // CAP * lax.rem(iota(shape, 0), CAP) + p
+        rows = dot(jnp.where(one, 1.0, 0.0).astype(BF16), rows_ref[...]).astype(BF16)
+        send_ref[:, :, ROW + KV * p : ROW + KV * (p + 1)] = rows.reshape(devices, CAP, KV)
 
 
 def pages_kernel(
     got_hbm, local_hbm, k_hbm, v_hbm, answer_ref, own_ref, got_ref, local_ref, k_ref, v_ref, sems
 ):
     devices = got_ref.shape[0]
-    first = load((got_hbm, local_hbm), (got_ref, local_ref), sems.at[pl.ds(KVH, 2)])
+    here = got_hbm.at[:, :, pl.ds(0, ROW)]
+    first = load((here, local_hbm), (got_ref, local_ref), sems.at[pl.ds(KVH, 2)])
     cells = devices * CAP
     pool = k_ref.shape[0]
     step = 16
@@ -226,14 +224,14 @@
     answer_ref[:, :, QCOLS:ROW] = rows.reshape(devices, CAP, SIDE)
 
 
-def prefix_kernel(q0, q1, kv_mine, kv_other, o0, o1):
+def prefix_kernel(q0, q1, q2, q3, kv_mine, kv_other, o0, o1, o2, o3):
     requests = q0.shape[0]
     rows = requests * SHARE
     step = 256
     chunks = [slice(c, c + step) for c in range(0, kv_mine.shape[0], step)]
     core = lax.rem(lax.axis_index("grp"), 2)
     lane = iota((rows, SIDE), 1)
-    outs = (o0, o1)
+    outs = (o0, o1, o2, o3)
 
     def attend(k_ref, v_ref):
         sums = jnp.zeros((rows, SIDE), F32)
@@ -243,7 +241,7 @@
                 [
                     q[:, (k * GROUP + i) * HD : (k * GROUP + i + 1) * HD]
                     for i in range(GROUP)
-                    for q in (q0, q1)
+                    for q in (q0, q1, q2, q3)
                 ],
                 axis=0,
             )
@@ -277,14 +275,13 @@
         attend(kv_other, kv_mine)
 
 
-def join_kernel(
-    got_hbm, own_hbm, where_hbm, p0_hbm, p1_hbm, out_ref, got_ref, own_ref, where_ref, p0, p1, sems
-):
-    hbm, vmem = (got_hbm, own_hbm, where_hbm, p0_hbm, p1_hbm), (got_ref, own_ref, where_ref, p0, p1)
+def join_kernel(*refs):
+    hbm, out_ref, vmem, sems = refs[:7], refs[7], refs[8:15], refs[15]
     for copy in load(hbm, vmem, sems):
         copy.wait()
+    got_ref, own_ref, where_ref, *served = vmem
     entries = where_ref.shape[0]
-    requests = p0.shape[0]
+    requests = served[0].shape[0]
     cells = got_ref.shape[0] * CAP
     pool = own_ref.shape[0]
     lane = iota((entries, 128), 1)
@@ -295,7 +292,7 @@
     sums = side + pltpu.roll(side, SIDE - QH, 1) + pltpu.roll(side, SIDE - 2 * QH, 1)
     sums = jnp.where(where >= 0.0, sums, VERY_LOW)
     turn = my_turn()
-    for o, p_ref in enumerate((p0, p1)):
+    for o, p_ref in enumerate(served):
         turned = turn ^ o
         at = pl.multiple_of(turned * BLOCK, 128)
         cols = pl.ds(at, BLOCK)
@@ -345,55 +342,35 @@
     devices = lax.axis_size("blk")
     group = lax.axis_size("grp")
     depth = prefix_keys.shape[0]
-    each = depth // (group // (2 * SHARE))
-    share, mine, away = call(
-        share_kernel,
-        [((devices * each, KV), BF16), ((requests, BLOCK), BF16), ((requests, BLOCK), BF16)],
-        10**7,
-        prefix_keys,
-        prefix_values,
-        queries,
-        in_hbm=range(3),
-        scratch=(pltpu.VMEM((depth, KV), BF16), like(queries), pltpu.SemaphoreType.DMA((2,))),
-    )
-    swap = lambda x: lax.ppermute(x, "grp", [(i, i ^ 2) for i in range(group)])
-    exchange = lambda x: lax.all_to_all(x, "blk", split_axis=0, concat_axis=0, tiled=True)
-    part = exchange(share.reshape(devices, each, KV)).reshape(devices * each, KV)
+    each = depth // 2
     tables, lengths, places = (
         page_table.T, suffix_len.reshape(1, requests), place.reshape(-1, 128)
     )
-    send, local, where = call(
+    wide = ROW + each // CAP * KV
+    send, local, where, *asked = call(
         functools.partial(route_kernel, pool),
-        [((devices, CAP, ROW), BF16), ((pool, ROW), BF16), ((requests * MAXP, 128), F32)],
+        [((devices, CAP, wide), BF16), ((pool, ROW), BF16), ((requests * MAXP, 128), F32)]
+        + [((requests, BLOCK), BF16)] * SHARE,
         10**8,
         queries,
         tables,
         lengths,
         places,
-        in_hbm=range(4),
-        scratch=(*map(like, (queries, tables, lengths, places)), pltpu.SemaphoreType.DMA((4,))),
-    )
-    send, part = lax.optimization_barrier((send, part))
+        prefix_keys,
+        prefix_values,
+        in_hbm=range(6),
+        scratch=(
+            *map(like, (queries, tables, lengths, places)),
+            pltpu.VMEM((depth, KV), BF16),
+            pltpu.SemaphoreType.DMA((5,)),
+        ),
+    )
+    flip = lambda x, bits: lax.ppermute(x, "grp", [(i, i ^ bits) for i in range(group)])
+    turned = lambda xs: [flip(x, (0, 2, 8, 10)[o]) if o else x for o, x in enumerate(xs)]
+    exchange = lambda x: lax.all_to_all(x, "blk", split_axis=0, concat_axis=0, tiled=True)
     got = exchange(send)
-    around = [
-        lax.ppermute(part, "grp", [(i, (i + 2 * SHARE * y) % group) for i in range(group)])
-        for y in range(1, group // (2 * SHARE))
-    ]
-    kv_mine = jnp.concatenate([part, *around], axis=0)
-    kv_other = lax.ppermute(kv_mine, "grp", [(i, i ^ 1) for i in range(group)])
-    asked = swap(away)
-    local, kv_mine, kv_other, asked = lax.optimization_barrier((local, kv_mine, kv_other, asked))
-    served, away = call(
-        prefix_kernel,
-        [((requests, BLOCK + SIDE), BF16)] * SHARE,
-        10**9,
-        mine,
-        asked,
-        kv_mine,
-        kv_other,
-        room=40 << 20,
-    )
-    away = swap(away)
+    asked = turned(asked)
+    local, *asked = lax.optimization_barrier((local, *asked))
     answer, own = call(
         pages_kernel,
         [((devices, CAP, ROW), BF16), ((pool, ROW), BF16)],
@@ -404,19 +381,33 @@
         suffix_values,
         in_hbm=range(4),
         scratch=(
-            *map(like, (got, local, suffix_keys, suffix_values)),
+            pltpu.VMEM((devices, CAP, ROW), BF16),
+            *map(like, (local, suffix_keys, suffix_values)),
             pltpu.SemaphoreType.DMA((KVH + 2,)),
         ),
     )
     back = exchange(answer)
-    last = (back, own, where, served, away)
+    part, own = lax.optimization_barrier((got[:, :, ROW:], own))
+    part = part.reshape(devices * each, KV)
+    kv_mine = jnp.concatenate([part, flip(part, 4)], axis=0)
+    kv_other = flip(kv_mine, 1)
+    served = call(
+        prefix_kernel,
+        [((requests, BLOCK + SIDE), BF16)] * SHARE,
+        10**9,
+        *asked,
+        kv_mine,
+        kv_other,
+        room=40 << 20,
+    )
+    last = (back, own, where, *turned(served))
     (out,) = call(
         join_kernel,
         [((requests, QCOLS), BF16)],
         10**8,
         *last,
-        in_hbm=range(5),
-        scratch=(*map(like, last), pltpu.SemaphoreType.DMA((5,))),
+        in_hbm=range(len(last)),
+        scratch=(*map(like, last), pltpu.SemaphoreType.DMA((len(last),))),
         room=32 << 20,
     )
     return out

time: 140 us -> 125 us (0.89)
  waiting for transfers between devices: 59.8 us -> 48.2 us
  local copies, waits for them, and re-layouts: 3.43 us -> 1.19 us
    all_to_all x3 -> x2, waiting for transfers between devices: 41.5 us -> 26.5 us  [body(): lax.all_to_all(x, 'blk', split_axis=0, concat_axis=0, tiled=True)]
    ppermute x6 -> x8, starting transfers between devices: 22.8 us -> 29.8 us  [body(): lax.ppermute(x, 'grp', [(i, i ^ bits) for i in range(group)])]
    all_to_all x3 -> x2, starting transfers between devices: 32.6 us -> 26 us  [body(): lax.all_to_all(x, 'blk', split_axis=0, concat_axis=0, tiled=True)]
    ppermute x6 -> x8, waiting for transfers between devices: 18.4 us -> 21.7 us  [body(): lax.ppermute(x, 'grp', [(i, i ^ bits) for i in range(group)])]
    unnamed x17 -> x15, local copies, waits for them, and re-layouts: 3.41 us -> 1 us
    pallas_call x5 -> x4, Pallas kernels: 19.1 us -> 18.1 us  [call(): pl.pallas_call(kernel, out_shape=[jax.ShapeDtypeStruct(s, d) for s, d in...]
  transfers between devices with their start and end apart: 9 -> 10, of which waited for: 7 -> 5; matrix products, arithmetic and copies ran while one was open for 0% -> 0% of each run, Pallas kernels for 4% -> 2%
where the time goes in v3:
time: 125 us; the launch traced here: 124 us
  starting transfers between devices  55.8 us (45%)
  waiting for transfers between devices  48.2 us (39%)
  Pallas kernels  18.1 us (14%)
    ppermute x8, starting transfers between devices, body(): lax.ppermute(x, 'grp', [(i, i ^ bits) for i in range(group)])  29.8 us
    all_to_all x2, waiting for transfers between devices, body(): lax.all_to_all(x, 'blk', split_axis=0, concat_axis=0, tiled=True)  26.5 us
    all_to_all x2, starting transfers between devices, body(): lax.all_to_all(x, 'blk', split_axis=0, concat_axis=0, tiled=True)  26 us
    ppermute x8, waiting for transfers between devices, body(): lax.ppermute(x, 'grp', [(i, i ^ bits) for i in range(group)])  21.7 us
    pallas_call x4, Pallas kernels, call(): pl.pallas_call(kernel, out_shape=[jax.ShapeDtypeStruct(s, d) for s, d in...  18.1 us
  transfers between devices with their start and end apart: 10, of which 5 were waited for; matrix products, arithmetic and copies ran while one was open for 0% of the time, Pallas kernels for 2%

profile of v3, /device:TPU:1, one launch (start us, length us, event | category | flops | bytes accessed | tf_op | source)
XLA Modules:
  0.0 123.6 jit_solution(11551696240889856846)
XLA Ops:
  0.0 3.4 %shard_map.82 = (bf16[32,2,7296]{2,1,0:T(2,128)(2,1)}, bf16[48,5248]{1,0:T(8,128)(2,1)}, f32[128,128]{1,0:T(8,128)}, bf16[32,1280]{1,0:T(8,128)(2,1)}, bf16[32,1...) custom-call(bf16[32,5120]{1,0:T(8,128)(2,1)} %q_hbm.1, s32[4,32]{1,0:T(4,128)} %bitcast.4, ...), custom_call_target="tpu_custom_call" | custom-call | flops 100000000 | bytes 4194304 | tf_op jit(solution)/shard_map/pallas_call | solution.py:323
  3.4 0.0 copy-start.6
  3.4 17.1 %all-to-all-start = ((bf16[32,2,7296]{2,1,0:T(2,128)(2,1)}), bf16[32,2,7296]{2,1,0:T(2,128)(2,1)S(1)}, u32[]{:S(2)}, u32[]{:S(2)}) async-start(bf16[32,2,7296]{2,1,0:T(2,128)(2,1)} %get-tuple-element.25), calls=%async_computation | async-start | bytes 1867776 | tf_op jit(solution)/shard_map/all_to_all | solution.py:370
  20.5 4.4 %collective-permute-start = (bf16[32,1280]{1,0:T(8,128)(2,1)S(1)}, bf16[32,1280]{1,0:T(8,128)(2,1)S(1)}, u32[]{:S(2)}, u32[]{:S(2)}) collective-permute-start(bf16[32,1280]{1,0:T(8,128)(2,1)S(1)} %copy-done.6), channel_id=1, source_target_pairs={{0,64},{32,96},{64,0},{96,32},{128,192},{160,224},{192,128},{224,1... | collective-permute-start | bytes 245768 | tf_op jit(solution)/shard_map/ppermute | solution.py:368
  24.9 0.0 copy-done.5
  24.9 4.8 %collective-permute-start.1 = (bf16[32,1280]{1,0:T(8,128)(2,1)S(1)}, bf16[32,1280]{1,0:T(8,128)(2,1)S(1)}, u32[]{:S(2)}, u32[]{:S(2)}) collective-permute-start(bf16[32,1280]{1,0:T(8,128)(2,1)S(1)} %copy-done.5), channel_id=1, source_target_pairs={{0,256},{32,288},{64,320},{96,352},{128,384},{160,416},{192,448},{... | collective-permute-start | bytes 245768 | tf_op jit(solution)/shard_map/ppermute | solution.py:368
  29.8 2.2 %collective-permute-start.2 = (bf16[32,1280]{1,0:T(8,128)(2,1)S(1)}, bf16[32,1280]{1,0:T(8,128)(2,1)S(1)}, u32[]{:S(2)}, u32[]{:S(2)}) collective-permute-start(bf16[32,1280]{1,0:T(8,128)(2,1)S(1)} %copy-done.4), channel_id=1, source_target_pairs={{0,320},{32,352},{64,256},{96,288},{128,448},{160,480},{192,384},{... | collective-permute-start | bytes 245768 | tf_op jit(solution)/shard_map/ppermute | solution.py:368
  32.0 0.0 collective-permute-done.q1
  32.0 0.0 collective-permute-done.1.q2
  32.0 7.3 %collective-permute-done.2.q3 = bf16[32,1280]{1,0:T(8,128)(2,1)S(1)} collective-permute-done((bf16[32,1280]{1,0:T(8,128)(2,1)S(1)}, bf16[32,1280]{1,0:T(8,128)(2,1)S(1)}, u32[]{:S(2)}, u32[]{:S(2)}) %collective-permute-start.2) | collective-permute-done | bytes 81952 | tf_op jit(solution)/shard_map/ppermute | solution.py:368
  39.2 26.5 %all-to-all-done.got_hbm = bf16[32,2,7296]{2,1,0:T(2,128)(2,1)S(1)} async-done(((bf16[32,2,7296]{2,1,0:T(2,128)(2,1)}), bf16[32,2,7296]{2,1,0:T(2,128)(2,1)S(1)}, u32[]{:S(2)}, u32[]{:S(2)}) %all-to-all-start) | async-done | bytes 933920 | tf_op jit(solution)/shard_map/all_to_all | solution.py:370
  65.8 1.0 copy-done.3
  66.7 8.0 %shard_map.83 = (bf16[32,2,5248]{2,1,0:T(2,128)(2,1)}, bf16[48,5248]{1,0:T(8,128)(2,1)}) custom-call(bf16[32,2,7296]{2,1,0:T(2,128)(2,1)} %copy-done.3, bf16[48,5248]{1,0:T(8,128)(2,1)} %get-tuple-element.31.local_hbm, bf16[48,16,1024]{2,1,0:T(8,128)(2,1)} %k_hbm.1, bf16[48,16,1024]{2,1,0:T(8,128)(2,1)} %v_hbm.1), custom_call_target="tpu_custom_call" | custom-call | flops 1000000000 | bytes 4194304 | tf_op jit(solution)/shard_map/pallas_call | solution.py:323
  74.7 0.0 slice-start
  74.7 0.0 copy-start.2
  74.7 8.9 %all-to-all-start.1 = ((bf16[32,2,5248]{2,1,0:T(2,128)(2,1)}), bf16[32,2,5248]{2,1,0:T(2,128)(2,1)S(1)}, u32[]{:S(2)}, u32[]{:S(2)}) async-start(bf16[32,2,5248]{2,1,0:T(2,128)(2,1)} %get-tuple-element.32), calls=%async_computation.1 | async-start | bytes 1343488 | tf_op jit(solution)/shard_map/all_to_all | solution.py:370
  83.6 0.0 slice-done
  83.6 0.2 reshape.11
  83.8 3.2 %collective-permute-start.3 = (bf16[512,256]{1,0:T(8,128)(2,1)S(1)}, bf16[512,256]{1,0:T(8,128)(2,1)S(1)}, u32[]{:S(2)}, u32[]{:S(2)}) collective-permute-start(bf16[512,256]{1,0:T(8,128)(2,1)S(1)} %reshape.11), channel_id=1, source_target_pairs={{0,128},{32,160},{64,192},{96,224},{128,0},{160,32},{192,64},{224,... | collective-permute-start | bytes 786440 | tf_op jit(solution)/shard_map/ppermute | solution.py:368
  87.1 5.6 %collective-permute-done.3 = bf16[512,256]{1,0:T(8,128)(2,1)S(1)} collective-permute-done((bf16[512,256]{1,0:T(8,128)(2,1)S(1)}, bf16[512,256]{1,0:T(8,128)(2,1)S(1)}, u32[]{:S(2)}, u32[]{:S(2)}) %collective-permute-start.3) | collective-permute-done | bytes 262176 | tf_op jit(solution)/shard_map/ppermute | solution.py:368
  92.7 3.9 %collective-permute-start.4 = (bf16[1024,256]{1,0:T(8,128)(2,1)S(1)}, bf16[1024,256]{1,0:T(8,128)(2,1)S(1)}, u32[]{:S(2)}, u32[]{:S(2)}) collective-permute-start(bf16[1024,256]{1,0:T(8,128)(2,1)S(1)} %constant_dynamic-update-slice_fusion.kv_mine), channel_id=1, source_target_pairs={{0,32},{32,0},{64,96},{96,64},{128,160},{160,128},{192,224},{224,1... | collective-permute-start | bytes 1572872 | tf_op jit(solution)/shard_map/ppermute | solution.py:368
  96.5 1.5 %collective-permute-done.4.kv_other = bf16[1024,256]{1,0:T(8,128)(2,1)S(1)} collective-permute-done((bf16[1024,256]{1,0:T(8,128)(2,1)S(1)}, bf16[1024,256]{1,0:T(8,128)(2,1)S(1)}, u32[]{:S(2)}, u32[]{:S(2)}) %collective-permute-start.4) | collective-permute-done | bytes 524320 | tf_op jit(solution)/shard_map/ppermute | solution.py:368
  98.0 2.8 %shard_map.84 = (bf16[32,1408]{1,0:T(8,128)(2,1)S(1)}, bf16[32,1408]{1,0:T(8,128)(2,1)S(1)}, bf16[32,1408]{1,0:T(8,128)(2,1)S(1)}, bf16[32,1408]{1,0:T(8,128)(2,1)S(1)}) custom-call(bf16[32,1280]{1,0:T(8,128)(2,1)S(1)} %copy-done.2, bf16[32,1280]{1,0:T(8,128)(2,1)S(1)} %collective-permute-done.q1, bf16[32,1280]{1,0:T(8,128)(2,1)S(1)} %collective-permute-done.1.q2, ...), custom_call_target="tpu_custom_call" | custom-call | flops 1000000000 | bytes 4194304 | tf_op jit(solution)/shard_map/pallas_call | solution.py:323
  100.8 4.4 %collective-permute-start.5 = (bf16[32,1408]{1,0:T(8,128)(2,1)S(1)}, bf16[32,1408]{1,0:T(8,128)(2,1)S(1)}, u32[]{:S(2)}, u32[]{:S(2)}) collective-permute-start(bf16[32,1408]{1,0:T(8,128)(2,1)S(1)} %get-tuple-element.42), channel_id=1, source_target_pairs={{0,64},{32,96},{64,0},{96,32},{128,192},{160,224},{192,128},{224,1... | collective-permute-start | bytes 270344 | tf_op jit(solution)/shard_map/ppermute | solution.py:368
  105.2 4.8 %collective-permute-start.6 = (bf16[32,1408]{1,0:T(8,128)(2,1)S(1)}, bf16[32,1408]{1,0:T(8,128)(2,1)S(1)}, u32[]{:S(2)}, u32[]{:S(2)}) collective-permute-start(bf16[32,1408]{1,0:T(8,128)(2,1)S(1)} %get-tuple-element.43), channel_id=1, source_target_pairs={{0,256},{32,288},{64,320},{96,352},{128,384},{160,416},{192,448},{... | collective-permute-start | bytes 270344 | tf_op jit(solution)/shard_map/ppermute | solution.py:368
  110.0 2.2 %collective-permute-start.7 = (bf16[32,1408]{1,0:T(8,128)(2,1)S(1)}, bf16[32,1408]{1,0:T(8,128)(2,1)S(1)}, u32[]{:S(2)}, u32[]{:S(2)}) collective-permute-start(bf16[32,1408]{1,0:T(8,128)(2,1)S(1)} %get-tuple-element.44), channel_id=1, source_target_pairs={{0,320},{32,352},{64,256},{96,288},{128,448},{160,480},{192,384},{... | collective-permute-start | bytes 270344 | tf_op jit(solution)/shard_map/ppermute | solution.py:368
  112.2 0.0 collective-permute-done.5.refs_4_
  112.3 0.0 collective-permute-done.6.refs_5_
  112.3 7.3 %collective-permute-done.7.refs_6_ = bf16[32,1408]{1,0:T(8,128)(2,1)S(1)} collective-permute-done((bf16[32,1408]{1,0:T(8,128)(2,1)S(1)}, bf16[32,1408]{1,0:T(8,128)(2,1)S(1)}, u32[]{:S(2)}, u32[]{:S(2)}) %collective-permute-start.7) | collective-permute-done | bytes 90144 | tf_op jit(solution)/shard_map/ppermute | solution.py:368
  119.6 0.0 all-to-all-done.1.refs_0_
  119.6 0.0 copy-done
  119.6 4.0 %shard_map.85 = bf16[32,5120]{1,0:T(8,128)(2,1)} custom-call(bf16[32,2,5248]{2,1,0:T(2,128)(2,1)S(1)} %all-to-all-done.1.refs_0_, bf16[48,5248]{1,0:T(8,128)(2,1)S(1)} %copy-done, f32[128,128]{1,0:T(8,128)S(1)} %copy-done.1, bf16[32,1408]{1,0:T(8,128)(2,1)S(1)} %get-tuple-element.41.refs_3_, bf16[32,1408]{1,0:T(8,128)(2,1)S(1)} %collective-permute-done.5.refs_4_, ...), custom_call_target="tpu_custom_call" | custom-call | flops 100000000 | bytes 4194304 | tf_op jit(solution)/shard_map/pallas_call | solution.py:323
  (11 shorter events, 0.1 us)
Async XLA Ops:
  3.4 17.1 %copy-start.6 = (bf16[32,1280]{1,0:T(8,128)(2,1)S(1)}, bf16[32,1280]{1,0:T(8,128)(2,1)}, u32[]{:S(2)}) copy-start(bf16[32,1280]{1,0:T(8,128)(2,1)} %get-tuple-element.28) | copy-start | bytes 245764
  3.4 21.5 %copy-start.5 = (bf16[32,1280]{1,0:T(8,128)(2,1)S(1)}, bf16[32,1280]{1,0:T(8,128)(2,1)}, u32[]{:S(2)}) copy-start(bf16[32,1280]{1,0:T(8,128)(2,1)} %get-tuple-element.29) | copy-start | bytes 245764
  3.4 26.3 %copy-start.4 = (bf16[32,1280]{1,0:T(8,128)(2,1)S(1)}, bf16[32,1280]{1,0:T(8,128)(2,1)}, u32[]{:S(2)}) copy-start(bf16[32,1280]{1,0:T(8,128)(2,1)} %get-tuple-element.30) | copy-start | bytes 245764
  3.4 62.3 %all-to-all-start = ((bf16[32,2,7296]{2,1,0:T(2,128)(2,1)}), bf16[32,2,7296]{2,1,0:T(2,128)(2,1)S(1)}, u32[]{:S(2)}, u32[]{:S(2)}) async-start(bf16[32,2,7296]{2,1,0:T(2,128)(2,1)} %get-tuple-element.25), calls=%async_computation | async-start | bytes 1867776 | tf_op jit(solution)/shard_map/all_to_all | solution.py:370
  20.5 11.4 %collective-permute-start = (bf16[32,1280]{1,0:T(8,128)(2,1)S(1)}, bf16[32,1280]{1,0:T(8,128)(2,1)S(1)}, u32[]{:S(2)}, u32[]{:S(2)}) collective-permute-start(bf16[32,1280]{1,0:T(8,128)(2,1)S(1)} %copy-done.6), channel_id=1, source_target_pairs={{0,64},{32,96},{64,0},{96,32},{128,192},{160,224},{192,128},{224,1... | collective-permute-start | bytes 245768 | tf_op jit(solution)/shard_map/ppermute | solution.py:368
  24.9 7.1 %collective-permute-start.1 = (bf16[32,1280]{1,0:T(8,128)(2,1)S(1)}, bf16[32,1280]{1,0:T(8,128)(2,1)S(1)}, u32[]{:S(2)}, u32[]{:S(2)}) collective-permute-start(bf16[32,1280]{1,0:T(8,128)(2,1)S(1)} %copy-done.5), channel_id=1, source_target_pairs={{0,256},{32,288},{64,320},{96,352},{128,384},{160,416},{192,448},{... | collective-permute-start | bytes 245768 | tf_op jit(solution)/shard_map/ppermute | solution.py:368
  29.8 9.5 %collective-permute-start.2 = (bf16[32,1280]{1,0:T(8,128)(2,1)S(1)}, bf16[32,1280]{1,0:T(8,128)(2,1)S(1)}, u32[]{:S(2)}, u32[]{:S(2)}) collective-permute-start(bf16[32,1280]{1,0:T(8,128)(2,1)S(1)} %copy-done.4), channel_id=1, source_target_pairs={{0,320},{32,352},{64,256},{96,288},{128,448},{160,480},{192,384},{... | collective-permute-start | bytes 245768 | tf_op jit(solution)/shard_map/ppermute | solution.py:368
  65.8 1.0 copy-start.3
  74.7 8.9 %slice-start = ((bf16[32,2,7296]{2,1,0:T(2,128)(2,1)}), bf16[32,2,2048]{2,1,0:T(2,128)(2,1)S(1)}, s32[]{:S(2)}) async-start(bf16[32,2,7296]{2,1,0:T(2,128)(2,1)} %copy-done.3), calls=%async_computation.2 | async-start | bytes 524288 | tf_op jit(solution)/shard_map/slice | solution.py:390
  74.7 23.3 %copy-start.2 = (bf16[32,1280]{1,0:T(8,128)(2,1)S(1)}, bf16[32,1280]{1,0:T(8,128)(2,1)}, u32[]{:S(2)}) copy-start(bf16[32,1280]{1,0:T(8,128)(2,1)} %get-tuple-element.36.q0) | copy-start | bytes 245764
  74.7 44.9 %all-to-all-start.1 = ((bf16[32,2,5248]{2,1,0:T(2,128)(2,1)}), bf16[32,2,5248]{2,1,0:T(2,128)(2,1)S(1)}, u32[]{:S(2)}, u32[]{:S(2)}) async-start(bf16[32,2,5248]{2,1,0:T(2,128)(2,1)} %get-tuple-element.32), calls=%async_computation.1 | async-start | bytes 1343488 | tf_op jit(solution)/shard_map/all_to_all | solution.py:370
  83.8 8.8 %collective-permute-start.3 = (bf16[512,256]{1,0:T(8,128)(2,1)S(1)}, bf16[512,256]{1,0:T(8,128)(2,1)S(1)}, u32[]{:S(2)}, u32[]{:S(2)}) collective-permute-start(bf16[512,256]{1,0:T(8,128)(2,1)S(1)} %reshape.11), channel_id=1, source_target_pairs={{0,128},{32,160},{64,192},{96,224},{128,0},{160,32},{192,64},{224,... | collective-permute-start | bytes 786440 | tf_op jit(solution)/shard_map/ppermute | solution.py:368
  92.6 27.0 %copy-start = (bf16[48,5248]{1,0:T(8,128)(2,1)S(1)}, bf16[48,5248]{1,0:T(8,128)(2,1)}, u32[]{:S(2)}) copy-start(bf16[48,5248]{1,0:T(8,128)(2,1)} %get-tuple-element.34.refs_1_) | copy-start | bytes 1511428
  92.7 27.0 %copy-start.1 = (f32[128,128]{1,0:T(8,128)S(1)}, f32[128,128]{1,0:T(8,128)}, u32[]{:S(2)}) copy-start(f32[128,128]{1,0:T(8,128)} %get-tuple-element.35.refs_2_) | copy-start | bytes 196612
  92.7 5.4 %collective-permute-start.4 = (bf16[1024,256]{1,0:T(8,128)(2,1)S(1)}, bf16[1024,256]{1,0:T(8,128)(2,1)S(1)}, u32[]{:S(2)}, u32[]{:S(2)}) collective-permute-start(bf16[1024,256]{1,0:T(8,128)(2,1)S(1)} %constant_dynamic-update-slice_fusion.kv_mine), channel_id=1, source_target_pairs={{0,32},{32,0},{64,96},{96,64},{128,160},{160,128},{192,224},{224,1... | collective-permute-start | bytes 1572872 | tf_op jit(solution)/shard_map/ppermute | solution.py:368
  100.8 11.4 %collective-permute-start.5 = (bf16[32,1408]{1,0:T(8,128)(2,1)S(1)}, bf16[32,1408]{1,0:T(8,128)(2,1)S(1)}, u32[]{:S(2)}, u32[]{:S(2)}) collective-permute-start(bf16[32,1408]{1,0:T(8,128)(2,1)S(1)} %get-tuple-element.42), channel_id=1, source_target_pairs={{0,64},{32,96},{64,0},{96,32},{128,192},{160,224},{192,128},{224,1... | collective-permute-start | bytes 270344 | tf_op jit(solution)/shard_map/ppermute | solution.py:368
  105.2 7.1 %collective-permute-start.6 = (bf16[32,1408]{1,0:T(8,128)(2,1)S(1)}, bf16[32,1408]{1,0:T(8,128)(2,1)S(1)}, u32[]{:S(2)}, u32[]{:S(2)}) collective-permute-start(bf16[32,1408]{1,0:T(8,128)(2,1)S(1)} %get-tuple-element.43), channel_id=1, source_target_pairs={{0,256},{32,288},{64,320},{96,352},{128,384},{160,416},{192,448},{... | collective-permute-start | bytes 270344 | tf_op jit(solution)/shard_map/ppermute | solution.py:368
  110.0 9.6 %collective-permute-start.7 = (bf16[32,1408]{1,0:T(8,128)(2,1)S(1)}, bf16[32,1408]{1,0:T(8,128)(2,1)S(1)}, u32[]{:S(2)}, u32[]{:S(2)}) collective-permute-start(bf16[32,1408]{1,0:T(8,128)(2,1)S(1)} %get-tuple-element.44), channel_id=1, source_target_pairs={{0,320},{32,352},{64,256},{96,288},{128,448},{160,480},{192,384},{... | collective-permute-start | bytes 270344 | tf_op jit(solution)/shard_map/ppermute | solution.py:368

commit v4 on v3

--- a/solution.py
+++ b/solution.py
@@ -140,11 +140,13 @@
         at = pl.multiple_of((turn ^ o) * BLOCK, BLOCK)
         ref[...] = q_ref[:, pl.ds(at, BLOCK)]
     fetch_rows(pk_hbm).wait()
-    shape = (cells, rows_ref.shape[0])
-    deep = rows_ref.shape[0] // 2
-    half = deep * lax.rem(lax.div(group, 4), 2)
-    for p in range(deep // CAP):
-        one = iota(shape, 1) == half + deep // CAP * lax.rem(iota(shape, 0), CAP) + p
+    depth = rows_ref.shape[0]
+    shape = (cells, depth)
+    cell = iota(shape, 0)
+    each = depth // 4 // CAP
+    first = depth // 2 * lax.rem(lax.div(group, 4), 2) + depth // 4 * lax.div(cell, cells // 2)
+    for p in range(each):
+        one = iota(shape, 1) == first + each * lax.rem(cell, CAP) + p
         rows = dot(jnp.where(one, 1.0, 0.0).astype(BF16), rows_ref[...]).astype(BF16)
         send_ref[:, :, ROW + KV * p : ROW + KV * (p + 1)] = rows.reshape(devices, CAP, KV)
 
@@ -342,7 +344,7 @@
     devices = lax.axis_size("blk")
     group = lax.axis_size("grp")
     depth = prefix_keys.shape[0]
-    each = depth // 2
+    each = depth // 4
     tables, lengths, places = (
         page_table.T, suffix_len.reshape(1, requests), place.reshape(-1, 128)
     )
@@ -389,7 +391,14 @@
     back = exchange(answer)
     part, own = lax.optimization_barrier((got[:, :, ROW:], own))
     part = part.reshape(devices * each, KV)
-    kv_mine = jnp.concatenate([part, flip(part, 4)], axis=0)
+    pairs = [(i, i ^ (devices // 2)) for i in range(devices)]
+    both = [
+        (g * devices + i, (g ^ 4) * devices + j) for g in range(group) for i, j in pairs
+    ]
+    around = [
+        flip(part, 4), lax.ppermute(part, "blk", pairs), lax.ppermute(part, ("grp", "blk"), both)
+    ]
+    kv_mine = jnp.concatenate([part, *around], axis=0)
     kv_other = flip(kv_mine, 1)
     served = call(
         prefix_kernel,

time: 125 us -> 124 us (level)
  waiting for transfers between devices: 48.2 us -> 43.2 us
  starting transfers between devices: 55.8 us -> 60.3 us
    ppermute x8, waiting for transfers between devices: 21.7 us -> 15.6 us  [body(): lax.ppermute(x, 'grp', [(i, i ^ bits) for i in range(group)])]
    ppermute x0 -> x2, waiting for transfers between devices: none -> 5.57 us  [the longest x1 4.22 us: body(): lax.ppermute(part, ('grp', 'blk'), both)]
    ppermute x0 -> x2, starting transfers between devices: none -> 5.18 us  [the longest x1 3.15 us: body(): lax.ppermute(part, 'blk', pairs)]
    all_to_all x2, waiting for transfers between devices: 26.5 us -> 22 us  [body(): lax.all_to_all(x, 'blk', split_axis=0, concat_axis=0, tiled=True)]
  transfers between devices with their start and end apart: 10 -> 12, of which waited for: 5 -> 6; matrix products, arithmetic and copies ran while one was open for 0% -> 0% of each run, Pallas kernels for 2% -> 2%
where the time goes in v4:
time: 124 us; the launch traced here: 123 us
  starting transfers between devices  60.3 us (49%)
  waiting for transfers between devices  43.2 us (35%)
  Pallas kernels  18.1 us (15%)
    ppermute x8, starting transfers between devices, body(): lax.ppermute(x, 'grp', [(i, i ^ bits) for i in range(group)])  30.3 us
    all_to_all x2, starting transfers between devices, body(): lax.all_to_all(x, 'blk', split_axis=0, concat_axis=0, tiled=True)  24.8 us
    all_to_all x2, waiting for transfers between devices, body(): lax.all_to_all(x, 'blk', split_axis=0, concat_axis=0, tiled=True)  22 us
    pallas_call x4, Pallas kernels, call(): pl.pallas_call(kernel, out_shape=[jax.ShapeDtypeStruct(s, d) for s, d in...  18.1 us
    ppermute x8, waiting for transfers between devices, body(): lax.ppermute(x, 'grp', [(i, i ^ bits) for i in range(group)])  15.6 us
    ppermute x1, waiting for transfers between devices, body(): lax.ppermute(part, ('grp', 'blk'), both)  4.22 us
    ppermute x1, starting transfers between devices, body(): lax.ppermute(part, 'blk', pairs)  3.15 us
  transfers between devices with their start and end apart: 12, of which 6 were waited for; matrix products, arithmetic and copies ran while one was open for 0% of the time, Pallas kernels for 2%

profile of v4, /device:TPU:1, one launch (start us, length us, event | category | flops | bytes accessed | tf_op | source)
XLA Modules:
  0.0 123.0 jit_solution(13156242821002974394)
XLA Ops:
  0.0 3.4 %shard_map.82 = (bf16[32,2,6272]{2,1,0:T(2,128)(2,1)}, bf16[48,5248]{1,0:T(8,128)(2,1)}, f32[128,128]{1,0:T(8,128)}, bf16[32,1280]{1,0:T(8,128)(2,1)}, bf16[32,1...) custom-call(bf16[32,5120]{1,0:T(8,128)(2,1)} %q_hbm.1, s32[4,32]{1,0:T(4,128)} %bitcast.4, ...), custom_call_target="tpu_custom_call" | custom-call | flops 100000000 | bytes 4194304 | tf_op jit(solution)/shard_map/pallas_call | solution.py:325
  3.4 17.1 %all-to-all-start = ((bf16[32,2,6272]{2,1,0:T(2,128)(2,1)}), bf16[32,2,6272]{2,1,0:T(2,128)(2,1)S(1)}, u32[]{:S(2)}, u32[]{:S(2)}) async-start(bf16[32,2,6272]{2,1,0:T(2,128)(2,1)} %get-tuple-element.25), calls=%async_computation | async-start | bytes 1605632 | tf_op jit(solution)/shard_map/all_to_all | solution.py:372
  20.5 4.4 %collective-permute-start = (bf16[32,1280]{1,0:T(8,128)(2,1)S(1)}, bf16[32,1280]{1,0:T(8,128)(2,1)S(1)}, u32[]{:S(2)}, u32[]{:S(2)}) collective-permute-start(bf16[32,1280]{1,0:T(8,128)(2,1)S(1)} %copy-done.6), channel_id=1, source_target_pairs={{0,64},{32,96},{64,0},{96,32},{128,192},{160,224},{192,128},{224,1... | collective-permute-start | bytes 245768 | tf_op jit(solution)/shard_map/ppermute | solution.py:370
  24.9 4.8 %collective-permute-start.1 = (bf16[32,1280]{1,0:T(8,128)(2,1)S(1)}, bf16[32,1280]{1,0:T(8,128)(2,1)S(1)}, u32[]{:S(2)}, u32[]{:S(2)}) collective-permute-start(bf16[32,1280]{1,0:T(8,128)(2,1)S(1)} %copy-done.5), channel_id=1, source_target_pairs={{0,256},{32,288},{64,320},{96,352},{128,384},{160,416},{192,448},{... | collective-permute-start | bytes 245768 | tf_op jit(solution)/shard_map/ppermute | solution.py:370
  29.7 2.2 %collective-permute-start.2 = (bf16[32,1280]{1,0:T(8,128)(2,1)S(1)}, bf16[32,1280]{1,0:T(8,128)(2,1)S(1)}, u32[]{:S(2)}, u32[]{:S(2)}) collective-permute-start(bf16[32,1280]{1,0:T(8,128)(2,1)S(1)} %copy-done.4), channel_id=1, source_target_pairs={{0,320},{32,352},{64,256},{96,288},{128,448},{160,480},{192,384},{... | collective-permute-start | bytes 245768 | tf_op jit(solution)/shard_map/ppermute | solution.py:370
  31.9 0.0 collective-permute-done.q1
  31.9 0.0 collective-permute-done.1.q2
  32.0 7.3 %collective-permute-done.2.q3 = bf16[32,1280]{1,0:T(8,128)(2,1)S(1)} collective-permute-done((bf16[32,1280]{1,0:T(8,128)(2,1)S(1)}, bf16[32,1280]{1,0:T(8,128)(2,1)S(1)}, u32[]{:S(2)}, u32[]{:S(2)}) %collective-permute-start.2) | collective-permute-done | bytes 81952 | tf_op jit(solution)/shard_map/ppermute | solution.py:370
  39.2 22.0 %all-to-all-done.got_hbm = bf16[32,2,6272]{2,1,0:T(2,128)(2,1)S(1)} async-done(((bf16[32,2,6272]{2,1,0:T(2,128)(2,1)}), bf16[32,2,6272]{2,1,0:T(2,128)(2,1)S(1)}, u32[]{:S(2)}, u32[]{:S(2)}) %all-to-all-start) | async-done | bytes 802848 | tf_op jit(solution)/shard_map/all_to_all | solution.py:372
  61.3 0.9 copy-done.3
  62.2 8.0 %shard_map.83 = (bf16[32,2,5248]{2,1,0:T(2,128)(2,1)}, bf16[48,5248]{1,0:T(8,128)(2,1)}) custom-call(bf16[32,2,6272]{2,1,0:T(2,128)(2,1)} %copy-done.3, bf16[48,5248]{1,0:T(8,128)(2,1)} %get-tuple-element.31.local_hbm, bf16[48,16,1024]{2,1,0:T(8,128)(2,1)} %k_hbm.1, bf16[48,16,1024]{2,1,0:T(8,128)(2,1)} %v_hbm.1), custom_call_target="tpu_custom_call" | custom-call | flops 1000000000 | bytes 4194304 | tf_op jit(solution)/shard_map/pallas_call | solution.py:325
  70.2 0.0 slice-start
  70.2 0.0 copy-start.2
  70.2 7.8 %all-to-all-start.1 = ((bf16[32,2,5248]{2,1,0:T(2,128)(2,1)}), bf16[32,2,5248]{2,1,0:T(2,128)(2,1)S(1)}, u32[]{:S(2)}, u32[]{:S(2)}) async-start(bf16[32,2,5248]{2,1,0:T(2,128)(2,1)} %get-tuple-element.32), calls=%async_computation.1 | async-start | bytes 1343488 | tf_op jit(solution)/shard_map/all_to_all | solution.py:372
  78.0 0.1 reshape.11
  78.0 3.2 %collective-permute-start.3 = (bf16[256,256]{1,0:T(8,128)(2,1)S(1)}, bf16[256,256]{1,0:T(8,128)(2,1)S(1)}, u32[]{:S(2)}, u32[]{:S(2)}) collective-permute-start(bf16[256,256]{1,0:T(8,128)(2,1)S(1)} %reshape.11), channel_id=1, source_target_pairs={{0,128},{32,160},{64,192},{96,224},{128,0},{160,32},{192,64},{224,... | collective-permute-start | bytes 393224 | tf_op jit(solution)/shard_map/ppermute | solution.py:370
  81.2 3.1 %collective-permute-start.4 = (bf16[256,256]{1,0:T(8,128)(2,1)S(1)}, bf16[256,256]{1,0:T(8,128)(2,1)S(1)}, u32[]{:S(2)}, u32[]{:S(2)}) collective-permute-start(bf16[256,256]{1,0:T(8,128)(2,1)S(1)} %reshape.11), channel_id=1, source_target_pairs={{0,16},{1,17},{2,18},{3,19},{4,20},{5,21},{6,22},{7,23},{8,24},{9,... | collective-permute-start | bytes 393224 | tf_op jit(solution)/shard_map/ppermute | solution.py:399
  84.4 2.0 %collective-permute-start.5 = (bf16[256,256]{1,0:T(8,128)(2,1)S(1)}, bf16[256,256]{1,0:T(8,128)(2,1)S(1)}, u32[]{:S(2)}, u32[]{:S(2)}) collective-permute-start(bf16[256,256]{1,0:T(8,128)(2,1)S(1)} %reshape.11), channel_id=1, source_target_pairs={{0,144},{1,145},{2,146},{3,147},{4,148},{5,149},{6,150},{7,151},{8... | collective-permute-start | bytes 393224 | tf_op jit(solution)/shard_map/ppermute | solution.py:399
  86.5 0.0 collective-permute-done.3
  86.5 1.3 %collective-permute-done.4 = bf16[256,256]{1,0:T(8,128)(2,1)S(1)} collective-permute-done((bf16[256,256]{1,0:T(8,128)(2,1)S(1)}, bf16[256,256]{1,0:T(8,128)(2,1)S(1)}, u32[]{:S(2)}, u32[]{:S(2)}) %collective-permute-start.4) | collective-permute-done | bytes 131104 | tf_op jit(solution)/shard_map/ppermute | solution.py:399
  87.8 4.2 %collective-permute-done.5 = bf16[256,256]{1,0:T(8,128)(2,1)S(1)} collective-permute-done((bf16[256,256]{1,0:T(8,128)(2,1)S(1)}, bf16[256,256]{1,0:T(8,128)(2,1)S(1)}, u32[]{:S(2)}, u32[]{:S(2)}) %collective-permute-start.5) | collective-permute-done | bytes 131104 | tf_op jit(solution)/shard_map/ppermute | solution.py:399
  92.1 4.3 %collective-permute-start.6 = (bf16[1024,256]{1,0:T(8,128)(2,1)S(1)}, bf16[1024,256]{1,0:T(8,128)(2,1)S(1)}, u32[]{:S(2)}, u32[]{:S(2)}) collective-permute-start(bf16[1024,256]{1,0:T(8,128)(2,1)S(1)} %constant_dynamic-update-slice_fusion.kv_mine), channel_id=1, source_target_pairs={{0,32},{32,0},{64,96},{96,64},{128,160},{160,128},{192,224},{224,1... | collective-permute-start | bytes 1572872 | tf_op jit(solution)/shard_map/ppermute | solution.py:370
  96.5 1.5 %collective-permute-done.6.kv_other = bf16[1024,256]{1,0:T(8,128)(2,1)S(1)} collective-permute-done((bf16[1024,256]{1,0:T(8,128)(2,1)S(1)}, bf16[1024,256]{1,0:T(8,128)(2,1)S(1)}, u32[]{:S(2)}, u32[]{:S(2)}) %collective-permute-start.6) | collective-permute-done | bytes 524320 | tf_op jit(solution)/shard_map/ppermute | solution.py:370
  98.0 2.8 %shard_map.84 = (bf16[32,1408]{1,0:T(8,128)(2,1)S(1)}, bf16[32,1408]{1,0:T(8,128)(2,1)S(1)}, bf16[32,1408]{1,0:T(8,128)(2,1)S(1)}, bf16[32,1408]{1,0:T(8,128)(2,1)S(1)}) custom-call(bf16[32,1280]{1,0:T(8,128)(2,1)S(1)} %copy-done.2, bf16[32,1280]{1,0:T(8,128)(2,1)S(1)} %collective-permute-done.q1, bf16[32,1280]{1,0:T(8,128)(2,1)S(1)} %collective-permute-done.1.q2, ...), custom_call_target="tpu_custom_call" | custom-call | flops 1000000000 | bytes 4194304 | tf_op jit(solution)/shard_map/pallas_call | solution.py:325
  100.8 4.3 %collective-permute-start.7 = (bf16[32,1408]{1,0:T(8,128)(2,1)S(1)}, bf16[32,1408]{1,0:T(8,128)(2,1)S(1)}, u32[]{:S(2)}, u32[]{:S(2)}) collective-permute-start(bf16[32,1408]{1,0:T(8,128)(2,1)S(1)} %get-tuple-element.42), channel_id=1, source_target_pairs={{0,64},{32,96},{64,0},{96,32},{128,192},{160,224},{192,128},{224,1... | collective-permute-start | bytes 270344 | tf_op jit(solution)/shard_map/ppermute | solution.py:370
  105.1 4.5 %collective-permute-start.8 = (bf16[32,1408]{1,0:T(8,128)(2,1)S(1)}, bf16[32,1408]{1,0:T(8,128)(2,1)S(1)}, u32[]{:S(2)}, u32[]{:S(2)}) collective-permute-start(bf16[32,1408]{1,0:T(8,128)(2,1)S(1)} %get-tuple-element.43), channel_id=1, source_target_pairs={{0,256},{32,288},{64,320},{96,352},{128,384},{160,416},{192,448},{... | collective-permute-start | bytes 270344 | tf_op jit(solution)/shard_map/ppermute | solution.py:370
  109.6 2.6 %collective-permute-start.9 = (bf16[32,1408]{1,0:T(8,128)(2,1)S(1)}, bf16[32,1408]{1,0:T(8,128)(2,1)S(1)}, u32[]{:S(2)}, u32[]{:S(2)}) collective-permute-start(bf16[32,1408]{1,0:T(8,128)(2,1)S(1)} %get-tuple-element.44), channel_id=1, source_target_pairs={{0,320},{32,352},{64,256},{96,288},{128,448},{160,480},{192,384},{... | collective-permute-start | bytes 270344 | tf_op jit(solution)/shard_map/ppermute | solution.py:370
  112.2 0.0 collective-permute-done.7.refs_4_
  112.2 0.0 collective-permute-done.8.refs_5_
  112.2 6.8 %collective-permute-done.9.refs_6_ = bf16[32,1408]{1,0:T(8,128)(2,1)S(1)} collective-permute-done((bf16[32,1408]{1,0:T(8,128)(2,1)S(1)}, bf16[32,1408]{1,0:T(8,128)(2,1)S(1)}, u32[]{:S(2)}, u32[]{:S(2)}) %collective-permute-start.9) | collective-permute-done | bytes 90144 | tf_op jit(solution)/shard_map/ppermute | solution.py:370
  119.0 0.0 all-to-all-done.1.refs_0_
  119.0 4.0 %shard_map.85 = bf16[32,5120]{1,0:T(8,128)(2,1)} custom-call(bf16[32,2,5248]{2,1,0:T(2,128)(2,1)S(1)} %all-to-all-done.1.refs_0_, bf16[48,5248]{1,0:T(8,128)(2,1)S(1)} %copy-done, f32[128,128]{1,0:T(8,128)S(1)} %copy-done.1, bf16[32,1408]{1,0:T(8,128)(2,1)S(1)} %get-tuple-element.41.refs_3_, bf16[32,1408]{1,0:T(8,128)(2,1)S(1)} %collective-permute-done.7.refs_4_, ...), custom_call_target="tpu_custom_call" | custom-call | flops 100000000 | bytes 4194304 | tf_op jit(solution)/shard_map/pallas_call | solution.py:325
  (17 shorter events, 0.1 us)
Async XLA Ops:
  3.4 17.1 %copy-start.6 = (bf16[32,1280]{1,0:T(8,128)(2,1)S(1)}, bf16[32,1280]{1,0:T(8,128)(2,1)}, u32[]{:S(2)}) copy-start(bf16[32,1280]{1,0:T(8,128)(2,1)} %get-tuple-element.28) | copy-start | bytes 245764
  3.4 21.5 %copy-start.5 = (bf16[32,1280]{1,0:T(8,128)(2,1)S(1)}, bf16[32,1280]{1,0:T(8,128)(2,1)}, u32[]{:S(2)}) copy-start(bf16[32,1280]{1,0:T(8,128)(2,1)} %get-tuple-element.29) | copy-start | bytes 245764
  3.4 26.3 %copy-start.4 = (bf16[32,1280]{1,0:T(8,128)(2,1)S(1)}, bf16[32,1280]{1,0:T(8,128)(2,1)}, u32[]{:S(2)}) copy-start(bf16[32,1280]{1,0:T(8,128)(2,1)} %get-tuple-element.30) | copy-start | bytes 245764
  3.4 57.9 %all-to-all-start = ((bf16[32,2,6272]{2,1,0:T(2,128)(2,1)}), bf16[32,2,6272]{2,1,0:T(2,128)(2,1)S(1)}, u32[]{:S(2)}, u32[]{:S(2)}) async-start(bf16[32,2,6272]{2,1,0:T(2,128)(2,1)} %get-tuple-element.25), calls=%async_computation | async-start | bytes 1605632 | tf_op jit(solution)/shard_map/all_to_all | solution.py:372
  20.5 11.4 %collective-permute-start = (bf16[32,1280]{1,0:T(8,128)(2,1)S(1)}, bf16[32,1280]{1,0:T(8,128)(2,1)S(1)}, u32[]{:S(2)}, u32[]{:S(2)}) collective-permute-start(bf16[32,1280]{1,0:T(8,128)(2,1)S(1)} %copy-done.6), channel_id=1, source_target_pairs={{0,64},{32,96},{64,0},{96,32},{128,192},{160,224},{192,128},{224,1... | collective-permute-start | bytes 245768 | tf_op jit(solution)/shard_map/ppermute | solution.py:370
  24.9 7.1 %collective-permute-start.1 = (bf16[32,1280]{1,0:T(8,128)(2,1)S(1)}, bf16[32,1280]{1,0:T(8,128)(2,1)S(1)}, u32[]{:S(2)}, u32[]{:S(2)}) collective-permute-start(bf16[32,1280]{1,0:T(8,128)(2,1)S(1)} %copy-done.5), channel_id=1, source_target_pairs={{0,256},{32,288},{64,320},{96,352},{128,384},{160,416},{192,448},{... | collective-permute-start | bytes 245768 | tf_op jit(solution)/shard_map/ppermute | solution.py:370
  29.7 9.5 %collective-permute-start.2 = (bf16[32,1280]{1,0:T(8,128)(2,1)S(1)}, bf16[32,1280]{1,0:T(8,128)(2,1)S(1)}, u32[]{:S(2)}, u32[]{:S(2)}) collective-permute-start(bf16[32,1280]{1,0:T(8,128)(2,1)S(1)} %copy-done.4), channel_id=1, source_target_pairs={{0,320},{32,352},{64,256},{96,288},{128,448},{160,480},{192,384},{... | collective-permute-start | bytes 245768 | tf_op jit(solution)/shard_map/ppermute | solution.py:370
  61.3 0.9 copy-start.3
  70.2 7.8 %slice-start = ((bf16[32,2,6272]{2,1,0:T(2,128)(2,1)}), bf16[32,2,1024]{2,1,0:T(2,128)(2,1)S(1)}, s32[]{:S(2)}) async-start(bf16[32,2,6272]{2,1,0:T(2,128)(2,1)} %copy-done.3), calls=%async_computation.2 | async-start | bytes 262144 | tf_op jit(solution)/shard_map/slice | solution.py:392
  70.2 27.8 %copy-start.2 = (bf16[32,1280]{1,0:T(8,128)(2,1)S(1)}, bf16[32,1280]{1,0:T(8,128)(2,1)}, u32[]{:S(2)}) copy-start(bf16[32,1280]{1,0:T(8,128)(2,1)} %get-tuple-element.36.q0) | copy-start | bytes 245764
  70.2 48.8 %all-to-all-start.1 = ((bf16[32,2,5248]{2,1,0:T(2,128)(2,1)}), bf16[32,2,5248]{2,1,0:T(2,128)(2,1)S(1)}, u32[]{:S(2)}, u32[]{:S(2)}) async-start(bf16[32,2,5248]{2,1,0:T(2,128)(2,1)} %get-tuple-element.32), calls=%async_computation.1 | async-start | bytes 1343488 | tf_op jit(solution)/shard_map/all_to_all | solution.py:372
  78.0 8.4 %collective-permute-start.3 = (bf16[256,256]{1,0:T(8,128)(2,1)S(1)}, bf16[256,256]{1,0:T(8,128)(2,1)S(1)}, u32[]{:S(2)}, u32[]{:S(2)}) collective-permute-start(bf16[256,256]{1,0:T(8,128)(2,1)S(1)} %reshape.11), channel_id=1, source_target_pairs={{0,128},{32,160},{64,192},{96,224},{128,0},{160,32},{192,64},{224,... | collective-permute-start | bytes 393224 | tf_op jit(solution)/shard_map/ppermute | solution.py:370
  81.2 6.6 %collective-permute-start.4 = (bf16[256,256]{1,0:T(8,128)(2,1)S(1)}, bf16[256,256]{1,0:T(8,128)(2,1)S(1)}, u32[]{:S(2)}, u32[]{:S(2)}) collective-permute-start(bf16[256,256]{1,0:T(8,128)(2,1)S(1)} %reshape.11), channel_id=1, source_target_pairs={{0,16},{1,17},{2,18},{3,19},{4,20},{5,21},{6,22},{7,23},{8,24},{9,... | collective-permute-start | bytes 393224 | tf_op jit(solution)/shard_map/ppermute | solution.py:399
  84.4 7.7 %collective-permute-start.5 = (bf16[256,256]{1,0:T(8,128)(2,1)S(1)}, bf16[256,256]{1,0:T(8,128)(2,1)S(1)}, u32[]{:S(2)}, u32[]{:S(2)}) collective-permute-start(bf16[256,256]{1,0:T(8,128)(2,1)S(1)} %reshape.11), channel_id=1, source_target_pairs={{0,144},{1,145},{2,146},{3,147},{4,148},{5,149},{6,150},{7,151},{8... | collective-permute-start | bytes 393224 | tf_op jit(solution)/shard_map/ppermute | solution.py:399
  92.1 26.9 %copy-start = (bf16[48,5248]{1,0:T(8,128)(2,1)S(1)}, bf16[48,5248]{1,0:T(8,128)(2,1)}, u32[]{:S(2)}) copy-start(bf16[48,5248]{1,0:T(8,128)(2,1)} %get-tuple-element.34.refs_1_) | copy-start | bytes 1511428
  92.1 26.9 %copy-start.1 = (f32[128,128]{1,0:T(8,128)S(1)}, f32[128,128]{1,0:T(8,128)}, u32[]{:S(2)}) copy-start(f32[128,128]{1,0:T(8,128)} %get-tuple-element.35.refs_2_) | copy-start | bytes 196612
  92.1 5.9 %collective-permute-start.6 = (bf16[1024,256]{1,0:T(8,128)(2,1)S(1)}, bf16[1024,256]{1,0:T(8,128)(2,1)S(1)}, u32[]{:S(2)}, u32[]{:S(2)}) collective-permute-start(bf16[1024,256]{1,0:T(8,128)(2,1)S(1)} %constant_dynamic-update-slice_fusion.kv_mine), channel_id=1, source_target_pairs={{0,32},{32,0},{64,96},{96,64},{128,160},{160,128},{192,224},{224,1... | collective-permute-start | bytes 1572872 | tf_op jit(solution)/shard_map/ppermute | solution.py:370
  100.8 11.4 %collective-permute-start.7 = (bf16[32,1408]{1,0:T(8,128)(2,1)S(1)}, bf16[32,1408]{1,0:T(8,128)(2,1)S(1)}, u32[]{:S(2)}, u32[]{:S(2)}) collective-permute-start(bf16[32,1408]{1,0:T(8,128)(2,1)S(1)} %get-tuple-element.42), channel_id=1, source_target_pairs={{0,64},{32,96},{64,0},{96,32},{128,192},{160,224},{192,128},{224,1... | collective-permute-start | bytes 270344 | tf_op jit(solution)/shard_map/ppermute | solution.py:370
  105.1 7.1 %collective-permute-start.8 = (bf16[32,1408]{1,0:T(8,128)(2,1)S(1)}, bf16[32,1408]{1,0:T(8,128)(2,1)S(1)}, u32[]{:S(2)}, u32[]{:S(2)}) collective-permute-start(bf16[32,1408]{1,0:T(8,128)(2,1)S(1)} %get-tuple-element.43), channel_id=1, source_target_pairs={{0,256},{32,288},{64,320},{96,352},{128,384},{160,416},{192,448},{... | collective-permute-start | bytes 270344 | tf_op jit(solution)/shard_map/ppermute | solution.py:370
  109.6 9.4 %collective-permute-start.9 = (bf16[32,1408]{1,0:T(8,128)(2,1)S(1)}, bf16[32,1408]{1,0:T(8,128)(2,1)S(1)}, u32[]{:S(2)}, u32[]{:S(2)}) collective-permute-start(bf16[32,1408]{1,0:T(8,128)(2,1)S(1)} %get-tuple-element.44), channel_id=1, source_target_pairs={{0,320},{32,352},{64,256},{96,288},{128,448},{160,480},{192,384},{... | collective-permute-start | bytes 270344 | tf_op jit(solution)/shard_map/ppermute | solution.py:370

commit v5 on v4

--- a/solution.py
+++ b/solution.py
@@ -57,8 +57,7 @@
 
 
 def my_turn():
-    group = lax.axis_index("grp")
-    return lax.rem(lax.div(group, 2), 2) + 2 * lax.div(group, 8)
+    return lax.div(lax.axis_index("grp"), 4)
 
 
 def route_kernel(
@@ -144,7 +143,7 @@
     shape = (cells, depth)
     cell = iota(shape, 0)
     each = depth // 4 // CAP
-    first = depth // 2 * lax.rem(lax.div(group, 4), 2) + depth // 4 * lax.div(cell, cells // 2)
+    first = depth // 2 * lax.rem(lax.div(group, 2), 2) + depth // 4 * lax.div(cell, cells // 2)
     for p in range(each):
         one = iota(shape, 1) == first + each * lax.rem(cell, CAP) + p
         rows = dot(jnp.where(one, 1.0, 0.0).astype(BF16), rows_ref[...]).astype(BF16)
@@ -277,11 +276,8 @@
         attend(kv_other, kv_mine)
 
 
-def join_kernel(*refs):
-    hbm, out_ref, vmem, sems = refs[:7], refs[7], refs[8:15], refs[15]
-    for copy in load(hbm, vmem, sems):
-        copy.wait()
-    got_ref, own_ref, where_ref, *served = vmem
+def join_kernel(got_ref, own_ref, where_ref, *refs):
+    *served, out_ref = refs
     entries = where_ref.shape[0]
     requests = served[0].shape[0]
     cells = got_ref.shape[0] * CAP
@@ -368,7 +364,7 @@
         ),
     )
     flip = lambda x, bits: lax.ppermute(x, "grp", [(i, i ^ bits) for i in range(group)])
-    turned = lambda xs: [flip(x, (0, 2, 8, 10)[o]) if o else x for o, x in enumerate(xs)]
+    turned = lambda xs: [flip(x, 4 * o) if o else x for o, x in enumerate(xs)]
     exchange = lambda x: lax.all_to_all(x, "blk", split_axis=0, concat_axis=0, tiled=True)
     got = exchange(send)
     asked = turned(asked)
@@ -393,10 +389,10 @@
     part = part.reshape(devices * each, KV)
     pairs = [(i, i ^ (devices // 2)) for i in range(devices)]
     both = [
-        (g * devices + i, (g ^ 4) * devices + j) for g in range(group) for i, j in pairs
+        (g * devices + i, (g ^ 2) * devices + j) for g in range(group) for i, j in pairs
     ]
     around = [
-        flip(part, 4), lax.ppermute(part, "blk", pairs), lax.ppermute(part, ("grp", "blk"), both)
+        flip(part, 2), lax.ppermute(part, "blk", pairs), lax.ppermute(part, ("grp", "blk"), both)
     ]
     kv_mine = jnp.concatenate([part, *around], axis=0)
     kv_other = flip(kv_mine, 1)
@@ -415,8 +411,6 @@
         [((requests, QCOLS), BF16)],
         10**8,
         *last,
-        in_hbm=range(len(last)),
-        scratch=(*map(like, last), pltpu.SemaphoreType.DMA((len(last),))),
         room=32 << 20,
     )
     return out

time: 124 us -> 119 us (0.960)
  starting transfers between devices: 60.3 us -> 58.2 us
  waiting for transfers between devices: 43.2 us -> 41.8 us
    ppermute x8, waiting for transfers between devices: 15.6 us -> 10.8 us  [body(): lax.ppermute(x, 'grp', [(i, i ^ bits) for i in range(group)])]
    all_to_all x2, waiting for transfers between devices: 22 us -> 26.3 us  [body(): lax.all_to_all(x, 'blk', split_axis=0, concat_axis=0, tiled=True)]
    ppermute x1, waiting for transfers between devices: 4.22 us -> 1.81 us  [body(): lax.ppermute(part, ('grp', 'blk'), both)]
    ppermute x8, starting transfers between devices: 30.3 us -> 28.3 us  [body(): lax.ppermute(x, 'grp', [(i, i ^ bits) for i in range(group)])]
    ppermute x1, waiting for transfers between devices: 1.35 us -> 2.89 us  [body(): lax.ppermute(part, 'blk', pairs)]
  transfers between devices with their start and end apart: 12 -> 12, of which waited for: 6 -> 8; matrix products, arithmetic and copies ran while one was open for 0% -> 0% of each run, Pallas kernels for 2% -> 2%
where the time goes in v5:
time: 119 us; the launch traced here: 118 us
  starting transfers between devices  58.2 us (49%)
  waiting for transfers between devices  41.8 us (35%)
  Pallas kernels  17 us (14%)
    ppermute x8, starting transfers between devices, body(): lax.ppermute(x, 'grp', [(i, i ^ bits) for i in range(group)])  28.3 us
    all_to_all x2, waiting for transfers between devices, body(): lax.all_to_all(x, 'blk', split_axis=0, concat_axis=0, tiled=True)  26.3 us
    all_to_all x2, starting transfers between devices, body(): lax.all_to_all(x, 'blk', split_axis=0, concat_axis=0, tiled=True)  24.8 us
    pallas_call x4, Pallas kernels, call(): pl.pallas_call(kernel, out_shape=[jax.ShapeDtypeStruct(s, d) for s, d in...  17 us
    ppermute x8, waiting for transfers between devices, body(): lax.ppermute(x, 'grp', [(i, i ^ bits) for i in range(group)])  10.8 us
    ppermute x1, waiting for transfers between devices, body(): lax.ppermute(part, 'blk', pairs)  2.89 us
    ppermute x1, starting transfers between devices, body(): lax.ppermute(part, 'blk', pairs)  2.54 us
    ppermute x1, starting transfers between devices, body(): lax.ppermute(part, ('grp', 'blk'), both)  2.47 us
  transfers between devices with their start and end apart: 12, of which 8 were waited for; matrix products, arithmetic and copies ran while one was open for 0% of the time, Pallas kernels for 2%

profile of v5, /device:TPU:1, one launch (start us, length us, event | category | flops | bytes accessed | tf_op | source)
XLA Modules:
  0.0 118.3 jit_solution(9436881887606679711)
XLA Ops:
  0.0 3.4 %shard_map.82 = (bf16[32,2,6272]{2,1,0:T(2,128)(2,1)}, bf16[48,5248]{1,0:T(8,128)(2,1)}, f32[128,128]{1,0:T(8,128)}, bf16[32,1280]{1,0:T(8,128)(2,1)}, bf16[32,1...) custom-call(bf16[32,5120]{1,0:T(8,128)(2,1)} %q_hbm.1, s32[4,32]{1,0:T(4,128)} %bitcast.4, ...), custom_call_target="tpu_custom_call" | custom-call | flops 100000000 | bytes 4194304 | tf_op jit(solution)/shard_map/pallas_call | solution.py:321
  3.4 17.1 %all-to-all-start = ((bf16[32,2,6272]{2,1,0:T(2,128)(2,1)}), bf16[32,2,6272]{2,1,0:T(2,128)(2,1)S(1)}, u32[]{:S(2)}, u32[]{:S(2)}) async-start(bf16[32,2,6272]{2,1,0:T(2,128)(2,1)} %get-tuple-element.25), calls=%async_computation | async-start | bytes 1605632 | tf_op jit(solution)/shard_map/all_to_all | solution.py:368
  20.5 3.2 %collective-permute-start = (bf16[32,1280]{1,0:T(8,128)(2,1)S(1)}, bf16[32,1280]{1,0:T(8,128)(2,1)S(1)}, u32[]{:S(2)}, u32[]{:S(2)}) collective-permute-start(bf16[32,1280]{1,0:T(8,128)(2,1)S(1)} %copy-done.6), channel_id=1, source_target_pairs={{0,128},{32,160},{64,192},{96,224},{128,0},{160,32},{192,64},{224,... | collective-permute-start | bytes 245768 | tf_op jit(solution)/shard_map/ppermute | solution.py:366
  23.7 4.5 %collective-permute-start.1 = (bf16[32,1280]{1,0:T(8,128)(2,1)S(1)}, bf16[32,1280]{1,0:T(8,128)(2,1)S(1)}, u32[]{:S(2)}, u32[]{:S(2)}) collective-permute-start(bf16[32,1280]{1,0:T(8,128)(2,1)S(1)} %copy-done.5), channel_id=1, source_target_pairs={{0,256},{32,288},{64,320},{96,352},{128,384},{160,416},{192,448},{... | collective-permute-start | bytes 245768 | tf_op jit(solution)/shard_map/ppermute | solution.py:366
  28.3 1.9 %collective-permute-start.2 = (bf16[32,1280]{1,0:T(8,128)(2,1)S(1)}, bf16[32,1280]{1,0:T(8,128)(2,1)S(1)}, u32[]{:S(2)}, u32[]{:S(2)}) collective-permute-start(bf16[32,1280]{1,0:T(8,128)(2,1)S(1)} %copy-done.4), channel_id=1, source_target_pairs={{0,384},{32,416},{64,448},{96,480},{128,256},{160,288},{192,320},{... | collective-permute-start | bytes 245768 | tf_op jit(solution)/shard_map/ppermute | solution.py:366
  30.2 0.0 collective-permute-done.q1
  30.2 0.2 collective-permute-done.1.q2
  30.4 4.5 %collective-permute-done.2.q3 = bf16[32,1280]{1,0:T(8,128)(2,1)S(1)} collective-permute-done((bf16[32,1280]{1,0:T(8,128)(2,1)S(1)}, bf16[32,1280]{1,0:T(8,128)(2,1)S(1)}, u32[]{:S(2)}, u32[]{:S(2)}) %collective-permute-start.2) | collective-permute-done | bytes 81952 | tf_op jit(solution)/shard_map/ppermute | solution.py:366
  35.0 26.3 %all-to-all-done.got_hbm = bf16[32,2,6272]{2,1,0:T(2,128)(2,1)S(1)} async-done(((bf16[32,2,6272]{2,1,0:T(2,128)(2,1)}), bf16[32,2,6272]{2,1,0:T(2,128)(2,1)S(1)}, u32[]{:S(2)}, u32[]{:S(2)}) %all-to-all-start) | async-done | bytes 802848 | tf_op jit(solution)/shard_map/all_to_all | solution.py:368
  61.3 0.9 copy-done.3
  62.2 8.0 %shard_map.83 = (bf16[32,2,5248]{2,1,0:T(2,128)(2,1)}, bf16[48,5248]{1,0:T(8,128)(2,1)}) custom-call(bf16[32,2,6272]{2,1,0:T(2,128)(2,1)} %copy-done.3, bf16[48,5248]{1,0:T(8,128)(2,1)} %get-tuple-element.31.local_hbm, bf16[48,16,1024]{2,1,0:T(8,128)(2,1)} %k_hbm.1, bf16[48,16,1024]{2,1,0:T(8,128)(2,1)} %v_hbm.1), custom_call_target="tpu_custom_call" | custom-call | flops 1000000000 | bytes 4194304 | tf_op jit(solution)/shard_map/pallas_call | solution.py:321
  70.2 0.0 slice-start
  70.2 0.0 copy-start.2
  70.2 7.8 %all-to-all-start.1 = ((bf16[32,2,5248]{2,1,0:T(2,128)(2,1)}), bf16[32,2,5248]{2,1,0:T(2,128)(2,1)S(1)}, u32[]{:S(2)}, u32[]{:S(2)}) async-start(bf16[32,2,5248]{2,1,0:T(2,128)(2,1)} %get-tuple-element.32), calls=%async_computation.1 | async-start | bytes 1343488 | tf_op jit(solution)/shard_map/all_to_all | solution.py:368
  78.0 0.1 reshape.11
  78.0 4.4 %collective-permute-start.3 = (bf16[256,256]{1,0:T(8,128)(2,1)S(1)}, bf16[256,256]{1,0:T(8,128)(2,1)S(1)}, u32[]{:S(2)}, u32[]{:S(2)}) collective-permute-start(bf16[256,256]{1,0:T(8,128)(2,1)S(1)} %reshape.11), channel_id=1, source_target_pairs={{0,64},{32,96},{64,0},{96,32},{128,192},{160,224},{192,128},{224,1... | collective-permute-start | bytes 393224 | tf_op jit(solution)/shard_map/ppermute | solution.py:366
  82.4 2.5 %collective-permute-start.4 = (bf16[256,256]{1,0:T(8,128)(2,1)S(1)}, bf16[256,256]{1,0:T(8,128)(2,1)S(1)}, u32[]{:S(2)}, u32[]{:S(2)}) collective-permute-start(bf16[256,256]{1,0:T(8,128)(2,1)S(1)} %reshape.11), channel_id=1, source_target_pairs={{0,16},{1,17},{2,18},{3,19},{4,20},{5,21},{6,22},{7,23},{8,24},{9,... | collective-permute-start | bytes 393224 | tf_op jit(solution)/shard_map/ppermute | solution.py:395
  85.0 2.5 %collective-permute-start.5 = (bf16[256,256]{1,0:T(8,128)(2,1)S(1)}, bf16[256,256]{1,0:T(8,128)(2,1)S(1)}, u32[]{:S(2)}, u32[]{:S(2)}) collective-permute-start(bf16[256,256]{1,0:T(8,128)(2,1)S(1)} %reshape.11), channel_id=1, source_target_pairs={{0,80},{1,81},{2,82},{3,83},{4,84},{5,85},{6,86},{7,87},{8,88},{9,... | collective-permute-start | bytes 393224 | tf_op jit(solution)/shard_map/ppermute | solution.py:395
  87.5 0.0 collective-permute-done.3
  87.5 2.9 %collective-permute-done.4 = bf16[256,256]{1,0:T(8,128)(2,1)S(1)} collective-permute-done((bf16[256,256]{1,0:T(8,128)(2,1)S(1)}, bf16[256,256]{1,0:T(8,128)(2,1)S(1)}, u32[]{:S(2)}, u32[]{:S(2)}) %collective-permute-start.4) | collective-permute-done | bytes 131104 | tf_op jit(solution)/shard_map/ppermute | solution.py:395
  90.4 1.8 %collective-permute-done.5 = bf16[256,256]{1,0:T(8,128)(2,1)S(1)} collective-permute-done((bf16[256,256]{1,0:T(8,128)(2,1)S(1)}, bf16[256,256]{1,0:T(8,128)(2,1)S(1)}, u32[]{:S(2)}, u32[]{:S(2)}) %collective-permute-start.5) | collective-permute-done | bytes 131104 | tf_op jit(solution)/shard_map/ppermute | solution.py:395
  92.2 4.6 %collective-permute-start.6 = (bf16[1024,256]{1,0:T(8,128)(2,1)S(1)}, bf16[1024,256]{1,0:T(8,128)(2,1)S(1)}, u32[]{:S(2)}, u32[]{:S(2)}) collective-permute-start(bf16[1024,256]{1,0:T(8,128)(2,1)S(1)} %constant_dynamic-update-slice_fusion.kv_mine), channel_id=1, source_target_pairs={{0,32},{32,0},{64,96},{96,64},{128,160},{160,128},{192,224},{224,1... | collective-permute-start | bytes 1572872 | tf_op jit(solution)/shard_map/ppermute | solution.py:366
  96.9 1.5 %collective-permute-done.6.kv_other = bf16[1024,256]{1,0:T(8,128)(2,1)S(1)} collective-permute-done((bf16[1024,256]{1,0:T(8,128)(2,1)S(1)}, bf16[1024,256]{1,0:T(8,128)(2,1)S(1)}, u32[]{:S(2)}, u32[]{:S(2)}) %collective-permute-start.6) | collective-permute-done | bytes 524320 | tf_op jit(solution)/shard_map/ppermute | solution.py:366
  98.4 2.8 %shard_map.84 = (bf16[32,1408]{1,0:T(8,128)(2,1)S(1)}, bf16[32,1408]{1,0:T(8,128)(2,1)S(1)}, bf16[32,1408]{1,0:T(8,128)(2,1)S(1)}, bf16[32,1408]{1,0:T(8,128)(2,1)S(1)}) custom-call(bf16[32,1280]{1,0:T(8,128)(2,1)S(1)} %copy-done.2, bf16[32,1280]{1,0:T(8,128)(2,1)S(1)} %collective-permute-done.q1, bf16[32,1280]{1,0:T(8,128)(2,1)S(1)} %collective-permute-done.1.q2, ...), custom_call_target="tpu_custom_call" | custom-call | flops 1000000000 | bytes 4194304 | tf_op jit(solution)/shard_map/pallas_call | solution.py:321
  101.2 3.2 %collective-permute-start.7 = (bf16[32,1408]{1,0:T(8,128)(2,1)S(1)}, bf16[32,1408]{1,0:T(8,128)(2,1)S(1)}, u32[]{:S(2)}, u32[]{:S(2)}) collective-permute-start(bf16[32,1408]{1,0:T(8,128)(2,1)S(1)} %get-tuple-element.42), channel_id=1, source_target_pairs={{0,128},{32,160},{64,192},{96,224},{128,0},{160,32},{192,64},{224,... | collective-permute-start | bytes 270344 | tf_op jit(solution)/shard_map/ppermute | solution.py:366
  104.4 4.5 %collective-permute-start.8 = (bf16[32,1408]{1,0:T(8,128)(2,1)S(1)}, bf16[32,1408]{1,0:T(8,128)(2,1)S(1)}, u32[]{:S(2)}, u32[]{:S(2)}) collective-permute-start(bf16[32,1408]{1,0:T(8,128)(2,1)S(1)} %get-tuple-element.43), channel_id=1, source_target_pairs={{0,256},{32,288},{64,320},{96,352},{128,384},{160,416},{192,448},{... | collective-permute-start | bytes 270344 | tf_op jit(solution)/shard_map/ppermute | solution.py:366
  108.9 1.9 %collective-permute-start.9 = (bf16[32,1408]{1,0:T(8,128)(2,1)S(1)}, bf16[32,1408]{1,0:T(8,128)(2,1)S(1)}, u32[]{:S(2)}, u32[]{:S(2)}) collective-permute-start(bf16[32,1408]{1,0:T(8,128)(2,1)S(1)} %get-tuple-element.44), channel_id=1, source_target_pairs={{0,384},{32,416},{64,448},{96,480},{128,256},{160,288},{192,320},{... | collective-permute-start | bytes 270344 | tf_op jit(solution)/shard_map/ppermute | solution.py:366
  110.9 0.0 collective-permute-done.7.refs_1_
  110.9 0.6 collective-permute-done.8.refs_2_
  111.5 3.9 %collective-permute-done.9.refs_3_ = bf16[32,1408]{1,0:T(8,128)(2,1)S(1)} collective-permute-done((bf16[32,1408]{1,0:T(8,128)(2,1)S(1)}, bf16[32,1408]{1,0:T(8,128)(2,1)S(1)}, u32[]{:S(2)}, u32[]{:S(2)}) %collective-permute-start.9) | collective-permute-done | bytes 90144 | tf_op jit(solution)/shard_map/ppermute | solution.py:366
  115.4 0.0 all-to-all-done.1.got_ref
  115.4 2.8 %shard_map.85 = bf16[32,5120]{1,0:T(8,128)(2,1)} custom-call(bf16[32,2,5248]{2,1,0:T(2,128)(2,1)S(1)} %all-to-all-done.1.got_ref, bf16[48,5248]{1,0:T(8,128)(2,1)S(1)} %copy-done, f32[128,128]{1,0:T(8,128)S(1)} %copy-done.1, bf16[32,1408]{1,0:T(8,128)(2,1)S(1)} %get-tuple-element.41.refs_0_, bf16[32,1408]{1,0:T(8,128)(2,1)S(1)} %collective-permute-done.7.refs_1_, ...), custom_call_target="tpu_custom_call" | custom-call | flops 100000000 | bytes 4194304 | tf_op jit(solution)/shard_map/pallas_call | solution.py:321
  (17 shorter events, 0.1 us)
Async XLA Ops:
  3.4 17.1 %copy-start.6 = (bf16[32,1280]{1,0:T(8,128)(2,1)S(1)}, bf16[32,1280]{1,0:T(8,128)(2,1)}, u32[]{:S(2)}) copy-start(bf16[32,1280]{1,0:T(8,128)(2,1)} %get-tuple-element.28) | copy-start | bytes 245764
  3.4 20.3 %copy-start.5 = (bf16[32,1280]{1,0:T(8,128)(2,1)S(1)}, bf16[32,1280]{1,0:T(8,128)(2,1)}, u32[]{:S(2)}) copy-start(bf16[32,1280]{1,0:T(8,128)(2,1)} %get-tuple-element.29) | copy-start | bytes 245764
  3.4 24.9 %copy-start.4 = (bf16[32,1280]{1,0:T(8,128)(2,1)S(1)}, bf16[32,1280]{1,0:T(8,128)(2,1)}, u32[]{:S(2)}) copy-start(bf16[32,1280]{1,0:T(8,128)(2,1)} %get-tuple-element.30) | copy-start | bytes 245764
  3.4 57.9 %all-to-all-start = ((bf16[32,2,6272]{2,1,0:T(2,128)(2,1)}), bf16[32,2,6272]{2,1,0:T(2,128)(2,1)S(1)}, u32[]{:S(2)}, u32[]{:S(2)}) async-start(bf16[32,2,6272]{2,1,0:T(2,128)(2,1)} %get-tuple-element.25), calls=%async_computation | async-start | bytes 1605632 | tf_op jit(solution)/shard_map/all_to_all | solution.py:368
  20.5 9.7 %collective-permute-start = (bf16[32,1280]{1,0:T(8,128)(2,1)S(1)}, bf16[32,1280]{1,0:T(8,128)(2,1)S(1)}, u32[]{:S(2)}, u32[]{:S(2)}) collective-permute-start(bf16[32,1280]{1,0:T(8,128)(2,1)S(1)} %copy-done.6), channel_id=1, source_target_pairs={{0,128},{32,160},{64,192},{96,224},{128,0},{160,32},{192,64},{224,... | collective-permute-start | bytes 245768 | tf_op jit(solution)/shard_map/ppermute | solution.py:366
  23.7 6.7 %collective-permute-start.1 = (bf16[32,1280]{1,0:T(8,128)(2,1)S(1)}, bf16[32,1280]{1,0:T(8,128)(2,1)S(1)}, u32[]{:S(2)}, u32[]{:S(2)}) collective-permute-start(bf16[32,1280]{1,0:T(8,128)(2,1)S(1)} %copy-done.5), channel_id=1, source_target_pairs={{0,256},{32,288},{64,320},{96,352},{128,384},{160,416},{192,448},{... | collective-permute-start | bytes 245768 | tf_op jit(solution)/shard_map/ppermute | solution.py:366
  28.3 6.7 %collective-permute-start.2 = (bf16[32,1280]{1,0:T(8,128)(2,1)S(1)}, bf16[32,1280]{1,0:T(8,128)(2,1)S(1)}, u32[]{:S(2)}, u32[]{:S(2)}) collective-permute-start(bf16[32,1280]{1,0:T(8,128)(2,1)S(1)} %copy-done.4), channel_id=1, source_target_pairs={{0,384},{32,416},{64,448},{96,480},{128,256},{160,288},{192,320},{... | collective-permute-start | bytes 245768 | tf_op jit(solution)/shard_map/ppermute | solution.py:366
  61.3 0.9 copy-start.3
  70.2 7.8 %slice-start = ((bf16[32,2,6272]{2,1,0:T(2,128)(2,1)}), bf16[32,2,1024]{2,1,0:T(2,128)(2,1)S(1)}, s32[]{:S(2)}) async-start(bf16[32,2,6272]{2,1,0:T(2,128)(2,1)} %copy-done.3), calls=%async_computation.2 | async-start | bytes 262144 | tf_op jit(solution)/shard_map/slice | solution.py:388
  70.2 28.2 %copy-start.2 = (bf16[32,1280]{1,0:T(8,128)(2,1)S(1)}, bf16[32,1280]{1,0:T(8,128)(2,1)}, u32[]{:S(2)}) copy-start(bf16[32,1280]{1,0:T(8,128)(2,1)} %get-tuple-element.36.q0) | copy-start | bytes 245764
  70.2 45.2 %all-to-all-start.1 = ((bf16[32,2,5248]{2,1,0:T(2,128)(2,1)}), bf16[32,2,5248]{2,1,0:T(2,128)(2,1)S(1)}, u32[]{:S(2)}, u32[]{:S(2)}) async-start(bf16[32,2,5248]{2,1,0:T(2,128)(2,1)} %get-tuple-element.32), calls=%async_computation.1 | async-start | bytes 1343488 | tf_op jit(solution)/shard_map/all_to_all | solution.py:368
  78.0 9.4 %collective-permute-start.3 = (bf16[256,256]{1,0:T(8,128)(2,1)S(1)}, bf16[256,256]{1,0:T(8,128)(2,1)S(1)}, u32[]{:S(2)}, u32[]{:S(2)}) collective-permute-start(bf16[256,256]{1,0:T(8,128)(2,1)S(1)} %reshape.11), channel_id=1, source_target_pairs={{0,64},{32,96},{64,0},{96,32},{128,192},{160,224},{192,128},{224,1... | collective-permute-start | bytes 393224 | tf_op jit(solution)/shard_map/ppermute | solution.py:366
  82.4 8.0 %collective-permute-start.4 = (bf16[256,256]{1,0:T(8,128)(2,1)S(1)}, bf16[256,256]{1,0:T(8,128)(2,1)S(1)}, u32[]{:S(2)}, u32[]{:S(2)}) collective-permute-start(bf16[256,256]{1,0:T(8,128)(2,1)S(1)} %reshape.11), channel_id=1, source_target_pairs={{0,16},{1,17},{2,18},{3,19},{4,20},{5,21},{6,22},{7,23},{8,24},{9,... | collective-permute-start | bytes 393224 | tf_op jit(solution)/shard_map/ppermute | solution.py:395
  85.0 7.2 %collective-permute-start.5 = (bf16[256,256]{1,0:T(8,128)(2,1)S(1)}, bf16[256,256]{1,0:T(8,128)(2,1)S(1)}, u32[]{:S(2)}, u32[]{:S(2)}) collective-permute-start(bf16[256,256]{1,0:T(8,128)(2,1)S(1)} %reshape.11), channel_id=1, source_target_pairs={{0,80},{1,81},{2,82},{3,83},{4,84},{5,85},{6,86},{7,87},{8,88},{9,... | collective-permute-start | bytes 393224 | tf_op jit(solution)/shard_map/ppermute | solution.py:395
  92.2 23.2 %copy-start = (bf16[48,5248]{1,0:T(8,128)(2,1)S(1)}, bf16[48,5248]{1,0:T(8,128)(2,1)}, u32[]{:S(2)}) copy-start(bf16[48,5248]{1,0:T(8,128)(2,1)} %get-tuple-element.34.own_ref) | copy-start | bytes 1511428
  92.2 23.2 %copy-start.1 = (f32[128,128]{1,0:T(8,128)S(1)}, f32[128,128]{1,0:T(8,128)}, u32[]{:S(2)}) copy-start(f32[128,128]{1,0:T(8,128)} %get-tuple-element.35.where_ref) | copy-start | bytes 196612
  92.2 6.2 %collective-permute-start.6 = (bf16[1024,256]{1,0:T(8,128)(2,1)S(1)}, bf16[1024,256]{1,0:T(8,128)(2,1)S(1)}, u32[]{:S(2)}, u32[]{:S(2)}) collective-permute-start(bf16[1024,256]{1,0:T(8,128)(2,1)S(1)} %constant_dynamic-update-slice_fusion.kv_mine), channel_id=1, source_target_pairs={{0,32},{32,0},{64,96},{96,64},{128,160},{160,128},{192,224},{224,1... | collective-permute-start | bytes 1572872 | tf_op jit(solution)/shard_map/ppermute | solution.py:366
  101.2 9.7 %collective-permute-start.7 = (bf16[32,1408]{1,0:T(8,128)(2,1)S(1)}, bf16[32,1408]{1,0:T(8,128)(2,1)S(1)}, u32[]{:S(2)}, u32[]{:S(2)}) collective-permute-start(bf16[32,1408]{1,0:T(8,128)(2,1)S(1)} %get-tuple-element.42), channel_id=1, source_target_pairs={{0,128},{32,160},{64,192},{96,224},{128,0},{160,32},{192,64},{224,... | collective-permute-start | bytes 270344 | tf_op jit(solution)/shard_map/ppermute | solution.py:366
  104.4 7.1 %collective-permute-start.8 = (bf16[32,1408]{1,0:T(8,128)(2,1)S(1)}, bf16[32,1408]{1,0:T(8,128)(2,1)S(1)}, u32[]{:S(2)}, u32[]{:S(2)}) collective-permute-start(bf16[32,1408]{1,0:T(8,128)(2,1)S(1)} %get-tuple-element.43), channel_id=1, source_target_pairs={{0,256},{32,288},{64,320},{96,352},{128,384},{160,416},{192,448},{... | collective-permute-start | bytes 270344 | tf_op jit(solution)/shard_map/ppermute | solution.py:366
  108.9 6.5 %collective-permute-start.9 = (bf16[32,1408]{1,0:T(8,128)(2,1)S(1)}, bf16[32,1408]{1,0:T(8,128)(2,1)S(1)}, u32[]{:S(2)}, u32[]{:S(2)}) collective-permute-start(bf16[32,1408]{1,0:T(8,128)(2,1)S(1)} %get-tuple-element.44), channel_id=1, source_target_pairs={{0,384},{32,416},{64,448},{96,480},{128,256},{160,288},{192,320},{... | collective-permute-start | bytes 270344 | tf_op jit(solution)/shard_map/ppermute | solution.py:366

commit v6 on v5

v6 whole, which is shorter than its diff:
```python
import functools

import jax
import jax.numpy as jnp
from jax import lax
from jax.experimental import pallas as pl
from jax.experimental.pallas import tpu as pltpu
from jax.sharding import PartitionSpec as P

QH = 40
KVH = 8
HD = 128
PAGE = 16
MAXP = 4
CAP = 2
GROUP = QH // KVH
QCOLS = QH * HD
SIDE = 128
ROW = QCOLS + SIDE
SHARE = 4
HEADS = QH // SHARE
BLOCK = HEADS * HD
KV = KVH // SHARE * HD
CHUNKS = 4
CHUNK = QCOLS // CHUNKS
TOKENS_AT = 64
SCALE = HD ** (-0.5)
VERY_LOW = -1e30
F32 = jnp.float32
BF16 = jnp.bfloat16


def iota(shape, axis):
    return lax.broadcasted_iota(jnp.int32, shape, axis)


def dot(a, b):
    return lax.dot_general(a, b, (((1,), (0,)), ((), ())), preferred_element_type=F32)


def dot_t(a, b):
    return lax.dot_general(a, b, (((1,), (1,)), ((), ())), preferred_element_type=F32)


def three_parts(x):
    hi = x.astype(BF16).astype(F32)
    mid = (x - hi).astype(BF16).astype(F32)
    lo = (x - hi - mid).astype(BF16).astype(F32)
    return hi, mid, lo


def load(refs, scratch, sems):
    copies = [
        pltpu.make_async_copy(ref, buf, sems.at[i])
        for i, (ref, buf) in enumerate(zip(refs, scratch, strict=True))
    ]
    for copy in copies:
        copy.start()
    return copies


def my_turn():
    return lax.div(lax.axis_index("grp"), 4)


def route_kernel(
    pool, q_hbm, table_hbm, len_hbm, place_hbm, pk_hbm, pv_hbm, send_ref, where_ref,
    q_ref, table_ref, len_ref, place_ref, rows_ref, sems,
):
    requests = q_ref.shape[0]
    entries = requests * MAXP
    devices = send_ref.shape[0]
    cells = devices * CAP
    mine = lax.axis_index("blk")
    group = lax.axis_index("grp")
    turn = my_turn()
    kv_at = pl.ds(pl.multiple_of(turn * KV, KV), KV)

    def fetch_rows(source):
        return pltpu.make_async_copy(source.at[:, kv_at], rows_ref, sems.at[4])

    @pl.when(lax.rem(group, 2) == 0)
    def _():
        fetch_rows(pk_hbm).start()

    @pl.when(lax.rem(group, 2) == 1)
    def _():
        fetch_rows(pv_hbm).start()

    copies = load(
        (place_hbm, table_hbm, len_hbm, q_hbm), (place_ref, table_ref, len_ref, q_ref), sems
    )
    fetch_rows(pk_hbm).wait()
    depth = rows_ref.shape[0]
    shape = (cells, depth)
    cell = iota(shape, 0)
    each = depth // 4 // CAP
    first = depth // 2 * lax.rem(lax.div(group, 2), 2) + depth // 4 * lax.div(cell, cells // 2)
    for p in range(each):
        one = iota(shape, 1) == first + each * lax.rem(cell, CAP) + p
        rows = dot(jnp.where(one, 1.0, 0.0).astype(BF16), rows_ref[...]).astype(BF16)
        send_ref[:, :, ROW + KV * p : ROW + KV * (p + 1)] = rows.reshape(devices, CAP, KV)

    base = group * (devices * pool)
    square = iota((requests, requests), 0) == iota((requests, requests), 1)

    def column(row):
        row = jnp.broadcast_to(row, (requests, requests)).astype(F32)
        return jnp.sum(jnp.where(square, row, 0.0), axis=1, keepdims=True)

    for copy in copies[:3]:
        copy.wait()
    table = table_ref[...] - base
    page = jnp.concatenate([column(table[j : j + 1]) for j in range(MAXP)], axis=0)
    place = (place_ref[...] - base).astype(F32)
    lane = iota((entries, 128), 1).astype(F32)
    found = jnp.zeros((entries, 128), F32)
    for k in range(place.shape[0]):
        found = found + jnp.where(page == lane + 128.0 * k, place[k : k + 1, :], 0.0)
    physical = jnp.sum(found, axis=1, keepdims=True)
    holder = jnp.floor((physical + 0.5) * (1.0 / pool))
    slot = physical - holder * pool
    length = column(len_ref[...])
    tokens = jnp.concatenate(
        [jnp.clip(length - PAGE * j, 0.0, PAGE) for j in range(MAXP)], axis=0
    )
    used = tokens > 0.0
    at_home = holder == mine.astype(F32)
    remote = jnp.where(used & jnp.logical_not(at_home), 1.0, 0.0)
    member = jnp.where(holder == lane, remote, 0.0)
    below = jnp.where(iota((entries, entries), 1) < iota((entries, entries), 0), 1.0, 0.0)
    before = dot(below.astype(BF16), member.astype(BF16))
    rank = jnp.sum(before * member, axis=1, keepdims=True)
    where = jnp.where(remote > 0.0, holder * CAP + rank, cells + slot)
    where = jnp.where(used, where, -1.0)
    where_ref[...] = jnp.where(lane < TOKENS_AT, where, tokens)
    pick = jnp.where(where == lane, 1.0, 0.0).T[:cells]
    facts = jnp.where(lane == 0.0, slot, jnp.where(lane == 1.0, tokens, 0.0))
    side = dot(pick.astype(BF16), facts.astype(BF16)).astype(BF16)
    send_ref[:, :, QCOLS:ROW] = side.reshape(devices, CAP, SIDE)
    picked = over_entries(pick, requests)
    copies[3].wait()
    for c in range(CHUNKS):
        begin = c * CHUNK
        rows = dot(picked, q_ref[:, begin : begin + CHUNK]).astype(BF16)
        send_ref[:, :, begin : begin + CHUNK] = rows.reshape(devices, CAP, CHUNK)


def over_entries(pick, requests):
    parts = [pick[:, requests * j : requests * (j + 1)] for j in range(MAXP)]
    return functools.reduce(jnp.add, parts).astype(BF16)


def home_kernel(q_hbm, where_hbm, local_ref, s0, s1, s2, s3, q_ref, where_ref, sems):
    copies = load((where_hbm, q_hbm), (where_ref, q_ref), sems)
    requests = q_ref.shape[0]
    entries = requests * MAXP
    pool = local_ref.shape[0]
    cells = CAP * lax.axis_size("blk")
    copies[0].wait()
    where, tokens = where_ref[:, 0:1], where_ref[:, TOKENS_AT : TOKENS_AT + 1]
    lane = iota((entries, 128), 1).astype(F32)
    pick = jnp.where(where == lane, 1.0, 0.0).T[cells : cells + pool]
    facts = jnp.where(lane == 0.0, where - cells, jnp.where(lane == 1.0, tokens, 0.0))
    local_ref[:, QCOLS:ROW] = dot(pick.astype(BF16), facts.astype(BF16)).astype(BF16)
    picked = over_entries(pick, requests)
    copies[1].wait()
    for c in range(CHUNKS):
        cols = slice(c * CHUNK, (c + 1) * CHUNK)
        local_ref[:, cols] = dot(picked, q_ref[:, cols]).astype(BF16)
    turn = my_turn()
    for o, ref in enumerate((s0, s1, s2, s3)):
        at = pl.multiple_of((turn ^ o) * BLOCK, BLOCK)
        ref[...] = q_ref[:, pl.ds(at, BLOCK)]


def pages_kernel(
    got_hbm, local_hbm, k_hbm, v_hbm, answer_ref, own_ref,
    got_ref, local_ref, k_ref, v_ref, sems, chunk_sems,
):
    devices = got_ref.shape[0]
    cells = devices * CAP
    pool = k_ref.shape[0]
    step = 16
    pair = 2 * HD
    every = slice(None)
    here = got_hbm.at[:, :, pl.ds(0, ROW)]
    first = load((here, local_hbm), (got_ref, local_ref), sems)
    chunks = []
    for c in range(CHUNKS):
        kv_at = (every, every, pl.ds(c * pair, pair))
        chunks.append(
            load(
                (k_hbm.at[kv_at], v_hbm.at[kv_at]),
                (k_ref.at[kv_at], v_ref.at[kv_at]),
                chunk_sems.at[c],
            )
        )
    wide = (step, step * PAGE)
    column = iota(wide, 1)
    same = lax.div(column, PAGE) == iota(wide, 0)
    token = lax.rem(column, PAGE).astype(F32)
    side_lane = iota((step, SIDE), 1)
    lane = iota((cells, 128), 1).astype(F32)
    for copy in first:
        copy.wait()
    plain = got_ref[:, :, QCOLS:ROW].reshape(cells, SIDE)
    facts = plain.astype(F32)
    pick = jnp.where((facts[:, 0:1] == lane) & (facts[:, 1:2] > 0.0), 1.0, 0.0)
    fetch = pick.T[:pool].astype(BF16)
    pick = pick[:, :pool].astype(BF16)
    tokens = (dot(fetch, plain) + local_ref[:, QCOLS:ROW].astype(F32))[:, 1:2]
    sums = [jnp.zeros((step, SIDE), F32) for _ in range(pool // step)]
    masks = []
    for g in range(pool // step):
        bias = jnp.where(same & (token < tokens[step * g : step * (g + 1)]), 0.0, VERY_LOW)
        masks.append(jnp.concatenate([bias] * (2 * GROUP), axis=0))
    nothing = jnp.zeros((step * GROUP, HD), BF16)
    spans = [slice(step * g, step * (g + 1)) for g in range(pool // step)]

    def score(c, g, rows):
        span = spans[g]
        one, two = (
            jnp.concatenate(
                [rows[span, (GROUP * k + i) * HD : (GROUP * k + i + 1) * HD] for i in range(GROUP)],
                axis=0,
            )
            for k in range(2)
        )
        heads = jnp.concatenate(
            [jnp.concatenate([one, nothing], axis=1), jnp.concatenate([nothing, two], axis=1)], axis=0
        )
        keys = k_ref[span, :, c * pair : (c + 1) * pair].reshape(step * PAGE, pair)
        return dot_t(heads, keys) * SCALE + masks[g]

    def weigh(scores):
        top = jnp.max(scores, axis=1, keepdims=True)
        weights = jnp.exp(scores - top)
        total = jnp.sum(weights, axis=1, keepdims=True)
        return weights.astype(BF16), total, top + jnp.log(total)

    def mix(c, g, weights, total, log_sum):
        span = spans[g]
        values = v_ref[span, :, c * pair : (c + 1) * pair].reshape(step * PAGE, pair)
        mixture = dot(weights, values) / total
        for i in range(2 * GROUP):
            here = slice(step * i, step * (i + 1))
            part = mixture[here, :HD] if i < GROUP else mixture[here, HD:]
            at = c * CHUNK + i * HD
            own_ref[span, at : at + HD] = part.astype(BF16)
            mine = lax.rem(side_lane, QH) == c * 2 * GROUP + i
            sums[g] = jnp.where(mine, log_sum[here], sums[g])

    def ask(c):
        cols = slice(c * CHUNK, (c + 1) * CHUNK)
        asked = got_ref[:, :, cols].reshape(cells, CHUNK)
        return (dot(fetch, asked) + local_ref[:, cols].astype(F32)).astype(BF16)

    for chunk in chunks:
        for copy in chunk:
            copy.wait()
    steps = [(c, g) for c in range(CHUNKS) for g in range(len(spans))]
    rows = {c: ask(c) for c in range(CHUNKS)}
    scores = {s: score(*s, rows[s[0]]) for s in steps[:2]}
    weighed = {}
    for n, s in enumerate(steps + [None]):
        if n + 2 < len(steps):
            t = steps[n + 2]
            scores[t] = score(*t, rows[t[0]])
        if s is not None:
            weighed[s] = weigh(scores.pop(s))
        if n >= 1:
            mix(*steps[n - 1], *weighed.pop(steps[n - 1]))
    for g in range(pool // step):
        hi, mid, lo = three_parts(sums[g])
        side = jnp.where(side_lane < QH, hi, jnp.where(side_lane < 2 * QH, mid, lo))
        own_ref[step * g : step * (g + 1), QCOLS:ROW] = side.astype(BF16)
    for c in range(0, QCOLS, 640):
        cols = slice(c, c + 640)
        rows = dot(pick, own_ref[:, cols]).astype(BF16)
        answer_ref[:, :, cols] = rows.reshape(devices, CAP, 640)
    rows = dot(pick, own_ref[:, QCOLS:ROW]).astype(BF16)
    answer_ref[:, :, QCOLS:ROW] = rows.reshape(devices, CAP, SIDE)


def prefix_kernel(q0, q1, q2, q3, kv_mine, kv_other, o0, o1, o2, o3):
    requests = q0.shape[0]
    rows = requests * SHARE
    step = 256
    chunks = [slice(c, c + step) for c in range(0, kv_mine.shape[0], step)]
    core = lax.rem(lax.axis_index("grp"), 2)
    lane = iota((rows, SIDE), 1)
    asked = (q0, q1, q2, q3)
    outs = (o0, o1, o2, o3)

    def attend(k_ref, v_ref):
        sums = jnp.zeros((rows, SIDE), F32)

        def score(h):
            heads = jnp.concatenate([q[:, h * HD : (h + 1) * HD] for q in asked], axis=0)
            kv = slice(h // GROUP * HD, (h // GROUP + 1) * HD)
            return [dot_t(heads, k_ref[c, kv]) * SCALE for c in chunks]

        def weigh(scores):
            top = jnp.max(functools.reduce(jnp.maximum, scores), axis=1, keepdims=True)
            weights = [jnp.exp(s - top) for s in scores]
            total = jnp.sum(functools.reduce(jnp.add, weights), axis=1, keepdims=True)
            return [w.astype(BF16) for w in weights], total, top + jnp.log(total)

        def mix(h, weights, total):
            kv = slice(h // GROUP * HD, (h // GROUP + 1) * HD)
            parts = [dot(w, v_ref[c, kv]) for c, w in zip(chunks, weights)]
            mixture = (functools.reduce(jnp.add, parts) / total).astype(BF16)
            for o, out in enumerate(outs):
                out[:, h * HD : (h + 1) * HD] = mixture[requests * o : requests * (o + 1)]

        scores, weighed = {0: score(0)}, {}
        for h in range(HEADS + 1):
            if h + 1 < HEADS:
                scores[h + 1] = score(h + 1)
            if h < HEADS:
                *weighed[h], log_sum = weigh(scores.pop(h))
                sums = jnp.where(lax.rem(lane, HEADS) == h, log_sum, sums)
            if h:
                mix(h - 1, *weighed.pop(h - 1))

        hi, mid, lo = three_parts(sums)
        side = jnp.where(lane < HEADS, hi, jnp.where(lane < 2 * HEADS, mid, lo)).astype(BF16)
        for o, out in enumerate(outs):
            out[:, BLOCK:] = side[requests * o : requests * (o + 1)]

    @pl.when(core == 0)
    def _():
        attend(kv_mine, kv_other)

    @pl.when(core == 1)
    def _():
        attend(kv_other, kv_mine)


def join_kernel(got_ref, own_ref, where_ref, *refs):
    *served, out_hbm, out_ref, sems = refs
    entries = where_ref.shape[0]
    requests = served[0].shape[0]
    cells = got_ref.shape[0] * CAP
    pool = own_ref.shape[0]
    lane = iota((entries, 128), 1)
    where = where_ref[:, 0:1]
    pick = jnp.where(where == lane.astype(F32), 1.0, 0.0).astype(BF16)
    far, near = pick[:, :cells], pick[:, cells : cells + pool]
    side = dot(far, got_ref[:, :, QCOLS:ROW].reshape(cells, SIDE)) + dot(near, own_ref[:, QCOLS:ROW])
    sums = side + pltpu.roll(side, SIDE - QH, 1) + pltpu.roll(side, SIDE - 2 * QH, 1)
    sums = jnp.where(where >= 0.0, sums, VERY_LOW)
    turn = my_turn()
    sent = []
    for o, p_ref in enumerate(served):
        turned = turn ^ o
        at = pl.multiple_of(turned * BLOCK, 128)
        cols = pl.ds(at, BLOCK)
        got = got_ref[:, :, cols].reshape(cells, BLOCK)
        rows = dot(far, got) + dot(near, own_ref[:, cols])
        moved = pltpu.roll(sums, lax.rem(SIDE - turned * HEADS, SIDE), 1)
        pre = p_ref[:, BLOCK:].astype(F32)
        pre = pre + pltpu.roll(pre, SIDE - HEADS, 1) + pltpu.roll(pre, SIDE - 2 * HEADS, 1)
        logs = [moved[requests * j : requests * (j + 1)] for j in range(MAXP)]
        top = functools.reduce(jnp.maximum, logs, pre)
        parts = [jnp.exp(x - top) for x in logs]
        part = jnp.exp(pre - top)
        total = functools.reduce(jnp.add, parts, part)
        parts = [x / total for x in parts]
        part = part / total
        for h in range(HEADS):
            here = slice(h * HD, (h + 1) * HD)
            mixture = part[:, h : h + 1] * p_ref[:, here].astype(F32)
            for j in range(MAXP):
                mixture = mixture + parts[j][:, h : h + 1] * rows[requests * j : requests * (j + 1), here]
            out_ref[:, pl.ds(pl.multiple_of(at + h * HD, 128), HD)] = mixture.astype(BF16)
        sent += load((out_ref.at[:, cols],), (out_hbm.at[:, cols],), sems.at[pl.ds(o, 1)])
    for copy in sent:
        copy.wait()


def call(kernel, out_shape, flops, *args, in_hbm=(), out_hbm=(), scratch=(), room=62_150_000):
    specs = [
        [pl.BlockSpec(memory_space=pl.ANY if i in hbm else pltpu.VMEM) for i in range(n)]
        for n, hbm in ((len(args), in_hbm), (len(out_shape), out_hbm))
    ]
    return pl.pallas_call(
        kernel,
        out_shape=[jax.ShapeDtypeStruct(s, d) for s, d in out_shape],
        in_specs=specs[0],
        out_specs=specs[1],
        scratch_shapes=list(scratch),
        compiler_params=pltpu.CompilerParams(vmem_limit_bytes=room),
        cost_estimate=pl.CostEstimate(flops=flops, bytes_accessed=1 << 22, transcendentals=0),
    )(*args)


def like(x):
    return pltpu.VMEM(x.shape, x.dtype)


def semaphores(*shape):
    return pltpu.SemaphoreType.DMA(shape)


def route(queries, tables, lengths, places, prefix_keys, prefix_values, devices, pool):
    requests, depth = queries.shape[0], prefix_keys.shape[0]
    shape = (devices, CAP, ROW + depth // 4 // CAP * KV)
    args = (queries, tables, lengths, places)
    return call(
        functools.partial(route_kernel, pool),
        [(shape, BF16), ((requests * MAXP, 128), F32)],
        10**8,
        *args,
        prefix_keys,
        prefix_values,
        in_hbm=range(6),
        scratch=(
            *map(like, args),
            pltpu.VMEM((depth, KV), BF16),
            semaphores(5),
        ),
    )


def home(queries, where, pool):
    return call(
        home_kernel,
        [((pool, ROW), BF16)] + [((queries.shape[0], BLOCK), BF16)] * SHARE,
        10**8,
        queries,
        where,
        in_hbm=range(2),
        scratch=(like(queries), like(where), semaphores(2)),
    )


def pages(got, local, suffix_keys, suffix_values):
    shape = (got.shape[0], CAP, ROW)
    return call(
        pages_kernel,
        [(shape, BF16), (local.shape, BF16)],
        10**9,
        got,
        local,
        suffix_keys,
        suffix_values,
        in_hbm=range(4),
        scratch=(
            pltpu.VMEM(shape, BF16),
            *map(like, (local, suffix_keys, suffix_values)),
            semaphores(2),
            semaphores(CHUNKS, 2),
        ),
    )


def prefix(asked, kv_mine, kv_other):
    shape = (asked[0].shape[0], BLOCK + SIDE)
    return call(
        prefix_kernel, [(shape, BF16)] * SHARE, 10**9, *asked, kv_mine, kv_other, room=40 << 20
    )


def join(back, own, where, served):
    shape = (served[0].shape[0], QCOLS)
    (out,) = call(
        join_kernel,
        [(shape, BF16)],
        10**8,
        back,
        own,
        where,
        *served,
        out_hbm=(0,),
        scratch=(pltpu.VMEM(shape, BF16), semaphores(SHARE)),
        room=32 << 20,
    )
    return out


def body(
    queries, page_table, suffix_len, place, suffix_keys, suffix_values, prefix_keys, prefix_values
):
    pool = suffix_keys.shape[0]
    devices = lax.axis_size("blk")
    group = lax.axis_size("grp")
    lengths, places = suffix_len.reshape(1, -1), place.reshape(-1, 128)
    send, where = route(
        queries, page_table.T, lengths, places, prefix_keys, prefix_values, devices, pool
    )
    flip = lambda x, bits: lax.ppermute(x, "grp", [(i, i ^ bits) for i in range(group)])
    turned = lambda xs: [flip(x, 4 * o) if o else x for o, x in enumerate(xs)]
    exchange = lambda x: lax.all_to_all(x, "blk", split_axis=0, concat_axis=0, tiled=True)
    got = exchange(send)
    local, *asked = home(queries, where, pool)
    asked = turned(asked)
    local, *asked = lax.optimization_barrier((local, *asked))
    answer, own = pages(got, local, suffix_keys, suffix_values)
    back = exchange(answer)
    part, own = lax.optimization_barrier((got[:, :, ROW:], own))
    part = part.reshape(-1, KV)
    pairs = [(i, i ^ (devices // 2)) for i in range(devices)]
    both = [
        (g * devices + i, (g ^ 2) * devices + j) for g in range(group) for i, j in pairs
    ]
    around = [
        flip(part, 2), lax.ppermute(part, "blk", pairs), lax.ppermute(part, ("grp", "blk"), both)
    ]
    kv_mine = jnp.concatenate([part, *around], axis=0)
    served = prefix(asked, kv_mine, flip(kv_mine, 1))
    return join(back, own, where, turned(served))


def solution(mesh):
    return jax.shard_map(
        body,
        mesh=mesh,
        in_specs=(
            P(("grp", "blk"), None),
            P(("grp", "blk"), None),
            P(("grp", "blk")),
            P("grp"),
            P(("grp", "blk"), None, None),
            P(("grp", "blk"), None, None),
            P("blk", None),
            P("blk", None),
        ),
        out_specs=P(("grp", "blk"), None),
        check_vma=False,
    )
```

time: 119 us -> 115 us (0.966)
  waiting for transfers between devices: 41.8 us -> 39.7 us
  Pallas kernels: 17 us -> 15.7 us
    all_to_all x2, waiting for transfers between devices: 26.3 us -> 23.9 us  [body(): lax.all_to_all(x, 'blk', split_axis=0, concat_axis=0, tiled=True)]
    pallas_call x4 -> x5, Pallas kernels: 17 us -> 15.7 us  [call(): pl.pallas_call(kernel, out_shape=[jax.ShapeDtypeStruct(s, d) for s, d in...]
  transfers between devices with their start and end apart: 12 -> 12, of which waited for: 8 -> 8; matrix products, arithmetic and copies ran while one was open for 0% -> 0% of each run, Pallas kernels for 2% -> 4%
where the time goes in v6:
time: 115 us
  starting transfers between devices  58 us (50%)
  waiting for transfers between devices  39.7 us (35%)
  Pallas kernels  15.7 us (14%)
    ppermute x8, starting transfers between devices, body(): lax.ppermute(x, 'grp', [(i, i ^ bits) for i in range(group)])  28.3 us
    all_to_all x2, starting transfers between devices, body(): lax.all_to_all(x, 'blk', split_axis=0, concat_axis=0, tiled=True)  24.7 us
    all_to_all x2, waiting for transfers between devices, body(): lax.all_to_all(x, 'blk', split_axis=0, concat_axis=0, tiled=True)  23.9 us
    pallas_call x5, Pallas kernels, call(): pl.pallas_call(kernel, out_shape=[jax.ShapeDtypeStruct(s, d) for s, d in...  15.7 us
    ppermute x8, waiting for transfers between devices, body(): lax.ppermute(x, 'grp', [(i, i ^ bits) for i in range(group)])  11.1 us
    ppermute x1, waiting for transfers between devices, body(): lax.ppermute(part, 'blk', pairs)  2.88 us
    ppermute x1, starting transfers between devices, body(): lax.ppermute(part, 'blk', pairs)  2.54 us
    ppermute x1, starting transfers between devices, body(): lax.ppermute(part, ('grp', 'blk'), both)  2.46 us
  transfers between devices with their start and end apart: 12, of which 8 were waited for; matrix products, arithmetic and copies ran while one was open for 0% of the time, Pallas kernels for 4%

profile of v6, /device:TPU:1, one launch (start us, length us, event | category | flops | bytes accessed | tf_op | source)
XLA Modules:
  0.0 114.6 jit_solution(2347817113508555640)
XLA Ops:
  0.0 3.0 %shard_map.82 = (bf16[32,2,6272]{2,1,0:T(2,128)(2,1)}, f32[128,128]{1,0:T(8,128)}) custom-call(bf16[32,5120]{1,0:T(8,128)(2,1)} %q_hbm.3, s32[4,32]{1,0:T(4,128)} %bitcast.4, s32[1,32]{1,0:T(1,128)} %bitcast.5, s32[12,128]{1,0:T(8,128)} %bitcast.3, bf16[32,1024]{1,0:T(8,128)(2,1)} %pk_hbm.1, bf16[32,1024]{1,0:T(8,128)(2,1)} %pv_hbm.1), custom_call_target="tpu_custom_call" | custom-call | flops 100000000 | bytes 4194304 | tf_op jit(solution)/shard_map/pallas_call | solution.py:388
  3.0 17.0 %all-to-all-start = ((bf16[32,2,6272]{2,1,0:T(2,128)(2,1)}), bf16[32,2,6272]{2,1,0:T(2,128)(2,1)S(1)}, u32[]{:S(2)}, u32[]{:S(2)}) async-start(bf16[32,2,6272]{2,1,0:T(2,128)(2,1)} %get-tuple-element.25), calls=%async_computation | async-start | bytes 1605632 | tf_op jit(solution)/shard_map/all_to_all | solution.py:495
  20.0 2.3 %shard_map.83 = (bf16[48,5248]{1,0:T(8,128)(2,1)}, bf16[32,1280]{1,0:T(8,128)(2,1)}, bf16[32,1280]{1,0:T(8,128)(2,1)}, bf16[32,1280]{1,0:T(8,128)(2,1)}, bf16[32,1280]{1,0:T(8,128)(2,1)}) custom-call(bf16[32,5120]{1,0:T(8,128)(2,1)} %q_hbm.3, f32[128,128]{1,0:T(8,128)} %get-tuple-element.26.where_hbm.where_ref), custom_call_target="tpu_custom_call" | custom-call | flops 100000000 | bytes 4194304 | tf_op jit(solution)/shard_map/pallas_call | solution.py:388
  22.3 3.2 %collective-permute-start = (bf16[32,1280]{1,0:T(8,128)(2,1)}, bf16[32,1280]{1,0:T(8,128)(2,1)S(1)}, u32[]{:S(2)}, u32[]{:S(2)}) collective-permute-start(bf16[32,1280]{1,0:T(8,128)(2,1)} %get-tuple-element.29), channel_id=1, source_target_pairs={{0,128},{32,160},{64,192},{96,224},{128,0},{160,32},{192,64},{224,... | collective-permute-start | bytes 245768 | tf_op jit(solution)/shard_map/ppermute | solution.py:493
  25.5 4.5 %collective-permute-start.1 = (bf16[32,1280]{1,0:T(8,128)(2,1)}, bf16[32,1280]{1,0:T(8,128)(2,1)S(1)}, u32[]{:S(2)}, u32[]{:S(2)}) collective-permute-start(bf16[32,1280]{1,0:T(8,128)(2,1)} %get-tuple-element.30), channel_id=1, source_target_pairs={{0,256},{32,288},{64,320},{96,352},{128,384},{160,416},{192,448},{... | collective-permute-start | bytes 245768 | tf_op jit(solution)/shard_map/ppermute | solution.py:493
  30.0 1.9 %collective-permute-start.2 = (bf16[32,1280]{1,0:T(8,128)(2,1)}, bf16[32,1280]{1,0:T(8,128)(2,1)S(1)}, u32[]{:S(2)}, u32[]{:S(2)}) collective-permute-start(bf16[32,1280]{1,0:T(8,128)(2,1)} %get-tuple-element.31), channel_id=1, source_target_pairs={{0,384},{32,416},{64,448},{96,480},{128,256},{160,288},{192,320},{... | collective-permute-start | bytes 245768 | tf_op jit(solution)/shard_map/ppermute | solution.py:493
  32.0 0.0 collective-permute-done.q1
  32.0 0.7 collective-permute-done.1.q2
  32.7 4.2 %collective-permute-done.2.q3 = bf16[32,1280]{1,0:T(8,128)(2,1)S(1)} collective-permute-done((bf16[32,1280]{1,0:T(8,128)(2,1)}, bf16[32,1280]{1,0:T(8,128)(2,1)S(1)}, u32[]{:S(2)}, u32[]{:S(2)}) %collective-permute-start.2) | collective-permute-done | bytes 81952 | tf_op jit(solution)/shard_map/ppermute | solution.py:493
  36.9 23.9 %all-to-all-done.got_hbm = bf16[32,2,6272]{2,1,0:T(2,128)(2,1)S(1)} async-done(((bf16[32,2,6272]{2,1,0:T(2,128)(2,1)}), bf16[32,2,6272]{2,1,0:T(2,128)(2,1)S(1)}, u32[]{:S(2)}, u32[]{:S(2)}) %all-to-all-start) | async-done | bytes 802848 | tf_op jit(solution)/shard_map/all_to_all | solution.py:495
  60.8 0.9 copy-done.3
  61.7 5.1 %shard_map.84 = (bf16[32,2,5248]{2,1,0:T(2,128)(2,1)}, bf16[48,5248]{1,0:T(8,128)(2,1)}) custom-call(bf16[32,2,6272]{2,1,0:T(2,128)(2,1)} %copy-done.3, bf16[48,5248]{1,0:T(8,128)(2,1)} %get-tuple-element.32.local_hbm, bf16[48,16,1024]{2,1,0:T(8,128)(2,1)} %k_hbm.1, bf16[48,16,1024]{2,1,0:T(8,128)(2,1)} %v_hbm.1), custom_call_target="tpu_custom_call" | custom-call | flops 1000000000 | bytes 4194304 | tf_op jit(solution)/shard_map/pallas_call | solution.py:388
  66.8 0.0 slice-start
  66.8 0.0 copy-start.2
  66.9 7.8 %all-to-all-start.1 = ((bf16[32,2,5248]{2,1,0:T(2,128)(2,1)}), bf16[32,2,5248]{2,1,0:T(2,128)(2,1)S(1)}, u32[]{:S(2)}, u32[]{:S(2)}) async-start(bf16[32,2,5248]{2,1,0:T(2,128)(2,1)} %get-tuple-element.33), calls=%async_computation.1 | async-start | bytes 1343488 | tf_op jit(solution)/shard_map/all_to_all | solution.py:495
  74.6 0.1 reshape.11
  74.7 4.4 %collective-permute-start.3 = (bf16[256,256]{1,0:T(8,128)(2,1)S(1)}, bf16[256,256]{1,0:T(8,128)(2,1)S(1)}, u32[]{:S(2)}, u32[]{:S(2)}) collective-permute-start(bf16[256,256]{1,0:T(8,128)(2,1)S(1)} %reshape.11), channel_id=1, source_target_pairs={{0,64},{32,96},{64,0},{96,32},{128,192},{160,224},{192,128},{224,1... | collective-permute-start | bytes 393224 | tf_op jit(solution)/shard_map/ppermute | solution.py:493
  79.1 2.5 %collective-permute-start.4 = (bf16[256,256]{1,0:T(8,128)(2,1)S(1)}, bf16[256,256]{1,0:T(8,128)(2,1)S(1)}, u32[]{:S(2)}, u32[]{:S(2)}) collective-permute-start(bf16[256,256]{1,0:T(8,128)(2,1)S(1)} %reshape.11), channel_id=1, source_target_pairs={{0,16},{1,17},{2,18},{3,19},{4,20},{5,21},{6,22},{7,23},{8,24},{9,... | collective-permute-start | bytes 393224 | tf_op jit(solution)/shard_map/ppermute | solution.py:509
  81.6 2.5 %collective-permute-start.5 = (bf16[256,256]{1,0:T(8,128)(2,1)S(1)}, bf16[256,256]{1,0:T(8,128)(2,1)S(1)}, u32[]{:S(2)}, u32[]{:S(2)}) collective-permute-start(bf16[256,256]{1,0:T(8,128)(2,1)S(1)} %reshape.11), channel_id=1, source_target_pairs={{0,80},{1,81},{2,82},{3,83},{4,84},{5,85},{6,86},{7,87},{8,88},{9,... | collective-permute-start | bytes 393224 | tf_op jit(solution)/shard_map/ppermute | solution.py:509
  84.1 2.9 %collective-permute-done.4 = bf16[256,256]{1,0:T(8,128)(2,1)S(1)} collective-permute-done((bf16[256,256]{1,0:T(8,128)(2,1)S(1)}, bf16[256,256]{1,0:T(8,128)(2,1)S(1)}, u32[]{:S(2)}, u32[]{:S(2)}) %collective-permute-start.4) | collective-permute-done | bytes 131104 | tf_op jit(solution)/shard_map/ppermute | solution.py:509
  87.0 1.8 %collective-permute-done.5 = bf16[256,256]{1,0:T(8,128)(2,1)S(1)} collective-permute-done((bf16[256,256]{1,0:T(8,128)(2,1)S(1)}, bf16[256,256]{1,0:T(8,128)(2,1)S(1)}, u32[]{:S(2)}, u32[]{:S(2)}) %collective-permute-start.5) | collective-permute-done | bytes 131104 | tf_op jit(solution)/shard_map/ppermute | solution.py:509
  88.9 4.6 %collective-permute-start.6 = (bf16[1024,256]{1,0:T(8,128)(2,1)S(1)}, bf16[1024,256]{1,0:T(8,128)(2,1)S(1)}, u32[]{:S(2)}, u32[]{:S(2)}) collective-permute-start(bf16[1024,256]{1,0:T(8,128)(2,1)S(1)} %constant_dynamic-update-slice_fusion.kv_mine), channel_id=1, source_target_pairs={{0,32},{32,0},{64,96},{96,64},{128,160},{160,128},{192,224},{224,1... | collective-permute-start | bytes 1572872 | tf_op jit(solution)/shard_map/ppermute | solution.py:493
  93.5 1.5 %collective-permute-done.6.kv_other = bf16[1024,256]{1,0:T(8,128)(2,1)S(1)} collective-permute-done((bf16[1024,256]{1,0:T(8,128)(2,1)S(1)}, bf16[1024,256]{1,0:T(8,128)(2,1)S(1)}, u32[]{:S(2)}, u32[]{:S(2)}) %collective-permute-start.6) | collective-permute-done | bytes 524320 | tf_op jit(solution)/shard_map/ppermute | solution.py:493
  95.1 2.3 %shard_map.85 = (bf16[32,1408]{1,0:T(8,128)(2,1)S(1)}, bf16[32,1408]{1,0:T(8,128)(2,1)S(1)}, bf16[32,1408]{1,0:T(8,128)(2,1)S(1)}, bf16[32,1408]{1,0:T(8,128)(2,1)S(1)}) custom-call(bf16[32,1280]{1,0:T(8,128)(2,1)S(1)} %copy-done.2, bf16[32,1280]{1,0:T(8,128)(2,1)S(1)} %collective-permute-done.q1, bf16[32,1280]{1,0:T(8,128)(2,1)S(1)} %collective-permute-done.1.q2, ...), custom_call_target="tpu_custom_call" | custom-call | flops 1000000000 | bytes 4194304 | tf_op jit(solution)/shard_map/pallas_call | solution.py:388
  97.4 3.2 %collective-permute-start.7 = (bf16[32,1408]{1,0:T(8,128)(2,1)S(1)}, bf16[32,1408]{1,0:T(8,128)(2,1)S(1)}, u32[]{:S(2)}, u32[]{:S(2)}) collective-permute-start(bf16[32,1408]{1,0:T(8,128)(2,1)S(1)} %get-tuple-element.42), channel_id=1, source_target_pairs={{0,128},{32,160},{64,192},{96,224},{128,0},{160,32},{192,64},{224,... | collective-permute-start | bytes 270344 | tf_op jit(solution)/shard_map/ppermute | solution.py:493
  100.6 4.5 %collective-permute-start.8 = (bf16[32,1408]{1,0:T(8,128)(2,1)S(1)}, bf16[32,1408]{1,0:T(8,128)(2,1)S(1)}, u32[]{:S(2)}, u32[]{:S(2)}) collective-permute-start(bf16[32,1408]{1,0:T(8,128)(2,1)S(1)} %get-tuple-element.43), channel_id=1, source_target_pairs={{0,256},{32,288},{64,320},{96,352},{128,384},{160,416},{192,448},{... | collective-permute-start | bytes 270344 | tf_op jit(solution)/shard_map/ppermute | solution.py:493
  105.1 1.9 %collective-permute-start.9 = (bf16[32,1408]{1,0:T(8,128)(2,1)S(1)}, bf16[32,1408]{1,0:T(8,128)(2,1)S(1)}, u32[]{:S(2)}, u32[]{:S(2)}) collective-permute-start(bf16[32,1408]{1,0:T(8,128)(2,1)S(1)} %get-tuple-element.44), channel_id=1, source_target_pairs={{0,384},{32,416},{64,448},{96,480},{128,256},{160,288},{192,320},{... | collective-permute-start | bytes 270344 | tf_op jit(solution)/shard_map/ppermute | solution.py:493
  107.1 0.0 collective-permute-done.7.refs_1_
  107.1 0.6 collective-permute-done.8.refs_2_
  107.7 4.0 %collective-permute-done.9.refs_3_ = bf16[32,1408]{1,0:T(8,128)(2,1)S(1)} collective-permute-done((bf16[32,1408]{1,0:T(8,128)(2,1)S(1)}, bf16[32,1408]{1,0:T(8,128)(2,1)S(1)}, u32[]{:S(2)}, u32[]{:S(2)}) %collective-permute-start.9) | collective-permute-done | bytes 90144 | tf_op jit(solution)/shard_map/ppermute | solution.py:493
  111.7 0.0 all-to-all-done.1.got_ref
  111.7 2.9 %shard_map.86 = bf16[32,5120]{1,0:T(8,128)(2,1)} custom-call(bf16[32,2,5248]{2,1,0:T(2,128)(2,1)S(1)} %all-to-all-done.1.got_ref, bf16[48,5248]{1,0:T(8,128)(2,1)S(1)} %copy-done, f32[128,128]{1,0:T(8,128)S(1)} %copy-done.1, bf16[32,1408]{1,0:T(8,128)(2,1)S(1)} %get-tuple-element.41.refs_0_, bf16[32,1408]{1,0:T(8,128)(2,1)S(1)} %collective-permute-done.7.refs_1_, ...), custom_call_target="tpu_custom_call" | custom-call | flops 100000000 | bytes 4194304 | tf_op jit(solution)/shard_map/pallas_call | solution.py:388
  (12 shorter events, 0.1 us)
Async XLA Ops:
  3.0 57.7 %all-to-all-start = ((bf16[32,2,6272]{2,1,0:T(2,128)(2,1)}), bf16[32,2,6272]{2,1,0:T(2,128)(2,1)S(1)}, u32[]{:S(2)}, u32[]{:S(2)}) async-start(bf16[32,2,6272]{2,1,0:T(2,128)(2,1)} %get-tuple-element.25), calls=%async_computation | async-start | bytes 1605632 | tf_op jit(solution)/shard_map/all_to_all | solution.py:495
  22.3 9.7 %collective-permute-start = (bf16[32,1280]{1,0:T(8,128)(2,1)}, bf16[32,1280]{1,0:T(8,128)(2,1)S(1)}, u32[]{:S(2)}, u32[]{:S(2)}) collective-permute-start(bf16[32,1280]{1,0:T(8,128)(2,1)} %get-tuple-element.29), channel_id=1, source_target_pairs={{0,128},{32,160},{64,192},{96,224},{128,0},{160,32},{192,64},{224,... | collective-permute-start | bytes 245768 | tf_op jit(solution)/shard_map/ppermute | solution.py:493
  25.5 7.2 %collective-permute-start.1 = (bf16[32,1280]{1,0:T(8,128)(2,1)}, bf16[32,1280]{1,0:T(8,128)(2,1)S(1)}, u32[]{:S(2)}, u32[]{:S(2)}) collective-permute-start(bf16[32,1280]{1,0:T(8,128)(2,1)} %get-tuple-element.30), channel_id=1, source_target_pairs={{0,256},{32,288},{64,320},{96,352},{128,384},{160,416},{192,448},{... | collective-permute-start | bytes 245768 | tf_op jit(solution)/shard_map/ppermute | solution.py:493
  30.0 6.9 %collective-permute-start.2 = (bf16[32,1280]{1,0:T(8,128)(2,1)}, bf16[32,1280]{1,0:T(8,128)(2,1)S(1)}, u32[]{:S(2)}, u32[]{:S(2)}) collective-permute-start(bf16[32,1280]{1,0:T(8,128)(2,1)} %get-tuple-element.31), channel_id=1, source_target_pairs={{0,384},{32,416},{64,448},{96,480},{128,256},{160,288},{192,320},{... | collective-permute-start | bytes 245768 | tf_op jit(solution)/shard_map/ppermute | solution.py:493
  60.8 0.9 copy-start.3
  66.8 7.8 %slice-start = ((bf16[32,2,6272]{2,1,0:T(2,128)(2,1)}), bf16[32,2,1024]{2,1,0:T(2,128)(2,1)S(1)}, s32[]{:S(2)}) async-start(bf16[32,2,6272]{2,1,0:T(2,128)(2,1)} %copy-done.3), calls=%async_computation.2 | async-start | bytes 262144 | tf_op jit(solution)/shard_map/slice | solution.py:502
  66.8 28.2 %copy-start.2 = (bf16[32,1280]{1,0:T(8,128)(2,1)S(1)}, bf16[32,1280]{1,0:T(8,128)(2,1)}, u32[]{:S(2)}) copy-start(bf16[32,1280]{1,0:T(8,128)(2,1)} %get-tuple-element.36.q0) | copy-start | bytes 245764
  66.9 44.8 %all-to-all-start.1 = ((bf16[32,2,5248]{2,1,0:T(2,128)(2,1)}), bf16[32,2,5248]{2,1,0:T(2,128)(2,1)S(1)}, u32[]{:S(2)}, u32[]{:S(2)}) async-start(bf16[32,2,5248]{2,1,0:T(2,128)(2,1)} %get-tuple-element.33), calls=%async_computation.1 | async-start | bytes 1343488 | tf_op jit(solution)/shard_map/all_to_all | solution.py:495
  74.7 9.4 %collective-permute-start.3 = (bf16[256,256]{1,0:T(8,128)(2,1)S(1)}, bf16[256,256]{1,0:T(8,128)(2,1)S(1)}, u32[]{:S(2)}, u32[]{:S(2)}) collective-permute-start(bf16[256,256]{1,0:T(8,128)(2,1)S(1)} %reshape.11), channel_id=1, source_target_pairs={{0,64},{32,96},{64,0},{96,32},{128,192},{160,224},{192,128},{224,1... | collective-permute-start | bytes 393224 | tf_op jit(solution)/shard_map/ppermute | solution.py:493
  79.1 7.9 %collective-permute-start.4 = (bf16[256,256]{1,0:T(8,128)(2,1)S(1)}, bf16[256,256]{1,0:T(8,128)(2,1)S(1)}, u32[]{:S(2)}, u32[]{:S(2)}) collective-permute-start(bf16[256,256]{1,0:T(8,128)(2,1)S(1)} %reshape.11), channel_id=1, source_target_pairs={{0,16},{1,17},{2,18},{3,19},{4,20},{5,21},{6,22},{7,23},{8,24},{9,... | collective-permute-start | bytes 393224 | tf_op jit(solution)/shard_map/ppermute | solution.py:509
  81.6 7.2 %collective-permute-start.5 = (bf16[256,256]{1,0:T(8,128)(2,1)S(1)}, bf16[256,256]{1,0:T(8,128)(2,1)S(1)}, u32[]{:S(2)}, u32[]{:S(2)}) collective-permute-start(bf16[256,256]{1,0:T(8,128)(2,1)S(1)} %reshape.11), channel_id=1, source_target_pairs={{0,80},{1,81},{2,82},{3,83},{4,84},{5,85},{6,86},{7,87},{8,88},{9,... | collective-permute-start | bytes 393224 | tf_op jit(solution)/shard_map/ppermute | solution.py:509
  88.9 22.8 %copy-start = (bf16[48,5248]{1,0:T(8,128)(2,1)S(1)}, bf16[48,5248]{1,0:T(8,128)(2,1)}, u32[]{:S(2)}) copy-start(bf16[48,5248]{1,0:T(8,128)(2,1)} %get-tuple-element.35.own_ref) | copy-start | bytes 1511428
  88.9 22.8 %copy-start.1 = (f32[128,128]{1,0:T(8,128)S(1)}, f32[128,128]{1,0:T(8,128)}, u32[]{:S(2)}) copy-start(f32[128,128]{1,0:T(8,128)} %get-tuple-element.26.where_hbm.where_ref) | copy-start | bytes 196612
  88.9 6.2 %collective-permute-start.6 = (bf16[1024,256]{1,0:T(8,128)(2,1)S(1)}, bf16[1024,256]{1,0:T(8,128)(2,1)S(1)}, u32[]{:S(2)}, u32[]{:S(2)}) collective-permute-start(bf16[1024,256]{1,0:T(8,128)(2,1)S(1)} %constant_dynamic-update-slice_fusion.kv_mine), channel_id=1, source_target_pairs={{0,32},{32,0},{64,96},{96,64},{128,160},{160,128},{192,224},{224,1... | collective-permute-start | bytes 1572872 | tf_op jit(solution)/shard_map/ppermute | solution.py:493
  97.4 9.7 %collective-permute-start.7 = (bf16[32,1408]{1,0:T(8,128)(2,1)S(1)}, bf16[32,1408]{1,0:T(8,128)(2,1)S(1)}, u32[]{:S(2)}, u32[]{:S(2)}) collective-permute-start(bf16[32,1408]{1,0:T(8,128)(2,1)S(1)} %get-tuple-element.42), channel_id=1, source_target_pairs={{0,128},{32,160},{64,192},{96,224},{128,0},{160,32},{192,64},{224,... | collective-permute-start | bytes 270344 | tf_op jit(solution)/shard_map/ppermute | solution.py:493
  100.6 7.1 %collective-permute-start.8 = (bf16[32,1408]{1,0:T(8,128)(2,1)S(1)}, bf16[32,1408]{1,0:T(8,128)(2,1)S(1)}, u32[]{:S(2)}, u32[]{:S(2)}) collective-permute-start(bf16[32,1408]{1,0:T(8,128)(2,1)S(1)} %get-tuple-element.43), channel_id=1, source_target_pairs={{0,256},{32,288},{64,320},{96,352},{128,384},{160,416},{192,448},{... | collective-permute-start | bytes 270344 | tf_op jit(solution)/shard_map/ppermute | solution.py:493
  105.1 6.6 %collective-permute-start.9 = (bf16[32,1408]{1,0:T(8,128)(2,1)S(1)}, bf16[32,1408]{1,0:T(8,128)(2,1)S(1)}, u32[]{:S(2)}, u32[]{:S(2)}) collective-permute-start(bf16[32,1408]{1,0:T(8,128)(2,1)S(1)} %get-tuple-element.44), channel_id=1, source_target_pairs={{0,384},{32,416},{64,448},{96,480},{128,256},{160,288},{192,320},{... | collective-permute-start | bytes 270344 | tf_op jit(solution)/shard_map/ppermute | solution.py:493

commit v7 on v6

--- a/solution.py
+++ b/solution.py
@@ -151,20 +151,19 @@
     return functools.reduce(jnp.add, parts).astype(BF16)
 
 
-def home_kernel(q_hbm, where_hbm, local_ref, s0, s1, s2, s3, q_ref, where_ref, sems):
-    copies = load((where_hbm, q_hbm), (where_ref, q_ref), sems)
+def home_kernel(q_hbm, where_ref, local_ref, s0, s1, s2, s3, q_ref, sems):
+    copies = load((q_hbm,), (q_ref,), sems)
     requests = q_ref.shape[0]
     entries = requests * MAXP
     pool = local_ref.shape[0]
     cells = CAP * lax.axis_size("blk")
-    copies[0].wait()
     where, tokens = where_ref[:, 0:1], where_ref[:, TOKENS_AT : TOKENS_AT + 1]
     lane = iota((entries, 128), 1).astype(F32)
     pick = jnp.where(where == lane, 1.0, 0.0).T[cells : cells + pool]
     facts = jnp.where(lane == 0.0, where - cells, jnp.where(lane == 1.0, tokens, 0.0))
     local_ref[:, QCOLS:ROW] = dot(pick.astype(BF16), facts.astype(BF16)).astype(BF16)
     picked = over_entries(pick, requests)
-    copies[1].wait()
+    copies[0].wait()
     for c in range(CHUNKS):
         cols = slice(c * CHUNK, (c + 1) * CHUNK)
         local_ref[:, cols] = dot(picked, q_ref[:, cols]).astype(BF16)
@@ -175,8 +174,7 @@
 
 
 def pages_kernel(
-    got_hbm, local_hbm, k_hbm, v_hbm, answer_ref, own_ref,
-    got_ref, local_ref, k_ref, v_ref, sems, chunk_sems,
+    got_ref, local_ref, k_hbm, v_hbm, answer_ref, own_ref, k_ref, v_ref, chunk_sems,
 ):
     devices = got_ref.shape[0]
     cells = devices * CAP
@@ -184,8 +182,6 @@
     step = 16
     pair = 2 * HD
     every = slice(None)
-    here = got_hbm.at[:, :, pl.ds(0, ROW)]
-    first = load((here, local_hbm), (got_ref, local_ref), sems)
     chunks = []
     for c in range(CHUNKS):
         kv_at = (every, every, pl.ds(c * pair, pair))
@@ -202,8 +198,6 @@
     token = lax.rem(column, PAGE).astype(F32)
     side_lane = iota((step, SIDE), 1)
     lane = iota((cells, 128), 1).astype(F32)
-    for copy in first:
-        copy.wait()
     plain = got_ref[:, :, QCOLS:ROW].reshape(cells, SIDE)
     facts = plain.astype(F32)
     pick = jnp.where((facts[:, 0:1] == lane) & (facts[:, 1:2] > 0.0), 1.0, 0.0)
@@ -353,34 +347,46 @@
     sums = jnp.where(where >= 0.0, sums, VERY_LOW)
     turn = my_turn()
     sent = []
-    for o, p_ref in enumerate(served):
-        turned = turn ^ o
-        at = pl.multiple_of(turned * BLOCK, 128)
-        cols = pl.ds(at, BLOCK)
+
+    def bring(o):
+        cols = pl.ds(pl.multiple_of((turn ^ o) * BLOCK, 128), BLOCK)
         got = got_ref[:, :, cols].reshape(cells, BLOCK)
-        rows = dot(far, got) + dot(near, own_ref[:, cols])
-        moved = pltpu.roll(sums, lax.rem(SIDE - turned * HEADS, SIDE), 1)
-        pre = p_ref[:, BLOCK:].astype(F32)
+        return dot(far, got) + dot(near, own_ref[:, cols])
+
+    def shares(o):
+        moved = pltpu.roll(sums, lax.rem(SIDE - (turn ^ o) * HEADS, SIDE), 1)
+        pre = served[o][:, BLOCK:].astype(F32)
         pre = pre + pltpu.roll(pre, SIDE - HEADS, 1) + pltpu.roll(pre, SIDE - 2 * HEADS, 1)
         logs = [moved[requests * j : requests * (j + 1)] for j in range(MAXP)]
         top = functools.reduce(jnp.maximum, logs, pre)
-        parts = [jnp.exp(x - top) for x in logs]
-        part = jnp.exp(pre - top)
-        total = functools.reduce(jnp.add, parts, part)
-        parts = [x / total for x in parts]
-        part = part / total
+        parts = [jnp.exp(x - top) for x in (*logs, pre)]
+        total = functools.reduce(jnp.add, parts)
+        return [x / total for x in parts]
+
+    weights = [shares(o) for o in range(SHARE)]
+    rows = bring(0)
+    for o in range(SHARE):
+        ahead = bring(o + 1) if o + 1 < SHARE else None
+        *parts, part = weights[o]
+        at = pl.multiple_of((turn ^ o) * BLOCK, 128)
         for h in range(HEADS):
             here = slice(h * HD, (h + 1) * HD)
-            mixture = part[:, h : h + 1] * p_ref[:, here].astype(F32)
+            mixture = part[:, h : h + 1] * served[o][:, here].astype(F32)
             for j in range(MAXP):
                 mixture = mixture + parts[j][:, h : h + 1] * rows[requests * j : requests * (j + 1), here]
             out_ref[:, pl.ds(pl.multiple_of(at + h * HD, 128), HD)] = mixture.astype(BF16)
+        rows = ahead
+        cols = pl.ds(at, BLOCK)
         sent += load((out_ref.at[:, cols],), (out_hbm.at[:, cols],), sems.at[pl.ds(o, 1)])
     for copy in sent:
         copy.wait()
 
 
-def call(kernel, out_shape, flops, *args, in_hbm=(), out_hbm=(), scratch=(), room=62_150_000):
+def call(kernel, out_shape, flops, *args, in_hbm=(), out_hbm=(), scratch=(), room=24 << 20):
+    args = [
+        pltpu.with_memory_space_constraint(x, pltpu.HBM) if i in in_hbm else x
+        for i, x in enumerate(args)
+    ]
     specs = [
         [pl.BlockSpec(memory_space=pl.ANY if i in hbm else pltpu.VMEM) for i in range(n)]
         for n, hbm in ((len(args), in_hbm), (len(out_shape), out_hbm))
@@ -431,8 +437,8 @@
         10**8,
         queries,
         where,
-        in_hbm=range(2),
-        scratch=(like(queries), like(where), semaphores(2)),
+        in_hbm=(0,),
+        scratch=(like(queries), semaphores(1)),
     )
 
 
@@ -446,20 +452,15 @@
         local,
         suffix_keys,
         suffix_values,
-        in_hbm=range(4),
-        scratch=(
-            pltpu.VMEM(shape, BF16),
-            *map(like, (local, suffix_keys, suffix_values)),
-            semaphores(2),
-            semaphores(CHUNKS, 2),
-        ),
+        in_hbm=(2, 3),
+        scratch=(*map(like, (suffix_keys, suffix_values)), semaphores(CHUNKS, 2)),
     )
 
 
 def prefix(asked, kv_mine, kv_other):
     shape = (asked[0].shape[0], BLOCK + SIDE)
     return call(
-        prefix_kernel, [(shape, BF16)] * SHARE, 10**9, *asked, kv_mine, kv_other, room=40 << 20
+        prefix_kernel, [(shape, BF16)] * SHARE, 10**9, *asked, kv_mine, kv_other
     )
 
 
@@ -475,7 +476,6 @@
         *served,
         out_hbm=(0,),
         scratch=(pltpu.VMEM(shape, BF16), semaphores(SHARE)),
-        room=32 << 20,
     )
     return out
 

time: 115 us -> 113 us (0.983)
  Pallas kernels: 15.7 us -> 13.4 us
    pallas_call x5, Pallas kernels: 15.7 us -> 13.4 us  [call(): pl.pallas_call(kernel, out_shape=[jax.ShapeDtypeStruct(s, d) for s, d in...]
    all_to_all x2, waiting for transfers between devices: 23.9 us -> 25 us  [body(): lax.all_to_all(x, 'blk', split_axis=0, concat_axis=0, tiled=True)]
  transfers between devices with their start and end apart: 12 -> 12, of which waited for: 8 -> 8; matrix products, arithmetic and copies ran while one was open for 0% -> 0% of each run, Pallas kernels for 4% -> 3%
where the time goes in v7:
time: 113 us; the launch traced here: 112 us
  starting transfers between devices  57.8 us (51%)
  waiting for transfers between devices  40.6 us (36%)
  Pallas kernels  13.4 us (12%)
    ppermute x8, starting transfers between devices, body(): lax.ppermute(x, 'grp', [(i, i ^ bits) for i in range(group)])  28.2 us
    all_to_all x2, waiting for transfers between devices, body(): lax.all_to_all(x, 'blk', split_axis=0, concat_axis=0, tiled=True)  25 us
    all_to_all x2, starting transfers between devices, body(): lax.all_to_all(x, 'blk', split_axis=0, concat_axis=0, tiled=True)  24.6 us
    pallas_call x5, Pallas kernels, call(): pl.pallas_call(kernel, out_shape=[jax.ShapeDtypeStruct(s, d) for s, d in...  13.4 us
    ppermute x8, waiting for transfers between devices, body(): lax.ppermute(x, 'grp', [(i, i ^ bits) for i in range(group)])  10.8 us
    ppermute x1, waiting for transfers between devices, body(): lax.ppermute(part, 'blk', pairs)  2.88 us
    ppermute x1, starting transfers between devices, body(): lax.ppermute(part, 'blk', pairs)  2.54 us
    ppermute x1, starting transfers between devices, body(): lax.ppermute(part, ('grp', 'blk'), both)  2.47 us
  transfers between devices with their start and end apart: 12, of which 8 were waited for; matrix products, arithmetic and copies ran while one was open for 0% of the time, Pallas kernels for 3%

profile of v7, /device:TPU:1, one launch (start us, length us, event | category | flops | bytes accessed | tf_op | source)
XLA Modules:
  0.0 112.1 jit_solution(13204599646337857998)
XLA Ops:
  0.0 3.0 %shard_map.82 = (bf16[32,2,6272]{2,1,0:T(2,128)(2,1)}, f32[128,128]{1,0:T(8,128)S(1)}) custom-call(bf16[32,5120]{1,0:T(8,128)(2,1)} %q_hbm.3, s32[4,32]{1,0:T(4,128)} %bitcast.4, s32[1,32]{1,0:T(1,128)} %bitcast.5, s32[12,128]{1,0:T(8,128)} %bitcast.3, bf16[32,1024]{1,0:T(8,128)(2,1)} %pk_hbm.1, bf16[32,1024]{1,0:T(8,128)(2,1)} %pv_hbm.1), custom_call_target="tpu_custom_call" | custom-call | flops 100000000 | bytes 4194304 | tf_op jit(solution)/shard_map/pallas_call | solution.py:394
  3.0 17.0 %all-to-all-start = ((bf16[32,2,6272]{2,1,0:T(2,128)(2,1)}), bf16[32,2,6272]{2,1,0:T(2,128)(2,1)S(1)}, u32[]{:S(2)}, u32[]{:S(2)}) async-start(bf16[32,2,6272]{2,1,0:T(2,128)(2,1)} %get-tuple-element.25), calls=%async_computation | async-start | bytes 1605632 | tf_op jit(solution)/shard_map/all_to_all | solution.py:495
  20.0 1.3 %shard_map.83 = (bf16[48,5248]{1,0:T(8,128)(2,1)S(1)}, bf16[32,1280]{1,0:T(8,128)(2,1)S(1)}, bf16[32,1280]{1,0:T(8,128)(2,1)S(1)}, bf16[32,1280]{1,0:T(8,128)(2,1)S(1)}, bf16[32,1280]{1,0:T(8,128)(2,1)S(1)}) custom-call(bf16[32,5120]{1,0:T(8,128)(2,1)} %q_hbm.3, f32[128,128]{1,0:T(8,128)S(1)} %get-tuple-element.26.where_ref), custom_call_target="tpu_custom_call" | custom-call | flops 100000000 | bytes 4194304 | tf_op jit(solution)/shard_map/pallas_call | solution.py:394
  21.3 3.2 %collective-permute-start = (bf16[32,1280]{1,0:T(8,128)(2,1)S(1)}, bf16[32,1280]{1,0:T(8,128)(2,1)S(1)}, u32[]{:S(2)}, u32[]{:S(2)}) collective-permute-start(bf16[32,1280]{1,0:T(8,128)(2,1)S(1)} %get-tuple-element.29), channel_id=1, source_target_pairs={{0,128},{32,160},{64,192},{96,224},{128,0},{160,32},{192,64},{224,... | collective-permute-start | bytes 245768 | tf_op jit(solution)/shard_map/ppermute | solution.py:493
  24.5 4.5 %collective-permute-start.1 = (bf16[32,1280]{1,0:T(8,128)(2,1)S(1)}, bf16[32,1280]{1,0:T(8,128)(2,1)S(1)}, u32[]{:S(2)}, u32[]{:S(2)}) collective-permute-start(bf16[32,1280]{1,0:T(8,128)(2,1)S(1)} %get-tuple-element.30), channel_id=1, source_target_pairs={{0,256},{32,288},{64,320},{96,352},{128,384},{160,416},{192,448},{... | collective-permute-start | bytes 245768 | tf_op jit(solution)/shard_map/ppermute | solution.py:493
  29.0 1.9 %collective-permute-start.2 = (bf16[32,1280]{1,0:T(8,128)(2,1)S(1)}, bf16[32,1280]{1,0:T(8,128)(2,1)S(1)}, u32[]{:S(2)}, u32[]{:S(2)}) collective-permute-start(bf16[32,1280]{1,0:T(8,128)(2,1)S(1)} %get-tuple-element.31), channel_id=1, source_target_pairs={{0,384},{32,416},{64,448},{96,480},{128,256},{160,288},{192,320},{... | collective-permute-start | bytes 245768 | tf_op jit(solution)/shard_map/ppermute | solution.py:493
  31.0 0.0 collective-permute-done.q1
  31.0 0.5 collective-permute-done.1.q2
  31.5 4.2 %collective-permute-done.2.q3 = bf16[32,1280]{1,0:T(8,128)(2,1)S(1)} collective-permute-done((bf16[32,1280]{1,0:T(8,128)(2,1)S(1)}, bf16[32,1280]{1,0:T(8,128)(2,1)S(1)}, u32[]{:S(2)}, u32[]{:S(2)}) %collective-permute-start.2) | collective-permute-done | bytes 81952 | tf_op jit(solution)/shard_map/ppermute | solution.py:493
  35.7 25.0 %all-to-all-done.got_ref = bf16[32,2,6272]{2,1,0:T(2,128)(2,1)S(1)} async-done(((bf16[32,2,6272]{2,1,0:T(2,128)(2,1)}), bf16[32,2,6272]{2,1,0:T(2,128)(2,1)S(1)}, u32[]{:S(2)}, u32[]{:S(2)}) %all-to-all-start) | async-done | bytes 802848 | tf_op jit(solution)/shard_map/all_to_all | solution.py:495
  60.8 4.5 %shard_map.84 = (bf16[32,2,5248]{2,1,0:T(2,128)(2,1)}, bf16[48,5248]{1,0:T(8,128)(2,1)S(1)}) custom-call(bf16[32,2,6272]{2,1,0:T(2,128)(2,1)S(1)} %all-to-all-done.got_ref, bf16[48,5248]{1,0:T(8,128)(2,1)S(1)} %get-tuple-element.32.local_ref, bf16[48,16,1024]{2,1,0:T(8,128)(2,1)} %k_hbm.1, bf16[48,16,1024]{2,1,0:T(8,128)(2,1)} %v_hbm.1), custom_call_target="tpu_custom_call" | custom-call | flops 1000000000 | bytes 4194304 | tf_op jit(solution)/shard_map/pallas_call | solution.py:394
  65.2 7.6 %all-to-all-start.1 = ((bf16[32,2,5248]{2,1,0:T(2,128)(2,1)}), bf16[32,2,5248]{2,1,0:T(2,128)(2,1)S(1)}, u32[]{:S(2)}, u32[]{:S(2)}) async-start(bf16[32,2,5248]{2,1,0:T(2,128)(2,1)} %get-tuple-element.33), calls=%async_computation.1 | async-start | bytes 1343488 | tf_op jit(solution)/shard_map/all_to_all | solution.py:495
  72.9 0.1 slice.4
  73.0 0.1 reshape.11
  73.0 4.4 %collective-permute-start.3 = (bf16[256,256]{1,0:T(8,128)(2,1)S(1)}, bf16[256,256]{1,0:T(8,128)(2,1)S(1)}, u32[]{:S(2)}, u32[]{:S(2)}) collective-permute-start(bf16[256,256]{1,0:T(8,128)(2,1)S(1)} %reshape.11), channel_id=1, source_target_pairs={{0,64},{32,96},{64,0},{96,32},{128,192},{160,224},{192,128},{224,1... | collective-permute-start | bytes 393224 | tf_op jit(solution)/shard_map/ppermute | solution.py:493
  77.4 2.5 %collective-permute-start.4 = (bf16[256,256]{1,0:T(8,128)(2,1)S(1)}, bf16[256,256]{1,0:T(8,128)(2,1)S(1)}, u32[]{:S(2)}, u32[]{:S(2)}) collective-permute-start(bf16[256,256]{1,0:T(8,128)(2,1)S(1)} %reshape.11), channel_id=1, source_target_pairs={{0,16},{1,17},{2,18},{3,19},{4,20},{5,21},{6,22},{7,23},{8,24},{9,... | collective-permute-start | bytes 393224 | tf_op jit(solution)/shard_map/ppermute | solution.py:509
  80.0 2.5 %collective-permute-start.5 = (bf16[256,256]{1,0:T(8,128)(2,1)S(1)}, bf16[256,256]{1,0:T(8,128)(2,1)S(1)}, u32[]{:S(2)}, u32[]{:S(2)}) collective-permute-start(bf16[256,256]{1,0:T(8,128)(2,1)S(1)} %reshape.11), channel_id=1, source_target_pairs={{0,80},{1,81},{2,82},{3,83},{4,84},{5,85},{6,86},{7,87},{8,88},{9,... | collective-permute-start | bytes 393224 | tf_op jit(solution)/shard_map/ppermute | solution.py:509
  82.5 0.0 collective-permute-done.3
  82.5 2.9 %collective-permute-done.4 = bf16[256,256]{1,0:T(8,128)(2,1)S(1)} collective-permute-done((bf16[256,256]{1,0:T(8,128)(2,1)S(1)}, bf16[256,256]{1,0:T(8,128)(2,1)S(1)}, u32[]{:S(2)}, u32[]{:S(2)}) %collective-permute-start.4) | collective-permute-done | bytes 131104 | tf_op jit(solution)/shard_map/ppermute | solution.py:509
  85.4 1.8 %collective-permute-done.5 = bf16[256,256]{1,0:T(8,128)(2,1)S(1)} collective-permute-done((bf16[256,256]{1,0:T(8,128)(2,1)S(1)}, bf16[256,256]{1,0:T(8,128)(2,1)S(1)}, u32[]{:S(2)}, u32[]{:S(2)}) %collective-permute-start.5) | collective-permute-done | bytes 131104 | tf_op jit(solution)/shard_map/ppermute | solution.py:509
  87.2 4.5 %collective-permute-start.6 = (bf16[1024,256]{1,0:T(8,128)(2,1)S(1)}, bf16[1024,256]{1,0:T(8,128)(2,1)S(1)}, u32[]{:S(2)}, u32[]{:S(2)}) collective-permute-start(bf16[1024,256]{1,0:T(8,128)(2,1)S(1)} %constant_dynamic-update-slice_fusion.kv_mine), channel_id=1, source_target_pairs={{0,32},{32,0},{64,96},{96,64},{128,160},{160,128},{192,224},{224,1... | collective-permute-start | bytes 1572872 | tf_op jit(solution)/shard_map/ppermute | solution.py:493
  91.7 1.5 %collective-permute-done.6.kv_other = bf16[1024,256]{1,0:T(8,128)(2,1)S(1)} collective-permute-done((bf16[1024,256]{1,0:T(8,128)(2,1)S(1)}, bf16[1024,256]{1,0:T(8,128)(2,1)S(1)}, u32[]{:S(2)}, u32[]{:S(2)}) %collective-permute-start.6) | collective-permute-done | bytes 524320 | tf_op jit(solution)/shard_map/ppermute | solution.py:493
  93.2 2.5 %shard_map.85 = (bf16[32,1408]{1,0:T(8,128)(2,1)S(1)}, bf16[32,1408]{1,0:T(8,128)(2,1)S(1)}, bf16[32,1408]{1,0:T(8,128)(2,1)S(1)}, bf16[32,1408]{1,0:T(8,128)(2,1)S(1)}) custom-call(bf16[32,1280]{1,0:T(8,128)(2,1)S(1)} %get-tuple-element.36.q0, bf16[32,1280]{1,0:T(8,128)(2,1)S(1)} %collective-permute-done.q1, ...), custom_call_target="tpu_custom_call" | custom-call | flops 1000000000 | bytes 4194304 | tf_op jit(solution)/shard_map/pallas_call | solution.py:394
  95.7 3.2 %collective-permute-start.7 = (bf16[32,1408]{1,0:T(8,128)(2,1)S(1)}, bf16[32,1408]{1,0:T(8,128)(2,1)S(1)}, u32[]{:S(2)}, u32[]{:S(2)}) collective-permute-start(bf16[32,1408]{1,0:T(8,128)(2,1)S(1)} %get-tuple-element.42), channel_id=1, source_target_pairs={{0,128},{32,160},{64,192},{96,224},{128,0},{160,32},{192,64},{224,... | collective-permute-start | bytes 270344 | tf_op jit(solution)/shard_map/ppermute | solution.py:493
  98.9 4.5 %collective-permute-start.8 = (bf16[32,1408]{1,0:T(8,128)(2,1)S(1)}, bf16[32,1408]{1,0:T(8,128)(2,1)S(1)}, u32[]{:S(2)}, u32[]{:S(2)}) collective-permute-start(bf16[32,1408]{1,0:T(8,128)(2,1)S(1)} %get-tuple-element.43), channel_id=1, source_target_pairs={{0,256},{32,288},{64,320},{96,352},{128,384},{160,416},{192,448},{... | collective-permute-start | bytes 270344 | tf_op jit(solution)/shard_map/ppermute | solution.py:493
  103.4 1.9 %collective-permute-start.9 = (bf16[32,1408]{1,0:T(8,128)(2,1)S(1)}, bf16[32,1408]{1,0:T(8,128)(2,1)S(1)}, u32[]{:S(2)}, u32[]{:S(2)}) collective-permute-start(bf16[32,1408]{1,0:T(8,128)(2,1)S(1)} %get-tuple-element.44), channel_id=1, source_target_pairs={{0,384},{32,416},{64,448},{96,480},{128,256},{160,288},{192,320},{... | collective-permute-start | bytes 270344 | tf_op jit(solution)/shard_map/ppermute | solution.py:493
  105.4 0.0 collective-permute-done.7.refs_1_
  105.4 0.6 collective-permute-done.8.refs_2_
  106.0 4.0 %collective-permute-done.9.refs_3_ = bf16[32,1408]{1,0:T(8,128)(2,1)S(1)} collective-permute-done((bf16[32,1408]{1,0:T(8,128)(2,1)S(1)}, bf16[32,1408]{1,0:T(8,128)(2,1)S(1)}, u32[]{:S(2)}, u32[]{:S(2)}) %collective-permute-start.9) | collective-permute-done | bytes 90144 | tf_op jit(solution)/shard_map/ppermute | solution.py:493
  109.9 0.0 all-to-all-done.1.got_ref
  109.9 2.2 %shard_map.86 = bf16[32,5120]{1,0:T(8,128)(2,1)} custom-call(bf16[32,2,5248]{2,1,0:T(2,128)(2,1)S(1)} %all-to-all-done.1.got_ref, bf16[48,5248]{1,0:T(8,128)(2,1)S(1)} %get-tuple-element.35.own_ref, f32[128,128]{1,0:T(8,128)S(1)} %get-tuple-element.26.where_ref, bf16[32,1408]{1,0:T(8,128)(2,1)S(1)} %get-tuple-element.41.refs_0_, ...), custom_call_target="tpu_custom_call" | custom-call | flops 100000000 | bytes 4194304 | tf_op jit(solution)/shard_map/pallas_call | solution.py:394
  (4 shorter events, 0.0 us)
Async XLA Ops:
  3.0 57.7 %all-to-all-start = ((bf16[32,2,6272]{2,1,0:T(2,128)(2,1)}), bf16[32,2,6272]{2,1,0:T(2,128)(2,1)S(1)}, u32[]{:S(2)}, u32[]{:S(2)}) async-start(bf16[32,2,6272]{2,1,0:T(2,128)(2,1)} %get-tuple-element.25), calls=%async_computation | async-start | bytes 1605632 | tf_op jit(solution)/shard_map/all_to_all | solution.py:495
  21.3 9.7 %collective-permute-start = (bf16[32,1280]{1,0:T(8,128)(2,1)S(1)}, bf16[32,1280]{1,0:T(8,128)(2,1)S(1)}, u32[]{:S(2)}, u32[]{:S(2)}) collective-permute-start(bf16[32,1280]{1,0:T(8,128)(2,1)S(1)} %get-tuple-element.29), channel_id=1, source_target_pairs={{0,128},{32,160},{64,192},{96,224},{128,0},{160,32},{192,64},{224,... | collective-permute-start | bytes 245768 | tf_op jit(solution)/shard_map/ppermute | solution.py:493
  24.5 7.0 %collective-permute-start.1 = (bf16[32,1280]{1,0:T(8,128)(2,1)S(1)}, bf16[32,1280]{1,0:T(8,128)(2,1)S(1)}, u32[]{:S(2)}, u32[]{:S(2)}) collective-permute-start(bf16[32,1280]{1,0:T(8,128)(2,1)S(1)} %get-tuple-element.30), channel_id=1, source_target_pairs={{0,256},{32,288},{64,320},{96,352},{128,384},{160,416},{192,448},{... | collective-permute-start | bytes 245768 | tf_op jit(solution)/shard_map/ppermute | solution.py:493
  29.0 6.7 %collective-permute-start.2 = (bf16[32,1280]{1,0:T(8,128)(2,1)S(1)}, bf16[32,1280]{1,0:T(8,128)(2,1)S(1)}, u32[]{:S(2)}, u32[]{:S(2)}) collective-permute-start(bf16[32,1280]{1,0:T(8,128)(2,1)S(1)} %get-tuple-element.31), channel_id=1, source_target_pairs={{0,384},{32,416},{64,448},{96,480},{128,256},{160,288},{192,320},{... | collective-permute-start | bytes 245768 | tf_op jit(solution)/shard_map/ppermute | solution.py:493
  65.2 44.7 %all-to-all-start.1 = ((bf16[32,2,5248]{2,1,0:T(2,128)(2,1)}), bf16[32,2,5248]{2,1,0:T(2,128)(2,1)S(1)}, u32[]{:S(2)}, u32[]{:S(2)}) async-start(bf16[32,2,5248]{2,1,0:T(2,128)(2,1)} %get-tuple-element.33), calls=%async_computation.1 | async-start | bytes 1343488 | tf_op jit(solution)/shard_map/all_to_all | solution.py:495
  73.0 9.4 %collective-permute-start.3 = (bf16[256,256]{1,0:T(8,128)(2,1)S(1)}, bf16[256,256]{1,0:T(8,128)(2,1)S(1)}, u32[]{:S(2)}, u32[]{:S(2)}) collective-permute-start(bf16[256,256]{1,0:T(8,128)(2,1)S(1)} %reshape.11), channel_id=1, source_target_pairs={{0,64},{32,96},{64,0},{96,32},{128,192},{160,224},{192,128},{224,1... | collective-permute-start | bytes 393224 | tf_op jit(solution)/shard_map/ppermute | solution.py:493
  77.4 7.9 %collective-permute-start.4 = (bf16[256,256]{1,0:T(8,128)(2,1)S(1)}, bf16[256,256]{1,0:T(8,128)(2,1)S(1)}, u32[]{:S(2)}, u32[]{:S(2)}) collective-permute-start(bf16[256,256]{1,0:T(8,128)(2,1)S(1)} %reshape.11), channel_id=1, source_target_pairs={{0,16},{1,17},{2,18},{3,19},{4,20},{5,21},{6,22},{7,23},{8,24},{9,... | collective-permute-start | bytes 393224 | tf_op jit(solution)/shard_map/ppermute | solution.py:509
  80.0 7.2 %collective-permute-start.5 = (bf16[256,256]{1,0:T(8,128)(2,1)S(1)}, bf16[256,256]{1,0:T(8,128)(2,1)S(1)}, u32[]{:S(2)}, u32[]{:S(2)}) collective-permute-start(bf16[256,256]{1,0:T(8,128)(2,1)S(1)} %reshape.11), channel_id=1, source_target_pairs={{0,80},{1,81},{2,82},{3,83},{4,84},{5,85},{6,86},{7,87},{8,88},{9,... | collective-permute-start | bytes 393224 | tf_op jit(solution)/shard_map/ppermute | solution.py:509
  87.2 6.0 %collective-permute-start.6 = (bf16[1024,256]{1,0:T(8,128)(2,1)S(1)}, bf16[1024,256]{1,0:T(8,128)(2,1)S(1)}, u32[]{:S(2)}, u32[]{:S(2)}) collective-permute-start(bf16[1024,256]{1,0:T(8,128)(2,1)S(1)} %constant_dynamic-update-slice_fusion.kv_mine), channel_id=1, source_target_pairs={{0,32},{32,0},{64,96},{96,64},{128,160},{160,128},{192,224},{224,1... | collective-permute-start | bytes 1572872 | tf_op jit(solution)/shard_map/ppermute | solution.py:493
  95.7 9.7 %collective-permute-start.7 = (bf16[32,1408]{1,0:T(8,128)(2,1)S(1)}, bf16[32,1408]{1,0:T(8,128)(2,1)S(1)}, u32[]{:S(2)}, u32[]{:S(2)}) collective-permute-start(bf16[32,1408]{1,0:T(8,128)(2,1)S(1)} %get-tuple-element.42), channel_id=1, source_target_pairs={{0,128},{32,160},{64,192},{96,224},{128,0},{160,32},{192,64},{224,... | collective-permute-start | bytes 270344 | tf_op jit(solution)/shard_map/ppermute | solution.py:493
  98.9 7.1 %collective-permute-start.8 = (bf16[32,1408]{1,0:T(8,128)(2,1)S(1)}, bf16[32,1408]{1,0:T(8,128)(2,1)S(1)}, u32[]{:S(2)}, u32[]{:S(2)}) collective-permute-start(bf16[32,1408]{1,0:T(8,128)(2,1)S(1)} %get-tuple-element.43), channel_id=1, source_target_pairs={{0,256},{32,288},{64,320},{96,352},{128,384},{160,416},{192,448},{... | collective-permute-start | bytes 270344 | tf_op jit(solution)/shard_map/ppermute | solution.py:493
  103.4 6.5 %collective-permute-start.9 = (bf16[32,1408]{1,0:T(8,128)(2,1)S(1)}, bf16[32,1408]{1,0:T(8,128)(2,1)S(1)}, u32[]{:S(2)}, u32[]{:S(2)}) collective-permute-start(bf16[32,1408]{1,0:T(8,128)(2,1)S(1)} %get-tuple-element.44), channel_id=1, source_target_pairs={{0,384},{32,416},{64,448},{96,480},{128,256},{160,288},{192,320},{... | collective-permute-start | bytes 270344 | tf_op jit(solution)/shard_map/ppermute | solution.py:493

commit v8 on v7

--- a/solution.py
+++ b/solution.py
@@ -174,7 +174,7 @@
 
 
 def pages_kernel(
-    got_ref, local_ref, k_hbm, v_hbm, answer_ref, own_ref, k_ref, v_ref, chunk_sems,
+    got_ref, local_ref, k_ref, v_hbm, answer_ref, own_ref, v_ref, chunk_sems,
 ):
     devices = got_ref.shape[0]
     cells = devices * CAP
@@ -187,9 +187,7 @@
         kv_at = (every, every, pl.ds(c * pair, pair))
         chunks.append(
             load(
-                (k_hbm.at[kv_at], v_hbm.at[kv_at]),
-                (k_ref.at[kv_at], v_ref.at[kv_at]),
-                chunk_sems.at[c],
+                (v_hbm.at[kv_at],), (v_ref.at[kv_at],), chunk_sems.at[pl.ds(c, 1)]
             )
         )
     wide = (step, step * PAGE)
@@ -250,9 +248,6 @@
         asked = got_ref[:, :, cols].reshape(cells, CHUNK)
         return (dot(fetch, asked) + local_ref[:, cols].astype(F32)).astype(BF16)
 
-    for chunk in chunks:
-        for copy in chunk:
-            copy.wait()
     steps = [(c, g) for c in range(CHUNKS) for g in range(len(spans))]
     rows = {c: ask(c) for c in range(CHUNKS)}
     scores = {s: score(*s, rows[s[0]]) for s in steps[:2]}
@@ -263,6 +258,12 @@
             scores[t] = score(*t, rows[t[0]])
         if s is not None:
             weighed[s] = weigh(scores.pop(s))
+        if n == 1:
+            for copy in chunks[0] + chunks[1]:
+                copy.wait()
+        if n == 7:
+            for copy in chunks[2] + chunks[3]:
+                copy.wait()
         if n >= 1:
             mix(*steps[n - 1], *weighed.pop(steps[n - 1]))
     for g in range(pool // step):
@@ -443,6 +444,7 @@
 
 
 def pages(got, local, suffix_keys, suffix_values):
+    suffix_keys = pltpu.with_memory_space_constraint(suffix_keys, pltpu.VMEM)
     shape = (got.shape[0], CAP, ROW)
     return call(
         pages_kernel,
@@ -452,8 +454,8 @@
         local,
         suffix_keys,
         suffix_values,
-        in_hbm=(2, 3),
-        scratch=(*map(like, (suffix_keys, suffix_values)), semaphores(CHUNKS, 2)),
+        in_hbm=(3,),
+        scratch=(like(suffix_values), semaphores(CHUNKS)),
     )
 
 

time: 113 us -> 112 us (level)
  local copies, waits for them, and re-layouts: 0.19 us -> 2.09 us
  waiting for transfers between devices: 40.6 us -> 38.7 us
    unnamed x3 -> x17, local copies, waits for them, and re-layouts: 0.03 us -> 1.93 us
    ppermute x8, waiting for transfers between devices: 10.8 us -> 9.54 us  [body(): lax.ppermute(x, 'grp', [(i, i ^ bits) for i in range(group)])]
  transfers between devices with their start and end apart: 12 -> 12, of which waited for: 8 -> 7; matrix products, arithmetic and copies ran while one was open for 0% -> 0% of each run, Pallas kernels for 3% -> 3%
where the time goes in v8:
time: 112 us; the launch traced here: 111 us
  starting transfers between devices  57.9 us (52%)
  waiting for transfers between devices  38.7 us (35%)
  Pallas kernels  12.6 us (11%)
  local copies, waits for them, and re-layouts  2.09 us (2%)
    ppermute x8, starting transfers between devices, body(): lax.ppermute(x, 'grp', [(i, i ^ bits) for i in range(group)])  28.2 us
    all_to_all x2, starting transfers between devices, body(): lax.all_to_all(x, 'blk', split_axis=0, concat_axis=0, tiled=True)  24.7 us
    all_to_all x2, waiting for transfers between devices, body(): lax.all_to_all(x, 'blk', split_axis=0, concat_axis=0, tiled=True)  24.4 us
    pallas_call x5, Pallas kernels, call(): pl.pallas_call(kernel, out_shape=[jax.ShapeDtypeStruct(s, d) for s, d in...  12.6 us
    ppermute x8, waiting for transfers between devices, body(): lax.ppermute(x, 'grp', [(i, i ^ bits) for i in range(group)])  9.54 us
    ppermute x1, waiting for transfers between devices, body(): lax.ppermute(part, 'blk', pairs)  2.88 us
    ppermute x1, starting transfers between devices, body(): lax.ppermute(part, 'blk', pairs)  2.54 us
    ppermute x1, starting transfers between devices, body(): lax.ppermute(part, ('grp', 'blk'), both)  2.46 us
  transfers between devices with their start and end apart: 12, of which 7 were waited for; matrix products, arithmetic and copies ran while one was open for 0% of the time, Pallas kernels for 3%

profile of v8, /device:TPU:1, one launch (start us, length us, event | category | flops | bytes accessed | tf_op | source)
XLA Modules:
  0.0 111.5 jit_solution(145049997106471915)
XLA Ops:
  0.0 3.1 %shard_map.82 = (bf16[32,2,6272]{2,1,0:T(2,128)(2,1)}, f32[128,128]{1,0:T(8,128)S(1)}) custom-call(bf16[32,5120]{1,0:T(8,128)(2,1)} %q_hbm.3, s32[4,32]{1,0:T(4,128)} %bitcast.4, s32[1,32]{1,0:T(1,128)} %bitcast.5, s32[12,128]{1,0:T(8,128)} %bitcast.3, bf16[32,1024]{1,0:T(8,128)(2,1)} %pk_hbm.1, bf16[32,1024]{1,0:T(8,128)(2,1)} %pv_hbm.1), custom_call_target="tpu_custom_call" | custom-call | flops 100000000 | bytes 4194304 | tf_op jit(solution)/shard_map/pallas_call | solution.py:395
  3.1 17.0 %all-to-all-start = ((bf16[32,2,6272]{2,1,0:T(2,128)(2,1)}), bf16[32,2,6272]{2,1,0:T(2,128)(2,1)S(1)}, u32[]{:S(2)}, u32[]{:S(2)}) async-start(bf16[32,2,6272]{2,1,0:T(2,128)(2,1)} %get-tuple-element.25), calls=%async_computation | async-start | bytes 1605632 | tf_op jit(solution)/shard_map/all_to_all | solution.py:497
  20.1 1.3 %shard_map.83 = (bf16[48,5248]{1,0:T(8,128)(2,1)S(1)}, bf16[32,1280]{1,0:T(8,128)(2,1)S(1)}, bf16[32,1280]{1,0:T(8,128)(2,1)S(1)}, bf16[32,1280]{1,0:T(8,128)(2,1)S(1)}, bf16[32,1280]{1,0:T(8,128)(2,1)S(1)}) custom-call(bf16[32,5120]{1,0:T(8,128)(2,1)} %q_hbm.3, f32[128,128]{1,0:T(8,128)S(1)} %get-tuple-element.26.where_ref), custom_call_target="tpu_custom_call" | custom-call | flops 100000000 | bytes 4194304 | tf_op jit(solution)/shard_map/pallas_call | solution.py:395
  21.4 3.2 %collective-permute-start = (bf16[32,1280]{1,0:T(8,128)(2,1)S(1)}, bf16[32,1280]{1,0:T(8,128)(2,1)S(1)}, u32[]{:S(2)}, u32[]{:S(2)}) collective-permute-start(bf16[32,1280]{1,0:T(8,128)(2,1)S(1)} %get-tuple-element.29), channel_id=1, source_target_pairs={{0,128},{32,160},{64,192},{96,224},{128,0},{160,32},{192,64},{224,... | collective-permute-start | bytes 245768 | tf_op jit(solution)/shard_map/ppermute | solution.py:495
  24.6 4.5 %collective-permute-start.1 = (bf16[32,1280]{1,0:T(8,128)(2,1)S(1)}, bf16[32,1280]{1,0:T(8,128)(2,1)S(1)}, u32[]{:S(2)}, u32[]{:S(2)}) collective-permute-start(bf16[32,1280]{1,0:T(8,128)(2,1)S(1)} %get-tuple-element.30), channel_id=1, source_target_pairs={{0,256},{32,288},{64,320},{96,352},{128,384},{160,416},{192,448},{... | collective-permute-start | bytes 245768 | tf_op jit(solution)/shard_map/ppermute | solution.py:495
  29.1 1.9 %collective-permute-start.2 = (bf16[32,1280]{1,0:T(8,128)(2,1)S(1)}, bf16[32,1280]{1,0:T(8,128)(2,1)S(1)}, u32[]{:S(2)}, u32[]{:S(2)}) collective-permute-start(bf16[32,1280]{1,0:T(8,128)(2,1)S(1)} %get-tuple-element.31), channel_id=1, source_target_pairs={{0,384},{32,416},{64,448},{96,480},{128,256},{160,288},{192,320},{... | collective-permute-start | bytes 245768 | tf_op jit(solution)/shard_map/ppermute | solution.py:495
  31.1 0.0 collective-permute-done.q1
  31.1 0.0 copy-start.1
  31.1 0.6 copy-done.1
  31.7 0.6 copy-done.3
  32.3 3.5 %collective-permute-done.2.q3 = bf16[32,1280]{1,0:T(8,128)(2,1)S(1)} collective-permute-done((bf16[32,1280]{1,0:T(8,128)(2,1)S(1)}, bf16[32,1280]{1,0:T(8,128)(2,1)S(1)}, u32[]{:S(2)}, u32[]{:S(2)}) %collective-permute-start.2) | collective-permute-done | bytes 81952 | tf_op jit(solution)/shard_map/ppermute | solution.py:495
  35.8 0.6 copy-done.5
  36.4 24.4 %all-to-all-done.got_ref = bf16[32,2,6272]{2,1,0:T(2,128)(2,1)S(1)} async-done(((bf16[32,2,6272]{2,1,0:T(2,128)(2,1)}), bf16[32,2,6272]{2,1,0:T(2,128)(2,1)S(1)}, u32[]{:S(2)}, u32[]{:S(2)}) %all-to-all-start) | async-done | bytes 802848 | tf_op jit(solution)/shard_map/all_to_all | solution.py:497
  60.9 3.5 %shard_map.84 = (bf16[32,2,5248]{2,1,0:T(2,128)(2,1)}, bf16[48,5248]{1,0:T(8,128)(2,1)S(1)}) custom-call(bf16[32,2,6272]{2,1,0:T(2,128)(2,1)S(1)} %all-to-all-done.got_ref, bf16[48,5248]{1,0:T(8,128)(2,1)S(1)} %get-tuple-element.32.local_ref, bf16[48,16,1024]{2,1,0:T(8,128)(2,1)S(1)} %copy-done, bf16[48,16,1024]{2,1,0:T(8,128)(2,1)} %v_hbm.1), custom_call_target="tpu_custom_call" | custom-call | flops 1000000000 | bytes 4194304 | tf_op jit(solution)/shard_map/pallas_call | solution.py:395
  64.4 0.0 copy-start.2
  64.4 7.8 %all-to-all-start.1 = ((bf16[32,2,5248]{2,1,0:T(2,128)(2,1)}), bf16[32,2,5248]{2,1,0:T(2,128)(2,1)S(1)}, u32[]{:S(2)}, u32[]{:S(2)}) async-start(bf16[32,2,5248]{2,1,0:T(2,128)(2,1)} %get-tuple-element.33), calls=%async_computation.1 | async-start | bytes 1343488 | tf_op jit(solution)/shard_map/all_to_all | solution.py:497
  72.2 0.1 slice.4
  72.3 0.1 reshape.11
  72.3 4.4 %collective-permute-start.3 = (bf16[256,256]{1,0:T(8,128)(2,1)S(1)}, bf16[256,256]{1,0:T(8,128)(2,1)S(1)}, u32[]{:S(2)}, u32[]{:S(2)}) collective-permute-start(bf16[256,256]{1,0:T(8,128)(2,1)S(1)} %reshape.11), channel_id=1, source_target_pairs={{0,64},{32,96},{64,0},{96,32},{128,192},{160,224},{192,128},{224,1... | collective-permute-start | bytes 393224 | tf_op jit(solution)/shard_map/ppermute | solution.py:495
  76.7 2.5 %collective-permute-start.4 = (bf16[256,256]{1,0:T(8,128)(2,1)S(1)}, bf16[256,256]{1,0:T(8,128)(2,1)S(1)}, u32[]{:S(2)}, u32[]{:S(2)}) collective-permute-start(bf16[256,256]{1,0:T(8,128)(2,1)S(1)} %reshape.11), channel_id=1, source_target_pairs={{0,16},{1,17},{2,18},{3,19},{4,20},{5,21},{6,22},{7,23},{8,24},{9,... | collective-permute-start | bytes 393224 | tf_op jit(solution)/shard_map/ppermute | solution.py:511
  79.3 2.5 %collective-permute-start.5 = (bf16[256,256]{1,0:T(8,128)(2,1)S(1)}, bf16[256,256]{1,0:T(8,128)(2,1)S(1)}, u32[]{:S(2)}, u32[]{:S(2)}) collective-permute-start(bf16[256,256]{1,0:T(8,128)(2,1)S(1)} %reshape.11), channel_id=1, source_target_pairs={{0,80},{1,81},{2,82},{3,83},{4,84},{5,85},{6,86},{7,87},{8,88},{9,... | collective-permute-start | bytes 393224 | tf_op jit(solution)/shard_map/ppermute | solution.py:511
  81.8 2.9 %collective-permute-done.4 = bf16[256,256]{1,0:T(8,128)(2,1)S(1)} collective-permute-done((bf16[256,256]{1,0:T(8,128)(2,1)S(1)}, bf16[256,256]{1,0:T(8,128)(2,1)S(1)}, u32[]{:S(2)}, u32[]{:S(2)}) %collective-permute-start.4) | collective-permute-done | bytes 131104 | tf_op jit(solution)/shard_map/ppermute | solution.py:511
  84.7 1.8 %collective-permute-done.5 = bf16[256,256]{1,0:T(8,128)(2,1)S(1)} collective-permute-done((bf16[256,256]{1,0:T(8,128)(2,1)S(1)}, bf16[256,256]{1,0:T(8,128)(2,1)S(1)}, u32[]{:S(2)}, u32[]{:S(2)}) %collective-permute-start.5) | collective-permute-done | bytes 131104 | tf_op jit(solution)/shard_map/ppermute | solution.py:511
  86.5 4.5 %collective-permute-start.6 = (bf16[1024,256]{1,0:T(8,128)(2,1)S(1)}, bf16[1024,256]{1,0:T(8,128)(2,1)S(1)}, u32[]{:S(2)}, u32[]{:S(2)}) collective-permute-start(bf16[1024,256]{1,0:T(8,128)(2,1)S(1)} %constant_dynamic-update-slice_fusion.kv_mine), channel_id=1, source_target_pairs={{0,32},{32,0},{64,96},{96,64},{128,160},{160,128},{192,224},{224,1... | collective-permute-start | bytes 1572872 | tf_op jit(solution)/shard_map/ppermute | solution.py:495
  91.0 1.5 %collective-permute-done.6.kv_other = bf16[1024,256]{1,0:T(8,128)(2,1)S(1)} collective-permute-done((bf16[1024,256]{1,0:T(8,128)(2,1)S(1)}, bf16[1024,256]{1,0:T(8,128)(2,1)S(1)}, u32[]{:S(2)}, u32[]{:S(2)}) %collective-permute-start.6) | collective-permute-done | bytes 524320 | tf_op jit(solution)/shard_map/ppermute | solution.py:495
  92.5 2.5 %shard_map.85 = (bf16[32,1408]{1,0:T(8,128)(2,1)S(1)}, bf16[32,1408]{1,0:T(8,128)(2,1)S(1)}, bf16[32,1408]{1,0:T(8,128)(2,1)S(1)}, bf16[32,1408]{1,0:T(8,128)(2,1)S(1)}) custom-call(bf16[32,1280]{1,0:T(8,128)(2,1)S(1)} %get-tuple-element.36.q0, bf16[32,1280]{1,0:T(8,128)(2,1)S(1)} %copy-done.2, bf16[32,1280]{1,0:T(8,128)(2,1)S(1)} %copy-done.4, ...), custom_call_target="tpu_custom_call" | custom-call | flops 1000000000 | bytes 4194304 | tf_op jit(solution)/shard_map/pallas_call | solution.py:395
  95.0 3.2 %collective-permute-start.7 = (bf16[32,1408]{1,0:T(8,128)(2,1)S(1)}, bf16[32,1408]{1,0:T(8,128)(2,1)S(1)}, u32[]{:S(2)}, u32[]{:S(2)}) collective-permute-start(bf16[32,1408]{1,0:T(8,128)(2,1)S(1)} %get-tuple-element.42), channel_id=1, source_target_pairs={{0,128},{32,160},{64,192},{96,224},{128,0},{160,32},{192,64},{224,... | collective-permute-start | bytes 270344 | tf_op jit(solution)/shard_map/ppermute | solution.py:495
  98.2 4.5 %collective-permute-start.8 = (bf16[32,1408]{1,0:T(8,128)(2,1)S(1)}, bf16[32,1408]{1,0:T(8,128)(2,1)S(1)}, u32[]{:S(2)}, u32[]{:S(2)}) collective-permute-start(bf16[32,1408]{1,0:T(8,128)(2,1)S(1)} %get-tuple-element.43), channel_id=1, source_target_pairs={{0,256},{32,288},{64,320},{96,352},{128,384},{160,416},{192,448},{... | collective-permute-start | bytes 270344 | tf_op jit(solution)/shard_map/ppermute | solution.py:495
  102.8 1.9 %collective-permute-start.9 = (bf16[32,1408]{1,0:T(8,128)(2,1)S(1)}, bf16[32,1408]{1,0:T(8,128)(2,1)S(1)}, u32[]{:S(2)}, u32[]{:S(2)}) collective-permute-start(bf16[32,1408]{1,0:T(8,128)(2,1)S(1)} %get-tuple-element.44), channel_id=1, source_target_pairs={{0,384},{32,416},{64,448},{96,480},{128,256},{160,288},{192,320},{... | collective-permute-start | bytes 270344 | tf_op jit(solution)/shard_map/ppermute | solution.py:495
  104.7 0.6 collective-permute-done.8.refs_2_
  105.3 4.0 %collective-permute-done.9.refs_3_ = bf16[32,1408]{1,0:T(8,128)(2,1)S(1)} collective-permute-done((bf16[32,1408]{1,0:T(8,128)(2,1)S(1)}, bf16[32,1408]{1,0:T(8,128)(2,1)S(1)}, u32[]{:S(2)}, u32[]{:S(2)}) %collective-permute-start.9) | collective-permute-done | bytes 90144 | tf_op jit(solution)/shard_map/ppermute | solution.py:495
  109.3 2.2 %shard_map.86 = bf16[32,5120]{1,0:T(8,128)(2,1)} custom-call(bf16[32,2,5248]{2,1,0:T(2,128)(2,1)S(1)} %all-to-all-done.1.got_ref, bf16[48,5248]{1,0:T(8,128)(2,1)S(1)} %get-tuple-element.35.own_ref, f32[128,128]{1,0:T(8,128)S(1)} %get-tuple-element.26.where_ref, bf16[32,1408]{1,0:T(8,128)(2,1)S(1)} %get-tuple-element.41.refs_0_, ...), custom_call_target="tpu_custom_call" | custom-call | flops 100000000 | bytes 4194304 | tf_op jit(solution)/shard_map/pallas_call | solution.py:395
  (17 shorter events, 0.1 us)
Async XLA Ops:
  0.0 60.9 %copy-start = (bf16[48,16,1024]{2,1,0:T(8,128)(2,1)S(1)}, bf16[48,16,1024]{2,1,0:T(8,128)(2,1)}, u32[]{:S(2)}) copy-start(bf16[48,16,1024]{2,1,0:T(8,128)(2,1)} %k_ref.1) | copy-start | bytes 4718596
  3.1 57.7 %all-to-all-start = ((bf16[32,2,6272]{2,1,0:T(2,128)(2,1)}), bf16[32,2,6272]{2,1,0:T(2,128)(2,1)S(1)}, u32[]{:S(2)}, u32[]{:S(2)}) async-start(bf16[32,2,6272]{2,1,0:T(2,128)(2,1)} %get-tuple-element.25), calls=%async_computation | async-start | bytes 1605632 | tf_op jit(solution)/shard_map/all_to_all | solution.py:497
  21.4 9.7 %collective-permute-start = (bf16[32,1280]{1,0:T(8,128)(2,1)S(1)}, bf16[32,1280]{1,0:T(8,128)(2,1)S(1)}, u32[]{:S(2)}, u32[]{:S(2)}) collective-permute-start(bf16[32,1280]{1,0:T(8,128)(2,1)S(1)} %get-tuple-element.29), channel_id=1, source_target_pairs={{0,128},{32,160},{64,192},{96,224},{128,0},{160,32},{192,64},{224,... | collective-permute-start | bytes 245768 | tf_op jit(solution)/shard_map/ppermute | solution.py:495
  24.6 7.1 %collective-permute-start.1 = (bf16[32,1280]{1,0:T(8,128)(2,1)S(1)}, bf16[32,1280]{1,0:T(8,128)(2,1)S(1)}, u32[]{:S(2)}, u32[]{:S(2)}) collective-permute-start(bf16[32,1280]{1,0:T(8,128)(2,1)S(1)} %get-tuple-element.30), channel_id=1, source_target_pairs={{0,256},{32,288},{64,320},{96,352},{128,384},{160,416},{192,448},{... | collective-permute-start | bytes 245768 | tf_op jit(solution)/shard_map/ppermute | solution.py:495
  29.1 6.7 %collective-permute-start.2 = (bf16[32,1280]{1,0:T(8,128)(2,1)S(1)}, bf16[32,1280]{1,0:T(8,128)(2,1)S(1)}, u32[]{:S(2)}, u32[]{:S(2)}) collective-permute-start(bf16[32,1280]{1,0:T(8,128)(2,1)S(1)} %get-tuple-element.31), channel_id=1, source_target_pairs={{0,384},{32,416},{64,448},{96,480},{128,256},{160,288},{192,320},{... | collective-permute-start | bytes 245768 | tf_op jit(solution)/shard_map/ppermute | solution.py:495
  31.1 0.6 copy-start.1
  31.7 0.6 copy-start.3
  35.8 0.6 copy-start.5
  64.4 28.2 %copy-start.2 = (bf16[32,1280]{1,0:T(8,128)(2,1)S(1)}, bf16[32,1280]{1,0:T(8,128)(2,1)}, u32[]{:S(2)}) copy-start(bf16[32,1280]{1,0:T(8,128)(2,1)} %copy-done.1) | copy-start | bytes 245764
  64.4 28.1 %copy-start.4 = (bf16[32,1280]{1,0:T(8,128)(2,1)S(1)}, bf16[32,1280]{1,0:T(8,128)(2,1)}, u32[]{:S(2)}) copy-start(bf16[32,1280]{1,0:T(8,128)(2,1)} %copy-done.3) | copy-start | bytes 245764
  64.4 28.1 %copy-start.6 = (bf16[32,1280]{1,0:T(8,128)(2,1)S(1)}, bf16[32,1280]{1,0:T(8,128)(2,1)}, u32[]{:S(2)}) copy-start(bf16[32,1280]{1,0:T(8,128)(2,1)} %copy-done.5) | copy-start | bytes 245764
  64.4 44.9 %all-to-all-start.1 = ((bf16[32,2,5248]{2,1,0:T(2,128)(2,1)}), bf16[32,2,5248]{2,1,0:T(2,128)(2,1)S(1)}, u32[]{:S(2)}, u32[]{:S(2)}) async-start(bf16[32,2,5248]{2,1,0:T(2,128)(2,1)} %get-tuple-element.33), calls=%async_computation.1 | async-start | bytes 1343488 | tf_op jit(solution)/shard_map/all_to_all | solution.py:497
  72.3 9.4 %collective-permute-start.3 = (bf16[256,256]{1,0:T(8,128)(2,1)S(1)}, bf16[256,256]{1,0:T(8,128)(2,1)S(1)}, u32[]{:S(2)}, u32[]{:S(2)}) collective-permute-start(bf16[256,256]{1,0:T(8,128)(2,1)S(1)} %reshape.11), channel_id=1, source_target_pairs={{0,64},{32,96},{64,0},{96,32},{128,192},{160,224},{192,128},{224,1... | collective-permute-start | bytes 393224 | tf_op jit(solution)/shard_map/ppermute | solution.py:495
  76.7 7.9 %collective-permute-start.4 = (bf16[256,256]{1,0:T(8,128)(2,1)S(1)}, bf16[256,256]{1,0:T(8,128)(2,1)S(1)}, u32[]{:S(2)}, u32[]{:S(2)}) collective-permute-start(bf16[256,256]{1,0:T(8,128)(2,1)S(1)} %reshape.11), channel_id=1, source_target_pairs={{0,16},{1,17},{2,18},{3,19},{4,20},{5,21},{6,22},{7,23},{8,24},{9,... | collective-permute-start | bytes 393224 | tf_op jit(solution)/shard_map/ppermute | solution.py:511
  79.3 7.2 %collective-permute-start.5 = (bf16[256,256]{1,0:T(8,128)(2,1)S(1)}, bf16[256,256]{1,0:T(8,128)(2,1)S(1)}, u32[]{:S(2)}, u32[]{:S(2)}) collective-permute-start(bf16[256,256]{1,0:T(8,128)(2,1)S(1)} %reshape.11), channel_id=1, source_target_pairs={{0,80},{1,81},{2,82},{3,83},{4,84},{5,85},{6,86},{7,87},{8,88},{9,... | collective-permute-start | bytes 393224 | tf_op jit(solution)/shard_map/ppermute | solution.py:511
  86.5 6.0 %collective-permute-start.6 = (bf16[1024,256]{1,0:T(8,128)(2,1)S(1)}, bf16[1024,256]{1,0:T(8,128)(2,1)S(1)}, u32[]{:S(2)}, u32[]{:S(2)}) collective-permute-start(bf16[1024,256]{1,0:T(8,128)(2,1)S(1)} %constant_dynamic-update-slice_fusion.kv_mine), channel_id=1, source_target_pairs={{0,32},{32,0},{64,96},{96,64},{128,160},{160,128},{192,224},{224,1... | collective-permute-start | bytes 1572872 | tf_op jit(solution)/shard_map/ppermute | solution.py:495
  95.0 9.7 %collective-permute-start.7 = (bf16[32,1408]{1,0:T(8,128)(2,1)S(1)}, bf16[32,1408]{1,0:T(8,128)(2,1)S(1)}, u32[]{:S(2)}, u32[]{:S(2)}) collective-permute-start(bf16[32,1408]{1,0:T(8,128)(2,1)S(1)} %get-tuple-element.42), channel_id=1, source_target_pairs={{0,128},{32,160},{64,192},{96,224},{128,0},{160,32},{192,64},{224,... | collective-permute-start | bytes 270344 | tf_op jit(solution)/shard_map/ppermute | solution.py:495
  98.2 7.0 %collective-permute-start.8 = (bf16[32,1408]{1,0:T(8,128)(2,1)S(1)}, bf16[32,1408]{1,0:T(8,128)(2,1)S(1)}, u32[]{:S(2)}, u32[]{:S(2)}) collective-permute-start(bf16[32,1408]{1,0:T(8,128)(2,1)S(1)} %get-tuple-element.43), channel_id=1, source_target_pairs={{0,256},{32,288},{64,320},{96,352},{128,384},{160,416},{192,448},{... | collective-permute-start | bytes 270344 | tf_op jit(solution)/shard_map/ppermute | solution.py:495
  102.8 6.5 %collective-permute-start.9 = (bf16[32,1408]{1,0:T(8,128)(2,1)S(1)}, bf16[32,1408]{1,0:T(8,128)(2,1)S(1)}, u32[]{:S(2)}, u32[]{:S(2)}) collective-permute-start(bf16[32,1408]{1,0:T(8,128)(2,1)S(1)} %get-tuple-element.44), channel_id=1, source_target_pairs={{0,384},{32,416},{64,448},{96,480},{128,256},{160,288},{192,320},{... | collective-permute-start | bytes 270344 | tf_op jit(solution)/shard_map/ppermute | solution.py:495

commit v9 on v8

--- a/solution.py
+++ b/solution.py
@@ -1,4 +1,5 @@
 import functools
+import math
 
 import jax
 import jax.numpy as jnp
@@ -25,6 +26,7 @@
 CHUNK = QCOLS // CHUNKS
 TOKENS_AT = 64
 SCALE = HD ** (-0.5)
+SCALE_2 = SCALE * math.log2(math.e)
 VERY_LOW = -1e30
 F32 = jnp.float32
 BF16 = jnp.bfloat16
@@ -223,13 +225,13 @@
             [jnp.concatenate([one, nothing], axis=1), jnp.concatenate([nothing, two], axis=1)], axis=0
         )
         keys = k_ref[span, :, c * pair : (c + 1) * pair].reshape(step * PAGE, pair)
-        return dot_t(heads, keys) * SCALE + masks[g]
+        return dot_t(heads, keys) + masks[g]
 
     def weigh(scores):
         top = jnp.max(scores, axis=1, keepdims=True)
-        weights = jnp.exp(scores - top)
+        weights = jnp.exp2((scores - top) * SCALE_2)
         total = jnp.sum(weights, axis=1, keepdims=True)
-        return weights.astype(BF16), total, top + jnp.log(total)
+        return weights.astype(BF16), total, top * SCALE + jnp.log(total)
 
     def mix(c, g, weights, total, log_sum):
         span = spans[g]
@@ -294,13 +296,13 @@
         def score(h):
             heads = jnp.concatenate([q[:, h * HD : (h + 1) * HD] for q in asked], axis=0)
             kv = slice(h // GROUP * HD, (h // GROUP + 1) * HD)
-            return [dot_t(heads, k_ref[c, kv]) * SCALE for c in chunks]
+            return [dot_t(heads, k_ref[c, kv]) for c in chunks]
 
         def weigh(scores):
             top = jnp.max(functools.reduce(jnp.maximum, scores), axis=1, keepdims=True)
-            weights = [jnp.exp(s - top) for s in scores]
+            weights = [jnp.exp2((s - top) * SCALE_2) for s in scores]
             total = jnp.sum(functools.reduce(jnp.add, weights), axis=1, keepdims=True)
-            return [w.astype(BF16) for w in weights], total, top + jnp.log(total)
+            return [w.astype(BF16) for w in weights], total, top * SCALE + jnp.log(total)
 
         def mix(h, weights, total):
             kv = slice(h // GROUP * HD, (h // GROUP + 1) * HD)

time: 112 us -> 112 us (level)
  no operation moved by 1% of the time
where the time goes in v9:
time: 112 us; the launch traced here: 111 us
  starting transfers between devices  57.9 us (52%)
  waiting for transfers between devices  39 us (35%)
  Pallas kernels  12.2 us (11%)
  local copies, waits for them, and re-layouts  2.09 us (2%)
    ppermute x8, starting transfers between devices, body(): lax.ppermute(x, 'grp', [(i, i ^ bits) for i in range(group)])  28.2 us
    all_to_all x2, starting transfers between devices, body(): lax.all_to_all(x, 'blk', split_axis=0, concat_axis=0, tiled=True)  24.7 us
    all_to_all x2, waiting for transfers between devices, body(): lax.all_to_all(x, 'blk', split_axis=0, concat_axis=0, tiled=True)  24.4 us
    pallas_call x5, Pallas kernels, call(): pl.pallas_call(kernel, out_shape=[jax.ShapeDtypeStruct(s, d) for s, d in...  12.2 us
    ppermute x8, waiting for transfers between devices, body(): lax.ppermute(x, 'grp', [(i, i ^ bits) for i in range(group)])  9.84 us
    ppermute x1, waiting for transfers between devices, body(): lax.ppermute(part, 'blk', pairs)  2.88 us
    ppermute x1, starting transfers between devices, body(): lax.ppermute(part, 'blk', pairs)  2.54 us
    ppermute x1, starting transfers between devices, body(): lax.ppermute(part, ('grp', 'blk'), both)  2.47 us
  transfers between devices with their start and end apart: 12, of which 7 were waited for; matrix products, arithmetic and copies ran while one was open for 0% of the time, Pallas kernels for 3%

profile of v9, /device:TPU:1, one launch (start us, length us, event | category | flops | bytes accessed | tf_op | source)
XLA Modules:
  0.0 111.4 jit_solution(11148575157625170517)
XLA Ops:
  0.0 3.1 %shard_map.82 = (bf16[32,2,6272]{2,1,0:T(2,128)(2,1)}, f32[128,128]{1,0:T(8,128)S(1)}) custom-call(bf16[32,5120]{1,0:T(8,128)(2,1)} %q_hbm.3, s32[4,32]{1,0:T(4,128)} %bitcast.4, s32[1,32]{1,0:T(1,128)} %bitcast.5, s32[12,128]{1,0:T(8,128)} %bitcast.3, bf16[32,1024]{1,0:T(8,128)(2,1)} %pk_hbm.1, bf16[32,1024]{1,0:T(8,128)(2,1)} %pv_hbm.1), custom_call_target="tpu_custom_call" | custom-call | flops 100000000 | bytes 4194304 | tf_op jit(solution)/shard_map/pallas_call | solution.py:397
  3.1 17.0 %all-to-all-start = ((bf16[32,2,6272]{2,1,0:T(2,128)(2,1)}), bf16[32,2,6272]{2,1,0:T(2,128)(2,1)S(1)}, u32[]{:S(2)}, u32[]{:S(2)}) async-start(bf16[32,2,6272]{2,1,0:T(2,128)(2,1)} %get-tuple-element.25), calls=%async_computation | async-start | bytes 1605632 | tf_op jit(solution)/shard_map/all_to_all | solution.py:499
  20.1 1.3 %shard_map.83 = (bf16[48,5248]{1,0:T(8,128)(2,1)S(1)}, bf16[32,1280]{1,0:T(8,128)(2,1)S(1)}, bf16[32,1280]{1,0:T(8,128)(2,1)S(1)}, bf16[32,1280]{1,0:T(8,128)(2,1)S(1)}, bf16[32,1280]{1,0:T(8,128)(2,1)S(1)}) custom-call(bf16[32,5120]{1,0:T(8,128)(2,1)} %q_hbm.3, f32[128,128]{1,0:T(8,128)S(1)} %get-tuple-element.26.where_ref), custom_call_target="tpu_custom_call" | custom-call | flops 100000000 | bytes 4194304 | tf_op jit(solution)/shard_map/pallas_call | solution.py:397
  21.4 3.2 %collective-permute-start = (bf16[32,1280]{1,0:T(8,128)(2,1)S(1)}, bf16[32,1280]{1,0:T(8,128)(2,1)S(1)}, u32[]{:S(2)}, u32[]{:S(2)}) collective-permute-start(bf16[32,1280]{1,0:T(8,128)(2,1)S(1)} %get-tuple-element.29), channel_id=1, source_target_pairs={{0,128},{32,160},{64,192},{96,224},{128,0},{160,32},{192,64},{224,... | collective-permute-start | bytes 245768 | tf_op jit(solution)/shard_map/ppermute | solution.py:497
  24.6 4.5 %collective-permute-start.1 = (bf16[32,1280]{1,0:T(8,128)(2,1)S(1)}, bf16[32,1280]{1,0:T(8,128)(2,1)S(1)}, u32[]{:S(2)}, u32[]{:S(2)}) collective-permute-start(bf16[32,1280]{1,0:T(8,128)(2,1)S(1)} %get-tuple-element.30), channel_id=1, source_target_pairs={{0,256},{32,288},{64,320},{96,352},{128,384},{160,416},{192,448},{... | collective-permute-start | bytes 245768 | tf_op jit(solution)/shard_map/ppermute | solution.py:497
  29.1 1.9 %collective-permute-start.2 = (bf16[32,1280]{1,0:T(8,128)(2,1)S(1)}, bf16[32,1280]{1,0:T(8,128)(2,1)S(1)}, u32[]{:S(2)}, u32[]{:S(2)}) collective-permute-start(bf16[32,1280]{1,0:T(8,128)(2,1)S(1)} %get-tuple-element.31), channel_id=1, source_target_pairs={{0,384},{32,416},{64,448},{96,480},{128,256},{160,288},{192,320},{... | collective-permute-start | bytes 245768 | tf_op jit(solution)/shard_map/ppermute | solution.py:497
  31.1 0.0 collective-permute-done.q1
  31.1 0.0 copy-start.1
  31.1 0.6 copy-done.1
  31.7 0.6 copy-done.3
  32.3 3.5 %collective-permute-done.2.q3 = bf16[32,1280]{1,0:T(8,128)(2,1)S(1)} collective-permute-done((bf16[32,1280]{1,0:T(8,128)(2,1)S(1)}, bf16[32,1280]{1,0:T(8,128)(2,1)S(1)}, u32[]{:S(2)}, u32[]{:S(2)}) %collective-permute-start.2) | collective-permute-done | bytes 81952 | tf_op jit(solution)/shard_map/ppermute | solution.py:497
  35.8 0.6 copy-done.5
  36.4 24.4 %all-to-all-done.got_ref = bf16[32,2,6272]{2,1,0:T(2,128)(2,1)S(1)} async-done(((bf16[32,2,6272]{2,1,0:T(2,128)(2,1)}), bf16[32,2,6272]{2,1,0:T(2,128)(2,1)S(1)}, u32[]{:S(2)}, u32[]{:S(2)}) %all-to-all-start) | async-done | bytes 802848 | tf_op jit(solution)/shard_map/all_to_all | solution.py:499
  60.9 3.5 %shard_map.84 = (bf16[32,2,5248]{2,1,0:T(2,128)(2,1)}, bf16[48,5248]{1,0:T(8,128)(2,1)S(1)}) custom-call(bf16[32,2,6272]{2,1,0:T(2,128)(2,1)S(1)} %all-to-all-done.got_ref, bf16[48,5248]{1,0:T(8,128)(2,1)S(1)} %get-tuple-element.32.local_ref, bf16[48,16,1024]{2,1,0:T(8,128)(2,1)S(1)} %copy-done, bf16[48,16,1024]{2,1,0:T(8,128)(2,1)} %v_hbm.1), custom_call_target="tpu_custom_call" | custom-call | flops 1000000000 | bytes 4194304 | tf_op jit(solution)/shard_map/pallas_call | solution.py:397
  64.4 0.0 copy-start.2
  64.4 7.8 %all-to-all-start.1 = ((bf16[32,2,5248]{2,1,0:T(2,128)(2,1)}), bf16[32,2,5248]{2,1,0:T(2,128)(2,1)S(1)}, u32[]{:S(2)}, u32[]{:S(2)}) async-start(bf16[32,2,5248]{2,1,0:T(2,128)(2,1)} %get-tuple-element.33), calls=%async_computation.1 | async-start | bytes 1343488 | tf_op jit(solution)/shard_map/all_to_all | solution.py:499
  72.2 0.1 slice.4
  72.3 0.1 reshape.11
  72.3 4.4 %collective-permute-start.3 = (bf16[256,256]{1,0:T(8,128)(2,1)S(1)}, bf16[256,256]{1,0:T(8,128)(2,1)S(1)}, u32[]{:S(2)}, u32[]{:S(2)}) collective-permute-start(bf16[256,256]{1,0:T(8,128)(2,1)S(1)} %reshape.11), channel_id=1, source_target_pairs={{0,64},{32,96},{64,0},{96,32},{128,192},{160,224},{192,128},{224,1... | collective-permute-start | bytes 393224 | tf_op jit(solution)/shard_map/ppermute | solution.py:497
  76.7 2.5 %collective-permute-start.4 = (bf16[256,256]{1,0:T(8,128)(2,1)S(1)}, bf16[256,256]{1,0:T(8,128)(2,1)S(1)}, u32[]{:S(2)}, u32[]{:S(2)}) collective-permute-start(bf16[256,256]{1,0:T(8,128)(2,1)S(1)} %reshape.11), channel_id=1, source_target_pairs={{0,16},{1,17},{2,18},{3,19},{4,20},{5,21},{6,22},{7,23},{8,24},{9,... | collective-permute-start | bytes 393224 | tf_op jit(solution)/shard_map/ppermute | solution.py:513
  79.3 2.5 %collective-permute-start.5 = (bf16[256,256]{1,0:T(8,128)(2,1)S(1)}, bf16[256,256]{1,0:T(8,128)(2,1)S(1)}, u32[]{:S(2)}, u32[]{:S(2)}) collective-permute-start(bf16[256,256]{1,0:T(8,128)(2,1)S(1)} %reshape.11), channel_id=1, source_target_pairs={{0,80},{1,81},{2,82},{3,83},{4,84},{5,85},{6,86},{7,87},{8,88},{9,... | collective-permute-start | bytes 393224 | tf_op jit(solution)/shard_map/ppermute | solution.py:513
  81.8 2.9 %collective-permute-done.4 = bf16[256,256]{1,0:T(8,128)(2,1)S(1)} collective-permute-done((bf16[256,256]{1,0:T(8,128)(2,1)S(1)}, bf16[256,256]{1,0:T(8,128)(2,1)S(1)}, u32[]{:S(2)}, u32[]{:S(2)}) %collective-permute-start.4) | collective-permute-done | bytes 131104 | tf_op jit(solution)/shard_map/ppermute | solution.py:513
  84.7 1.8 %collective-permute-done.5 = bf16[256,256]{1,0:T(8,128)(2,1)S(1)} collective-permute-done((bf16[256,256]{1,0:T(8,128)(2,1)S(1)}, bf16[256,256]{1,0:T(8,128)(2,1)S(1)}, u32[]{:S(2)}, u32[]{:S(2)}) %collective-permute-start.5) | collective-permute-done | bytes 131104 | tf_op jit(solution)/shard_map/ppermute | solution.py:513
  86.5 4.5 %collective-permute-start.6 = (bf16[1024,256]{1,0:T(8,128)(2,1)S(1)}, bf16[1024,256]{1,0:T(8,128)(2,1)S(1)}, u32[]{:S(2)}, u32[]{:S(2)}) collective-permute-start(bf16[1024,256]{1,0:T(8,128)(2,1)S(1)} %constant_dynamic-update-slice_fusion.kv_mine), channel_id=1, source_target_pairs={{0,32},{32,0},{64,96},{96,64},{128,160},{160,128},{192,224},{224,1... | collective-permute-start | bytes 1572872 | tf_op jit(solution)/shard_map/ppermute | solution.py:497
  91.0 1.5 %collective-permute-done.6.kv_other = bf16[1024,256]{1,0:T(8,128)(2,1)S(1)} collective-permute-done((bf16[1024,256]{1,0:T(8,128)(2,1)S(1)}, bf16[1024,256]{1,0:T(8,128)(2,1)S(1)}, u32[]{:S(2)}, u32[]{:S(2)}) %collective-permute-start.6) | collective-permute-done | bytes 524320 | tf_op jit(solution)/shard_map/ppermute | solution.py:497
  92.6 2.1 %shard_map.85 = (bf16[32,1408]{1,0:T(8,128)(2,1)S(1)}, bf16[32,1408]{1,0:T(8,128)(2,1)S(1)}, bf16[32,1408]{1,0:T(8,128)(2,1)S(1)}, bf16[32,1408]{1,0:T(8,128)(2,1)S(1)}) custom-call(bf16[32,1280]{1,0:T(8,128)(2,1)S(1)} %get-tuple-element.36.q0, bf16[32,1280]{1,0:T(8,128)(2,1)S(1)} %copy-done.2, bf16[32,1280]{1,0:T(8,128)(2,1)S(1)} %copy-done.4, ...), custom_call_target="tpu_custom_call" | custom-call | flops 1000000000 | bytes 4194304 | tf_op jit(solution)/shard_map/pallas_call | solution.py:397
  94.7 3.2 %collective-permute-start.7 = (bf16[32,1408]{1,0:T(8,128)(2,1)S(1)}, bf16[32,1408]{1,0:T(8,128)(2,1)S(1)}, u32[]{:S(2)}, u32[]{:S(2)}) collective-permute-start(bf16[32,1408]{1,0:T(8,128)(2,1)S(1)} %get-tuple-element.42), channel_id=1, source_target_pairs={{0,128},{32,160},{64,192},{96,224},{128,0},{160,32},{192,64},{224,... | collective-permute-start | bytes 270344 | tf_op jit(solution)/shard_map/ppermute | solution.py:497
  97.9 4.5 %collective-permute-start.8 = (bf16[32,1408]{1,0:T(8,128)(2,1)S(1)}, bf16[32,1408]{1,0:T(8,128)(2,1)S(1)}, u32[]{:S(2)}, u32[]{:S(2)}) collective-permute-start(bf16[32,1408]{1,0:T(8,128)(2,1)S(1)} %get-tuple-element.43), channel_id=1, source_target_pairs={{0,256},{32,288},{64,320},{96,352},{128,384},{160,416},{192,448},{... | collective-permute-start | bytes 270344 | tf_op jit(solution)/shard_map/ppermute | solution.py:497
  102.4 1.9 %collective-permute-start.9 = (bf16[32,1408]{1,0:T(8,128)(2,1)S(1)}, bf16[32,1408]{1,0:T(8,128)(2,1)S(1)}, u32[]{:S(2)}, u32[]{:S(2)}) collective-permute-start(bf16[32,1408]{1,0:T(8,128)(2,1)S(1)} %get-tuple-element.44), channel_id=1, source_target_pairs={{0,384},{32,416},{64,448},{96,480},{128,256},{160,288},{192,320},{... | collective-permute-start | bytes 270344 | tf_op jit(solution)/shard_map/ppermute | solution.py:497
  104.4 0.6 collective-permute-done.8.refs_2_
  105.0 4.2 %collective-permute-done.9.refs_3_ = bf16[32,1408]{1,0:T(8,128)(2,1)S(1)} collective-permute-done((bf16[32,1408]{1,0:T(8,128)(2,1)S(1)}, bf16[32,1408]{1,0:T(8,128)(2,1)S(1)}, u32[]{:S(2)}, u32[]{:S(2)}) %collective-permute-start.9) | collective-permute-done | bytes 90144 | tf_op jit(solution)/shard_map/ppermute | solution.py:497
  109.2 2.2 %shard_map.86 = bf16[32,5120]{1,0:T(8,128)(2,1)} custom-call(bf16[32,2,5248]{2,1,0:T(2,128)(2,1)S(1)} %all-to-all-done.1.got_ref, bf16[48,5248]{1,0:T(8,128)(2,1)S(1)} %get-tuple-element.35.own_ref, f32[128,128]{1,0:T(8,128)S(1)} %get-tuple-element.26.where_ref, bf16[32,1408]{1,0:T(8,128)(2,1)S(1)} %get-tuple-element.41.refs_0_, ...), custom_call_target="tpu_custom_call" | custom-call | flops 100000000 | bytes 4194304 | tf_op jit(solution)/shard_map/pallas_call | solution.py:397
  (17 shorter events, 0.1 us)
Async XLA Ops:
  0.0 60.9 %copy-start = (bf16[48,16,1024]{2,1,0:T(8,128)(2,1)S(1)}, bf16[48,16,1024]{2,1,0:T(8,128)(2,1)}, u32[]{:S(2)}) copy-start(bf16[48,16,1024]{2,1,0:T(8,128)(2,1)} %k_ref.1) | copy-start | bytes 4718596
  3.1 57.7 %all-to-all-start = ((bf16[32,2,6272]{2,1,0:T(2,128)(2,1)}), bf16[32,2,6272]{2,1,0:T(2,128)(2,1)S(1)}, u32[]{:S(2)}, u32[]{:S(2)}) async-start(bf16[32,2,6272]{2,1,0:T(2,128)(2,1)} %get-tuple-element.25), calls=%async_computation | async-start | bytes 1605632 | tf_op jit(solution)/shard_map/all_to_all | solution.py:499
  21.4 9.7 %collective-permute-start = (bf16[32,1280]{1,0:T(8,128)(2,1)S(1)}, bf16[32,1280]{1,0:T(8,128)(2,1)S(1)}, u32[]{:S(2)}, u32[]{:S(2)}) collective-permute-start(bf16[32,1280]{1,0:T(8,128)(2,1)S(1)} %get-tuple-element.29), channel_id=1, source_target_pairs={{0,128},{32,160},{64,192},{96,224},{128,0},{160,32},{192,64},{224,... | collective-permute-start | bytes 245768 | tf_op jit(solution)/shard_map/ppermute | solution.py:497
  24.6 7.1 %collective-permute-start.1 = (bf16[32,1280]{1,0:T(8,128)(2,1)S(1)}, bf16[32,1280]{1,0:T(8,128)(2,1)S(1)}, u32[]{:S(2)}, u32[]{:S(2)}) collective-permute-start(bf16[32,1280]{1,0:T(8,128)(2,1)S(1)} %get-tuple-element.30), channel_id=1, source_target_pairs={{0,256},{32,288},{64,320},{96,352},{128,384},{160,416},{192,448},{... | collective-permute-start | bytes 245768 | tf_op jit(solution)/shard_map/ppermute | solution.py:497
  29.1 6.7 %collective-permute-start.2 = (bf16[32,1280]{1,0:T(8,128)(2,1)S(1)}, bf16[32,1280]{1,0:T(8,128)(2,1)S(1)}, u32[]{:S(2)}, u32[]{:S(2)}) collective-permute-start(bf16[32,1280]{1,0:T(8,128)(2,1)S(1)} %get-tuple-element.31), channel_id=1, source_target_pairs={{0,384},{32,416},{64,448},{96,480},{128,256},{160,288},{192,320},{... | collective-permute-start | bytes 245768 | tf_op jit(solution)/shard_map/ppermute | solution.py:497
  31.1 0.6 copy-start.1
  31.7 0.6 copy-start.3
  35.8 0.6 copy-start.5
  64.4 28.2 %copy-start.2 = (bf16[32,1280]{1,0:T(8,128)(2,1)S(1)}, bf16[32,1280]{1,0:T(8,128)(2,1)}, u32[]{:S(2)}) copy-start(bf16[32,1280]{1,0:T(8,128)(2,1)} %copy-done.1) | copy-start | bytes 245764
  64.4 28.2 %copy-start.4 = (bf16[32,1280]{1,0:T(8,128)(2,1)S(1)}, bf16[32,1280]{1,0:T(8,128)(2,1)}, u32[]{:S(2)}) copy-start(bf16[32,1280]{1,0:T(8,128)(2,1)} %copy-done.3) | copy-start | bytes 245764
  64.4 28.1 %copy-start.6 = (bf16[32,1280]{1,0:T(8,128)(2,1)S(1)}, bf16[32,1280]{1,0:T(8,128)(2,1)}, u32[]{:S(2)}) copy-start(bf16[32,1280]{1,0:T(8,128)(2,1)} %copy-done.5) | copy-start | bytes 245764
  64.4 44.8 %all-to-all-start.1 = ((bf16[32,2,5248]{2,1,0:T(2,128)(2,1)}), bf16[32,2,5248]{2,1,0:T(2,128)(2,1)S(1)}, u32[]{:S(2)}, u32[]{:S(2)}) async-start(bf16[32,2,5248]{2,1,0:T(2,128)(2,1)} %get-tuple-element.33), calls=%async_computation.1 | async-start | bytes 1343488 | tf_op jit(solution)/shard_map/all_to_all | solution.py:499
  72.3 9.4 %collective-permute-start.3 = (bf16[256,256]{1,0:T(8,128)(2,1)S(1)}, bf16[256,256]{1,0:T(8,128)(2,1)S(1)}, u32[]{:S(2)}, u32[]{:S(2)}) collective-permute-start(bf16[256,256]{1,0:T(8,128)(2,1)S(1)} %reshape.11), channel_id=1, source_target_pairs={{0,64},{32,96},{64,0},{96,32},{128,192},{160,224},{192,128},{224,1... | collective-permute-start | bytes 393224 | tf_op jit(solution)/shard_map/ppermute | solution.py:497
  76.7 8.0 %collective-permute-start.4 = (bf16[256,256]{1,0:T(8,128)(2,1)S(1)}, bf16[256,256]{1,0:T(8,128)(2,1)S(1)}, u32[]{:S(2)}, u32[]{:S(2)}) collective-permute-start(bf16[256,256]{1,0:T(8,128)(2,1)S(1)} %reshape.11), channel_id=1, source_target_pairs={{0,16},{1,17},{2,18},{3,19},{4,20},{5,21},{6,22},{7,23},{8,24},{9,... | collective-permute-start | bytes 393224 | tf_op jit(solution)/shard_map/ppermute | solution.py:513
  79.3 7.2 %collective-permute-start.5 = (bf16[256,256]{1,0:T(8,128)(2,1)S(1)}, bf16[256,256]{1,0:T(8,128)(2,1)S(1)}, u32[]{:S(2)}, u32[]{:S(2)}) collective-permute-start(bf16[256,256]{1,0:T(8,128)(2,1)S(1)} %reshape.11), channel_id=1, source_target_pairs={{0,80},{1,81},{2,82},{3,83},{4,84},{5,85},{6,86},{7,87},{8,88},{9,... | collective-permute-start | bytes 393224 | tf_op jit(solution)/shard_map/ppermute | solution.py:513
  86.5 6.0 %collective-permute-start.6 = (bf16[1024,256]{1,0:T(8,128)(2,1)S(1)}, bf16[1024,256]{1,0:T(8,128)(2,1)S(1)}, u32[]{:S(2)}, u32[]{:S(2)}) collective-permute-start(bf16[1024,256]{1,0:T(8,128)(2,1)S(1)} %constant_dynamic-update-slice_fusion.kv_mine), channel_id=1, source_target_pairs={{0,32},{32,0},{64,96},{96,64},{128,160},{160,128},{192,224},{224,1... | collective-permute-start | bytes 1572872 | tf_op jit(solution)/shard_map/ppermute | solution.py:497
  94.7 9.7 %collective-permute-start.7 = (bf16[32,1408]{1,0:T(8,128)(2,1)S(1)}, bf16[32,1408]{1,0:T(8,128)(2,1)S(1)}, u32[]{:S(2)}, u32[]{:S(2)}) collective-permute-start(bf16[32,1408]{1,0:T(8,128)(2,1)S(1)} %get-tuple-element.42), channel_id=1, source_target_pairs={{0,128},{32,160},{64,192},{96,224},{128,0},{160,32},{192,64},{224,... | collective-permute-start | bytes 270344 | tf_op jit(solution)/shard_map/ppermute | solution.py:497
  97.9 7.1 %collective-permute-start.8 = (bf16[32,1408]{1,0:T(8,128)(2,1)S(1)}, bf16[32,1408]{1,0:T(8,128)(2,1)S(1)}, u32[]{:S(2)}, u32[]{:S(2)}) collective-permute-start(bf16[32,1408]{1,0:T(8,128)(2,1)S(1)} %get-tuple-element.43), channel_id=1, source_target_pairs={{0,256},{32,288},{64,320},{96,352},{128,384},{160,416},{192,448},{... | collective-permute-start | bytes 270344 | tf_op jit(solution)/shard_map/ppermute | solution.py:497
  102.4 6.8 %collective-permute-start.9 = (bf16[32,1408]{1,0:T(8,128)(2,1)S(1)}, bf16[32,1408]{1,0:T(8,128)(2,1)S(1)}, u32[]{:S(2)}, u32[]{:S(2)}) collective-permute-start(bf16[32,1408]{1,0:T(8,128)(2,1)S(1)} %get-tuple-element.44), channel_id=1, source_target_pairs={{0,384},{32,416},{64,448},{96,480},{128,256},{160,288},{192,320},{... | collective-permute-start | bytes 270344 | tf_op jit(solution)/shard_map/ppermute | solution.py:497

commit v10 on v9

--- a/solution.py
+++ b/solution.py
@@ -97,7 +97,7 @@
     shape = (cells, depth)
     cell = iota(shape, 0)
     each = depth // 4 // CAP
-    first = depth // 2 * lax.rem(lax.div(group, 2), 2) + depth // 4 * lax.div(cell, cells // 2)
+    first = depth // 2 * lax.rem(lax.div(group, 2), 2) + depth // 4 * (1 - lax.div(cell, cells // 2))
     for p in range(each):
         one = iota(shape, 1) == first + each * lax.rem(cell, CAP) + p
         rows = dot(jnp.where(one, 1.0, 0.0).astype(BF16), rows_ref[...]).astype(BF16)
@@ -133,7 +133,7 @@
     below = jnp.where(iota((entries, entries), 1) < iota((entries, entries), 0), 1.0, 0.0)
     before = dot(below.astype(BF16), member.astype(BF16))
     rank = jnp.sum(before * member, axis=1, keepdims=True)
-    where = jnp.where(remote > 0.0, holder * CAP + rank, cells + slot)
+    where = jnp.where(remote > 0.0, (devices - 1 - holder) * CAP + rank, cells + slot)
     where = jnp.where(used, where, -1.0)
     where_ref[...] = jnp.where(lane < TOKENS_AT, where, tokens)
     pick = jnp.where(where == lane, 1.0, 0.0).T[:cells]
@@ -496,7 +496,10 @@
     )
     flip = lambda x, bits: lax.ppermute(x, "grp", [(i, i ^ bits) for i in range(group)])
     turned = lambda xs: [flip(x, 4 * o) if o else x for o, x in enumerate(xs)]
-    exchange = lambda x: lax.all_to_all(x, "blk", split_axis=0, concat_axis=0, tiled=True)
+    descending = [list(range(devices))[::-1]]
+    exchange = lambda x: lax.all_to_all(
+        x, "blk", split_axis=0, concat_axis=0, tiled=True, axis_index_groups=descending
+    )
     got = exchange(send)
     local, *asked = home(queries, where, pool)
     asked = turned(asked)

time: 112 us -> 111 us (level)
  waiting for transfers between devices: 39 us -> 31.7 us
  starting transfers between devices: 57.9 us -> 64.3 us
    all_to_all x2, starting transfers between devices: 24.7 us -> 31.5 us  [body(): lax.all_to_all(x, 'blk', split_axis=0, concat_axis=0, tiled=True, axis_in...]
    all_to_all x2, waiting for transfers between devices: 24.4 us -> 18.1 us  [body(): lax.all_to_all(x, 'blk', split_axis=0, concat_axis=0, tiled=True, axis_in...]
  transfers between devices with their start and end apart: 12 -> 12, of which waited for: 7 -> 8; matrix products, arithmetic and copies ran while one was open for 0% -> 0% of each run, Pallas kernels for 3% -> 3%
where the time goes in v10:
time: 111 us
  starting transfers between devices  64.3 us (58%)
  waiting for transfers between devices  31.7 us (29%)
  Pallas kernels  12.2 us (11%)
  local copies, waits for them, and re-layouts  2.09 us (2%)
    all_to_all x2, starting transfers between devices, body(): lax.all_to_all(x, 'blk', split_axis=0, concat_axis=0, tiled=True, axis_in...  31.5 us
    ppermute x8, starting transfers between devices, body(): lax.ppermute(x, 'grp', [(i, i ^ bits) for i in range(group)])  28.5 us
    all_to_all x2, waiting for transfers between devices, body(): lax.all_to_all(x, 'blk', split_axis=0, concat_axis=0, tiled=True, axis_in...  18.1 us
    pallas_call x5, Pallas kernels, call(): pl.pallas_call(kernel, out_shape=[jax.ShapeDtypeStruct(s, d) for s, d in...  12.2 us
    ppermute x8, waiting for transfers between devices, body(): lax.ppermute(x, 'grp', [(i, i ^ bits) for i in range(group)])  9.25 us
    ppermute x1, starting transfers between devices, body(): lax.ppermute(part, ('grp', 'blk'), both)  2.44 us
    ppermute x1, waiting for transfers between devices, body(): lax.ppermute(part, 'blk', pairs)  2.25 us
  transfers between devices with their start and end apart: 12, of which 8 were waited for; matrix products, arithmetic and copies ran while one was open for 0% of the time, Pallas kernels for 3%

profile of v10, /device:TPU:1, one launch (start us, length us, event | category | flops | bytes accessed | tf_op | source)
XLA Modules:
  0.0 110.6 jit_solution(15351125524627668890)
XLA Ops:
  0.0 3.1 %shard_map.82 = (bf16[32,2,6272]{2,1,0:T(2,128)(2,1)}, f32[128,128]{1,0:T(8,128)S(1)}) custom-call(bf16[32,5120]{1,0:T(8,128)(2,1)} %q_hbm.3, s32[4,32]{1,0:T(4,128)} %bitcast.4, s32[1,32]{1,0:T(1,128)} %bitcast.5, s32[12,128]{1,0:T(8,128)} %bitcast.3, bf16[32,1024]{1,0:T(8,128)(2,1)} %pk_hbm.1, bf16[32,1024]{1,0:T(8,128)(2,1)} %pv_hbm.1), custom_call_target="tpu_custom_call" | custom-call | flops 100000000 | bytes 4194304 | tf_op jit(solution)/shard_map/pallas_call | solution.py:397
  3.1 17.1 %all-to-all-start = ((bf16[32,2,6272]{2,1,0:T(2,128)(2,1)}), bf16[32,2,6272]{2,1,0:T(2,128)(2,1)S(1)}, u32[]{:S(2)}, u32[]{:S(2)}) async-start(bf16[32,2,6272]{2,1,0:T(2,128)(2,1)} %get-tuple-element.25), calls=%async_computation | async-start | bytes 1605632 | tf_op jit(solution)/shard_map/all_to_all | solution.py:500
  20.3 1.3 %shard_map.83 = (bf16[48,5248]{1,0:T(8,128)(2,1)S(1)}, bf16[32,1280]{1,0:T(8,128)(2,1)S(1)}, bf16[32,1280]{1,0:T(8,128)(2,1)S(1)}, bf16[32,1280]{1,0:T(8,128)(2,1)S(1)}, bf16[32,1280]{1,0:T(8,128)(2,1)S(1)}) custom-call(bf16[32,5120]{1,0:T(8,128)(2,1)} %q_hbm.3, f32[128,128]{1,0:T(8,128)S(1)} %get-tuple-element.26.where_ref), custom_call_target="tpu_custom_call" | custom-call | flops 100000000 | bytes 4194304 | tf_op jit(solution)/shard_map/pallas_call | solution.py:397
  21.5 3.2 %collective-permute-start = (bf16[32,1280]{1,0:T(8,128)(2,1)S(1)}, bf16[32,1280]{1,0:T(8,128)(2,1)S(1)}, u32[]{:S(2)}, u32[]{:S(2)}) collective-permute-start(bf16[32,1280]{1,0:T(8,128)(2,1)S(1)} %get-tuple-element.29), channel_id=1, source_target_pairs={{0,128},{32,160},{64,192},{96,224},{128,0},{160,32},{192,64},{224,... | collective-permute-start | bytes 245768 | tf_op jit(solution)/shard_map/ppermute | solution.py:497
  24.7 4.5 %collective-permute-start.1 = (bf16[32,1280]{1,0:T(8,128)(2,1)S(1)}, bf16[32,1280]{1,0:T(8,128)(2,1)S(1)}, u32[]{:S(2)}, u32[]{:S(2)}) collective-permute-start(bf16[32,1280]{1,0:T(8,128)(2,1)S(1)} %get-tuple-element.30), channel_id=1, source_target_pairs={{0,256},{32,288},{64,320},{96,352},{128,384},{160,416},{192,448},{... | collective-permute-start | bytes 245768 | tf_op jit(solution)/shard_map/ppermute | solution.py:497
  29.3 1.9 %collective-permute-start.2 = (bf16[32,1280]{1,0:T(8,128)(2,1)S(1)}, bf16[32,1280]{1,0:T(8,128)(2,1)S(1)}, u32[]{:S(2)}, u32[]{:S(2)}) collective-permute-start(bf16[32,1280]{1,0:T(8,128)(2,1)S(1)} %get-tuple-element.31), channel_id=1, source_target_pairs={{0,384},{32,416},{64,448},{96,480},{128,256},{160,288},{192,320},{... | collective-permute-start | bytes 245768 | tf_op jit(solution)/shard_map/ppermute | solution.py:497
  31.2 0.0 copy-start.1
  31.2 0.6 copy-done.1
  31.9 0.2 collective-permute-done.1.q2
  32.0 0.6 copy-done.3
  32.7 3.0 %collective-permute-done.2.q3 = bf16[32,1280]{1,0:T(8,128)(2,1)S(1)} collective-permute-done((bf16[32,1280]{1,0:T(8,128)(2,1)S(1)}, bf16[32,1280]{1,0:T(8,128)(2,1)S(1)}, u32[]{:S(2)}, u32[]{:S(2)}) %collective-permute-start.2) | collective-permute-done | bytes 81952 | tf_op jit(solution)/shard_map/ppermute | solution.py:497
  35.7 0.6 copy-done.5
  36.3 18.1 %all-to-all-done.got_ref = bf16[32,2,6272]{2,1,0:T(2,128)(2,1)S(1)} async-done(((bf16[32,2,6272]{2,1,0:T(2,128)(2,1)}), bf16[32,2,6272]{2,1,0:T(2,128)(2,1)S(1)}, u32[]{:S(2)}, u32[]{:S(2)}) %all-to-all-start) | async-done | bytes 802848 | tf_op jit(solution)/shard_map/all_to_all | solution.py:500
  54.4 3.5 %shard_map.84 = (bf16[32,2,5248]{2,1,0:T(2,128)(2,1)}, bf16[48,5248]{1,0:T(8,128)(2,1)S(1)}) custom-call(bf16[32,2,6272]{2,1,0:T(2,128)(2,1)S(1)} %all-to-all-done.got_ref, bf16[48,5248]{1,0:T(8,128)(2,1)S(1)} %get-tuple-element.32.local_ref, bf16[48,16,1024]{2,1,0:T(8,128)(2,1)S(1)} %copy-done, bf16[48,16,1024]{2,1,0:T(8,128)(2,1)} %v_hbm.1), custom_call_target="tpu_custom_call" | custom-call | flops 1000000000 | bytes 4194304 | tf_op jit(solution)/shard_map/pallas_call | solution.py:397
  57.9 0.0 copy-start.2
  57.9 14.4 %all-to-all-start.1 = ((bf16[32,2,5248]{2,1,0:T(2,128)(2,1)}), bf16[32,2,5248]{2,1,0:T(2,128)(2,1)S(1)}, u32[]{:S(2)}, u32[]{:S(2)}) async-start(bf16[32,2,5248]{2,1,0:T(2,128)(2,1)} %get-tuple-element.33), calls=%async_computation.1 | async-start | bytes 1343488 | tf_op jit(solution)/shard_map/all_to_all | solution.py:500
  72.3 0.1 slice.4
  72.4 0.1 reshape.11
  72.5 4.6 %collective-permute-start.3 = (bf16[256,256]{1,0:T(8,128)(2,1)S(1)}, bf16[256,256]{1,0:T(8,128)(2,1)S(1)}, u32[]{:S(2)}, u32[]{:S(2)}) collective-permute-start(bf16[256,256]{1,0:T(8,128)(2,1)S(1)} %reshape.11), channel_id=1, source_target_pairs={{0,64},{32,96},{64,0},{96,32},{128,192},{160,224},{192,128},{224,1... | collective-permute-start | bytes 393224 | tf_op jit(solution)/shard_map/ppermute | solution.py:497
  77.1 1.9 %collective-permute-start.4 = (bf16[256,256]{1,0:T(8,128)(2,1)S(1)}, bf16[256,256]{1,0:T(8,128)(2,1)S(1)}, u32[]{:S(2)}, u32[]{:S(2)}) collective-permute-start(bf16[256,256]{1,0:T(8,128)(2,1)S(1)} %reshape.11), channel_id=1, source_target_pairs={{0,16},{1,17},{2,18},{3,19},{4,20},{5,21},{6,22},{7,23},{8,24},{9,... | collective-permute-start | bytes 393224 | tf_op jit(solution)/shard_map/ppermute | solution.py:516
  79.1 2.4 %collective-permute-start.5 = (bf16[256,256]{1,0:T(8,128)(2,1)S(1)}, bf16[256,256]{1,0:T(8,128)(2,1)S(1)}, u32[]{:S(2)}, u32[]{:S(2)}) collective-permute-start(bf16[256,256]{1,0:T(8,128)(2,1)S(1)} %reshape.11), channel_id=1, source_target_pairs={{0,80},{1,81},{2,82},{3,83},{4,84},{5,85},{6,86},{7,87},{8,88},{9,... | collective-permute-start | bytes 393224 | tf_op jit(solution)/shard_map/ppermute | solution.py:516
  81.5 2.3 %collective-permute-done.4 = bf16[256,256]{1,0:T(8,128)(2,1)S(1)} collective-permute-done((bf16[256,256]{1,0:T(8,128)(2,1)S(1)}, bf16[256,256]{1,0:T(8,128)(2,1)S(1)}, u32[]{:S(2)}, u32[]{:S(2)}) %collective-permute-start.4) | collective-permute-done | bytes 131104 | tf_op jit(solution)/shard_map/ppermute | solution.py:516
  83.8 2.2 %collective-permute-done.5 = bf16[256,256]{1,0:T(8,128)(2,1)S(1)} collective-permute-done((bf16[256,256]{1,0:T(8,128)(2,1)S(1)}, bf16[256,256]{1,0:T(8,128)(2,1)S(1)}, u32[]{:S(2)}, u32[]{:S(2)}) %collective-permute-start.5) | collective-permute-done | bytes 131104 | tf_op jit(solution)/shard_map/ppermute | solution.py:516
  86.0 4.5 %collective-permute-start.6 = (bf16[1024,256]{1,0:T(8,128)(2,1)S(1)}, bf16[1024,256]{1,0:T(8,128)(2,1)S(1)}, u32[]{:S(2)}, u32[]{:S(2)}) collective-permute-start(bf16[1024,256]{1,0:T(8,128)(2,1)S(1)} %constant_dynamic-update-slice_fusion.kv_mine), channel_id=1, source_target_pairs={{0,32},{32,0},{64,96},{96,64},{128,160},{160,128},{192,224},{224,1... | collective-permute-start | bytes 1572872 | tf_op jit(solution)/shard_map/ppermute | solution.py:497
  90.5 1.5 %collective-permute-done.6.kv_other = bf16[1024,256]{1,0:T(8,128)(2,1)S(1)} collective-permute-done((bf16[1024,256]{1,0:T(8,128)(2,1)S(1)}, bf16[1024,256]{1,0:T(8,128)(2,1)S(1)}, u32[]{:S(2)}, u32[]{:S(2)}) %collective-permute-start.6) | collective-permute-done | bytes 524320 | tf_op jit(solution)/shard_map/ppermute | solution.py:497
  92.1 2.1 %shard_map.85 = (bf16[32,1408]{1,0:T(8,128)(2,1)S(1)}, bf16[32,1408]{1,0:T(8,128)(2,1)S(1)}, bf16[32,1408]{1,0:T(8,128)(2,1)S(1)}, bf16[32,1408]{1,0:T(8,128)(2,1)S(1)}) custom-call(bf16[32,1280]{1,0:T(8,128)(2,1)S(1)} %get-tuple-element.36.q0, bf16[32,1280]{1,0:T(8,128)(2,1)S(1)} %copy-done.2, bf16[32,1280]{1,0:T(8,128)(2,1)S(1)} %copy-done.4, ...), custom_call_target="tpu_custom_call" | custom-call | flops 1000000000 | bytes 4194304 | tf_op jit(solution)/shard_map/pallas_call | solution.py:397
  94.2 3.2 %collective-permute-start.7 = (bf16[32,1408]{1,0:T(8,128)(2,1)S(1)}, bf16[32,1408]{1,0:T(8,128)(2,1)S(1)}, u32[]{:S(2)}, u32[]{:S(2)}) collective-permute-start(bf16[32,1408]{1,0:T(8,128)(2,1)S(1)} %get-tuple-element.42), channel_id=1, source_target_pairs={{0,128},{32,160},{64,192},{96,224},{128,0},{160,32},{192,64},{224,... | collective-permute-start | bytes 270344 | tf_op jit(solution)/shard_map/ppermute | solution.py:497
  97.4 4.5 %collective-permute-start.8 = (bf16[32,1408]{1,0:T(8,128)(2,1)S(1)}, bf16[32,1408]{1,0:T(8,128)(2,1)S(1)}, u32[]{:S(2)}, u32[]{:S(2)}) collective-permute-start(bf16[32,1408]{1,0:T(8,128)(2,1)S(1)} %get-tuple-element.43), channel_id=1, source_target_pairs={{0,256},{32,288},{64,320},{96,352},{128,384},{160,416},{192,448},{... | collective-permute-start | bytes 270344 | tf_op jit(solution)/shard_map/ppermute | solution.py:497
  101.9 1.9 %collective-permute-start.9 = (bf16[32,1408]{1,0:T(8,128)(2,1)S(1)}, bf16[32,1408]{1,0:T(8,128)(2,1)S(1)}, u32[]{:S(2)}, u32[]{:S(2)}) collective-permute-start(bf16[32,1408]{1,0:T(8,128)(2,1)S(1)} %get-tuple-element.44), channel_id=1, source_target_pairs={{0,384},{32,416},{64,448},{96,480},{128,256},{160,288},{192,320},{... | collective-permute-start | bytes 270344 | tf_op jit(solution)/shard_map/ppermute | solution.py:497
  103.9 0.6 collective-permute-done.8.refs_2_
  104.5 3.9 %collective-permute-done.9.refs_3_ = bf16[32,1408]{1,0:T(8,128)(2,1)S(1)} collective-permute-done((bf16[32,1408]{1,0:T(8,128)(2,1)S(1)}, bf16[32,1408]{1,0:T(8,128)(2,1)S(1)}, u32[]{:S(2)}, u32[]{:S(2)}) %collective-permute-start.9) | collective-permute-done | bytes 90144 | tf_op jit(solution)/shard_map/ppermute | solution.py:497
  108.4 2.2 %shard_map.86 = bf16[32,5120]{1,0:T(8,128)(2,1)} custom-call(bf16[32,2,5248]{2,1,0:T(2,128)(2,1)S(1)} %all-to-all-done.1.got_ref, bf16[48,5248]{1,0:T(8,128)(2,1)S(1)} %get-tuple-element.35.own_ref, f32[128,128]{1,0:T(8,128)S(1)} %get-tuple-element.26.where_ref, bf16[32,1408]{1,0:T(8,128)(2,1)S(1)} %get-tuple-element.41.refs_0_, ...), custom_call_target="tpu_custom_call" | custom-call | flops 100000000 | bytes 4194304 | tf_op jit(solution)/shard_map/pallas_call | solution.py:397
  (17 shorter events, 0.1 us)
Async XLA Ops:
  0.0 54.4 %copy-start = (bf16[48,16,1024]{2,1,0:T(8,128)(2,1)S(1)}, bf16[48,16,1024]{2,1,0:T(8,128)(2,1)}, u32[]{:S(2)}) copy-start(bf16[48,16,1024]{2,1,0:T(8,128)(2,1)} %k_ref.1) | copy-start | bytes 4718596
  3.1 51.2 %all-to-all-start = ((bf16[32,2,6272]{2,1,0:T(2,128)(2,1)}), bf16[32,2,6272]{2,1,0:T(2,128)(2,1)S(1)}, u32[]{:S(2)}, u32[]{:S(2)}) async-start(bf16[32,2,6272]{2,1,0:T(2,128)(2,1)} %get-tuple-element.25), calls=%async_computation | async-start | bytes 1605632 | tf_op jit(solution)/shard_map/all_to_all | solution.py:500
  21.5 9.7 %collective-permute-start = (bf16[32,1280]{1,0:T(8,128)(2,1)S(1)}, bf16[32,1280]{1,0:T(8,128)(2,1)S(1)}, u32[]{:S(2)}, u32[]{:S(2)}) collective-permute-start(bf16[32,1280]{1,0:T(8,128)(2,1)S(1)} %get-tuple-element.29), channel_id=1, source_target_pairs={{0,128},{32,160},{64,192},{96,224},{128,0},{160,32},{192,64},{224,... | collective-permute-start | bytes 245768 | tf_op jit(solution)/shard_map/ppermute | solution.py:497
  24.7 7.3 %collective-permute-start.1 = (bf16[32,1280]{1,0:T(8,128)(2,1)S(1)}, bf16[32,1280]{1,0:T(8,128)(2,1)S(1)}, u32[]{:S(2)}, u32[]{:S(2)}) collective-permute-start(bf16[32,1280]{1,0:T(8,128)(2,1)S(1)} %get-tuple-element.30), channel_id=1, source_target_pairs={{0,256},{32,288},{64,320},{96,352},{128,384},{160,416},{192,448},{... | collective-permute-start | bytes 245768 | tf_op jit(solution)/shard_map/ppermute | solution.py:497
  29.3 6.4 %collective-permute-start.2 = (bf16[32,1280]{1,0:T(8,128)(2,1)S(1)}, bf16[32,1280]{1,0:T(8,128)(2,1)S(1)}, u32[]{:S(2)}, u32[]{:S(2)}) collective-permute-start(bf16[32,1280]{1,0:T(8,128)(2,1)S(1)} %get-tuple-element.31), channel_id=1, source_target_pairs={{0,384},{32,416},{64,448},{96,480},{128,256},{160,288},{192,320},{... | collective-permute-start | bytes 245768 | tf_op jit(solution)/shard_map/ppermute | solution.py:497
  31.2 0.6 copy-start.1
  32.0 0.6 copy-start.3
  35.7 0.6 copy-start.5
  57.9 34.2 %copy-start.2 = (bf16[32,1280]{1,0:T(8,128)(2,1)S(1)}, bf16[32,1280]{1,0:T(8,128)(2,1)}, u32[]{:S(2)}) copy-start(bf16[32,1280]{1,0:T(8,128)(2,1)} %copy-done.1) | copy-start | bytes 245764
  57.9 34.2 %copy-start.4 = (bf16[32,1280]{1,0:T(8,128)(2,1)S(1)}, bf16[32,1280]{1,0:T(8,128)(2,1)}, u32[]{:S(2)}) copy-start(bf16[32,1280]{1,0:T(8,128)(2,1)} %copy-done.3) | copy-start | bytes 245764
  57.9 34.2 %copy-start.6 = (bf16[32,1280]{1,0:T(8,128)(2,1)S(1)}, bf16[32,1280]{1,0:T(8,128)(2,1)}, u32[]{:S(2)}) copy-start(bf16[32,1280]{1,0:T(8,128)(2,1)} %copy-done.5) | copy-start | bytes 245764
  57.9 50.5 %all-to-all-start.1 = ((bf16[32,2,5248]{2,1,0:T(2,128)(2,1)}), bf16[32,2,5248]{2,1,0:T(2,128)(2,1)S(1)}, u32[]{:S(2)}, u32[]{:S(2)}) async-start(bf16[32,2,5248]{2,1,0:T(2,128)(2,1)} %get-tuple-element.33), calls=%async_computation.1 | async-start | bytes 1343488 | tf_op jit(solution)/shard_map/all_to_all | solution.py:500
  72.5 9.0 %collective-permute-start.3 = (bf16[256,256]{1,0:T(8,128)(2,1)S(1)}, bf16[256,256]{1,0:T(8,128)(2,1)S(1)}, u32[]{:S(2)}, u32[]{:S(2)}) collective-permute-start(bf16[256,256]{1,0:T(8,128)(2,1)S(1)} %reshape.11), channel_id=1, source_target_pairs={{0,64},{32,96},{64,0},{96,32},{128,192},{160,224},{192,128},{224,1... | collective-permute-start | bytes 393224 | tf_op jit(solution)/shard_map/ppermute | solution.py:497
  77.1 6.7 %collective-permute-start.4 = (bf16[256,256]{1,0:T(8,128)(2,1)S(1)}, bf16[256,256]{1,0:T(8,128)(2,1)S(1)}, u32[]{:S(2)}, u32[]{:S(2)}) collective-permute-start(bf16[256,256]{1,0:T(8,128)(2,1)S(1)} %reshape.11), channel_id=1, source_target_pairs={{0,16},{1,17},{2,18},{3,19},{4,20},{5,21},{6,22},{7,23},{8,24},{9,... | collective-permute-start | bytes 393224 | tf_op jit(solution)/shard_map/ppermute | solution.py:516
  79.1 6.9 %collective-permute-start.5 = (bf16[256,256]{1,0:T(8,128)(2,1)S(1)}, bf16[256,256]{1,0:T(8,128)(2,1)S(1)}, u32[]{:S(2)}, u32[]{:S(2)}) collective-permute-start(bf16[256,256]{1,0:T(8,128)(2,1)S(1)} %reshape.11), channel_id=1, source_target_pairs={{0,80},{1,81},{2,82},{3,83},{4,84},{5,85},{6,86},{7,87},{8,88},{9,... | collective-permute-start | bytes 393224 | tf_op jit(solution)/shard_map/ppermute | solution.py:516
  86.0 6.0 %collective-permute-start.6 = (bf16[1024,256]{1,0:T(8,128)(2,1)S(1)}, bf16[1024,256]{1,0:T(8,128)(2,1)S(1)}, u32[]{:S(2)}, u32[]{:S(2)}) collective-permute-start(bf16[1024,256]{1,0:T(8,128)(2,1)S(1)} %constant_dynamic-update-slice_fusion.kv_mine), channel_id=1, source_target_pairs={{0,32},{32,0},{64,96},{96,64},{128,160},{160,128},{192,224},{224,1... | collective-permute-start | bytes 1572872 | tf_op jit(solution)/shard_map/ppermute | solution.py:497
  94.2 9.7 %collective-permute-start.7 = (bf16[32,1408]{1,0:T(8,128)(2,1)S(1)}, bf16[32,1408]{1,0:T(8,128)(2,1)S(1)}, u32[]{:S(2)}, u32[]{:S(2)}) collective-permute-start(bf16[32,1408]{1,0:T(8,128)(2,1)S(1)} %get-tuple-element.42), channel_id=1, source_target_pairs={{0,128},{32,160},{64,192},{96,224},{128,0},{160,32},{192,64},{224,... | collective-permute-start | bytes 270344 | tf_op jit(solution)/shard_map/ppermute | solution.py:497
  97.4 7.1 %collective-permute-start.8 = (bf16[32,1408]{1,0:T(8,128)(2,1)S(1)}, bf16[32,1408]{1,0:T(8,128)(2,1)S(1)}, u32[]{:S(2)}, u32[]{:S(2)}) collective-permute-start(bf16[32,1408]{1,0:T(8,128)(2,1)S(1)} %get-tuple-element.43), channel_id=1, source_target_pairs={{0,256},{32,288},{64,320},{96,352},{128,384},{160,416},{192,448},{... | collective-permute-start | bytes 270344 | tf_op jit(solution)/shard_map/ppermute | solution.py:497
  101.9 6.5 %collective-permute-start.9 = (bf16[32,1408]{1,0:T(8,128)(2,1)S(1)}, bf16[32,1408]{1,0:T(8,128)(2,1)S(1)}, u32[]{:S(2)}, u32[]{:S(2)}) collective-permute-start(bf16[32,1408]{1,0:T(8,128)(2,1)S(1)} %get-tuple-element.44), channel_id=1, source_target_pairs={{0,384},{32,416},{64,448},{96,480},{128,256},{160,288},{192,320},{... | collective-permute-start | bytes 270344 | tf_op jit(solution)/shard_map/ppermute | solution.py:497

commit v11 on v10

--- a/solution.py
+++ b/solution.py
@@ -280,23 +280,27 @@
     answer_ref[:, :, QCOLS:ROW] = rows.reshape(devices, CAP, SIDE)
 
 
-def prefix_kernel(q0, q1, q2, q3, kv_mine, kv_other, o0, o1, o2, o3):
+def prefix_kernel(q0, q1, q2, q3, mine_a, mine_b, other_a, other_b, o0, o1, o2, o3):
     requests = q0.shape[0]
     rows = requests * SHARE
     step = 256
-    chunks = [slice(c, c + step) for c in range(0, kv_mine.shape[0], step)]
+    chunks = [
+        (i, slice(c, c + step))
+        for i, x in enumerate((mine_a, mine_b))
+        for c in range(0, x.shape[0], step)
+    ]
     core = lax.rem(lax.axis_index("grp"), 2)
     lane = iota((rows, SIDE), 1)
     asked = (q0, q1, q2, q3)
     outs = (o0, o1, o2, o3)
 
-    def attend(k_ref, v_ref):
+    def attend(k_refs, v_refs):
         sums = jnp.zeros((rows, SIDE), F32)
 
         def score(h):
             heads = jnp.concatenate([q[:, h * HD : (h + 1) * HD] for q in asked], axis=0)
             kv = slice(h // GROUP * HD, (h // GROUP + 1) * HD)
-            return [dot_t(heads, k_ref[c, kv]) for c in chunks]
+            return [dot_t(heads, k_refs[i][c, kv]) for i, c in chunks]
 
         def weigh(scores):
             top = jnp.max(functools.reduce(jnp.maximum, scores), axis=1, keepdims=True)
@@ -306,7 +310,7 @@
 
         def mix(h, weights, total):
             kv = slice(h // GROUP * HD, (h // GROUP + 1) * HD)
-            parts = [dot(w, v_ref[c, kv]) for c, w in zip(chunks, weights)]
+            parts = [dot(w, v_refs[i][c, kv]) for (i, c), w in zip(chunks, weights)]
             mixture = (functools.reduce(jnp.add, parts) / total).astype(BF16)
             for o, out in enumerate(outs):
                 out[:, h * HD : (h + 1) * HD] = mixture[requests * o : requests * (o + 1)]
@@ -328,11 +332,11 @@
 
     @pl.when(core == 0)
     def _():
-        attend(kv_mine, kv_other)
+        attend((mine_a, mine_b), (other_a, other_b))
 
     @pl.when(core == 1)
     def _():
-        attend(kv_other, kv_mine)
+        attend((other_a, other_b), (mine_a, mine_b))
 
 
 def join_kernel(got_ref, own_ref, where_ref, *refs):
@@ -461,10 +465,10 @@
     )
 
 
-def prefix(asked, kv_mine, kv_other):
+def prefix(asked, *kv):
     shape = (asked[0].shape[0], BLOCK + SIDE)
     return call(
-        prefix_kernel, [(shape, BF16)] * SHARE, 10**9, *asked, kv_mine, kv_other
+        prefix_kernel, [(shape, BF16)] * SHARE, 10**9, *asked, *kv
     )
 
 
@@ -515,8 +519,8 @@
     around = [
         flip(part, 2), lax.ppermute(part, "blk", pairs), lax.ppermute(part, ("grp", "blk"), both)
     ]
-    kv_mine = jnp.concatenate([part, *around], axis=0)
-    served = prefix(asked, kv_mine, flip(kv_mine, 1))
+    rest = jnp.concatenate(around, axis=0)
+    served = prefix(asked, part, rest, flip(part, 1), flip(rest, 1))
     return join(back, own, where, turned(served))
 
 

time: 111 us -> 113 us (1.018)
  starting transfers between devices: 64.3 us -> 66.3 us
    ppermute x8 -> x9, starting transfers between devices: 28.5 us -> 30.4 us  [body(): lax.ppermute(x, 'grp', [(i, i ^ bits) for i in range(group)])]
    ppermute x8 -> x9, waiting for transfers between devices: 9.25 us -> 8.52 us  [body(): lax.ppermute(x, 'grp', [(i, i ^ bits) for i in range(group)])]
  transfers between devices with their start and end apart: 12 -> 13, of which waited for: 8 -> 8; matrix products, arithmetic and copies ran while one was open for 0% -> 0% of each run, Pallas kernels for 3% -> 3%
where the time goes in v11:
time: 113 us; the launch traced here: 112 us
  starting transfers between devices  66.3 us (59%)
  waiting for transfers between devices  31 us (27%)
  Pallas kernels  12.2 us (11%)
  local copies, waits for them, and re-layouts  2.09 us (2%)
    all_to_all x2, starting transfers between devices, body(): lax.all_to_all(x, 'blk', split_axis=0, concat_axis=0, tiled=True, axis_in...  31.5 us
    ppermute x9, starting transfers between devices, body(): lax.ppermute(x, 'grp', [(i, i ^ bits) for i in range(group)])  30.4 us
    all_to_all x2, waiting for transfers between devices, body(): lax.all_to_all(x, 'blk', split_axis=0, concat_axis=0, tiled=True, axis_in...  18.1 us
    pallas_call x5, Pallas kernels, call(): pl.pallas_call(kernel, out_shape=[jax.ShapeDtypeStruct(s, d) for s, d in...  12.2 us
    ppermute x9, waiting for transfers between devices, body(): lax.ppermute(x, 'grp', [(i, i ^ bits) for i in range(group)])  8.52 us
    ppermute x1, starting transfers between devices, body(): lax.ppermute(part, ('grp', 'blk'), both)  2.44 us
    ppermute x1, waiting for transfers between devices, body(): lax.ppermute(part, 'blk', pairs)  2.28 us
  transfers between devices with their start and end apart: 13, of which 8 were waited for; matrix products, arithmetic and copies ran while one was open for 0% of the time, Pallas kernels for 3%

profile of v11, /device:TPU:1, one launch (start us, length us, event | category | flops | bytes accessed | tf_op | source)
XLA Modules:
  0.0 111.8 jit_solution(14424643286684262641)
XLA Ops:
  0.0 3.1 %shard_map.82 = (bf16[32,2,6272]{2,1,0:T(2,128)(2,1)}, f32[128,128]{1,0:T(8,128)S(1)}) custom-call(bf16[32,5120]{1,0:T(8,128)(2,1)} %q_hbm.3, s32[4,32]{1,0:T(4,128)} %bitcast.4, s32[1,32]{1,0:T(1,128)} %bitcast.5, s32[12,128]{1,0:T(8,128)} %bitcast.3, bf16[32,1024]{1,0:T(8,128)(2,1)} %pk_hbm.1, bf16[32,1024]{1,0:T(8,128)(2,1)} %pv_hbm.1), custom_call_target="tpu_custom_call" | custom-call | flops 100000000 | bytes 4194304 | tf_op jit(solution)/shard_map/pallas_call | solution.py:401
  3.2 17.1 %all-to-all-start = ((bf16[32,2,6272]{2,1,0:T(2,128)(2,1)}), bf16[32,2,6272]{2,1,0:T(2,128)(2,1)S(1)}, u32[]{:S(2)}, u32[]{:S(2)}) async-start(bf16[32,2,6272]{2,1,0:T(2,128)(2,1)} %get-tuple-element.25), calls=%async_computation | async-start | bytes 1605632 | tf_op jit(solution)/shard_map/all_to_all | solution.py:504
  20.3 1.3 %shard_map.83 = (bf16[48,5248]{1,0:T(8,128)(2,1)S(1)}, bf16[32,1280]{1,0:T(8,128)(2,1)S(1)}, bf16[32,1280]{1,0:T(8,128)(2,1)S(1)}, bf16[32,1280]{1,0:T(8,128)(2,1)S(1)}, bf16[32,1280]{1,0:T(8,128)(2,1)S(1)}) custom-call(bf16[32,5120]{1,0:T(8,128)(2,1)} %q_hbm.3, f32[128,128]{1,0:T(8,128)S(1)} %get-tuple-element.26.where_ref), custom_call_target="tpu_custom_call" | custom-call | flops 100000000 | bytes 4194304 | tf_op jit(solution)/shard_map/pallas_call | solution.py:401
  21.5 3.2 %collective-permute-start = (bf16[32,1280]{1,0:T(8,128)(2,1)S(1)}, bf16[32,1280]{1,0:T(8,128)(2,1)S(1)}, u32[]{:S(2)}, u32[]{:S(2)}) collective-permute-start(bf16[32,1280]{1,0:T(8,128)(2,1)S(1)} %get-tuple-element.29), channel_id=1, source_target_pairs={{0,128},{32,160},{64,192},{96,224},{128,0},{160,32},{192,64},{224,... | collective-permute-start | bytes 245768 | tf_op jit(solution)/shard_map/ppermute | solution.py:501
  24.8 4.5 %collective-permute-start.1 = (bf16[32,1280]{1,0:T(8,128)(2,1)S(1)}, bf16[32,1280]{1,0:T(8,128)(2,1)S(1)}, u32[]{:S(2)}, u32[]{:S(2)}) collective-permute-start(bf16[32,1280]{1,0:T(8,128)(2,1)S(1)} %get-tuple-element.30), channel_id=1, source_target_pairs={{0,256},{32,288},{64,320},{96,352},{128,384},{160,416},{192,448},{... | collective-permute-start | bytes 245768 | tf_op jit(solution)/shard_map/ppermute | solution.py:501
  29.3 1.9 %collective-permute-start.2 = (bf16[32,1280]{1,0:T(8,128)(2,1)S(1)}, bf16[32,1280]{1,0:T(8,128)(2,1)S(1)}, u32[]{:S(2)}, u32[]{:S(2)}) collective-permute-start(bf16[32,1280]{1,0:T(8,128)(2,1)S(1)} %get-tuple-element.31), channel_id=1, source_target_pairs={{0,384},{32,416},{64,448},{96,480},{128,256},{160,288},{192,320},{... | collective-permute-start | bytes 245768 | tf_op jit(solution)/shard_map/ppermute | solution.py:501
  31.2 0.0 copy-start.1
  31.2 0.6 copy-done.1
  31.9 0.2 collective-permute-done.1.q2
  32.1 0.6 copy-done.3
  32.7 3.0 %collective-permute-done.2.q3 = bf16[32,1280]{1,0:T(8,128)(2,1)S(1)} collective-permute-done((bf16[32,1280]{1,0:T(8,128)(2,1)S(1)}, bf16[32,1280]{1,0:T(8,128)(2,1)S(1)}, u32[]{:S(2)}, u32[]{:S(2)}) %collective-permute-start.2) | collective-permute-done | bytes 81952 | tf_op jit(solution)/shard_map/ppermute | solution.py:501
  35.7 0.6 copy-done.5
  36.3 18.1 %all-to-all-done.got_ref = bf16[32,2,6272]{2,1,0:T(2,128)(2,1)S(1)} async-done(((bf16[32,2,6272]{2,1,0:T(2,128)(2,1)}), bf16[32,2,6272]{2,1,0:T(2,128)(2,1)S(1)}, u32[]{:S(2)}, u32[]{:S(2)}) %all-to-all-start) | async-done | bytes 802848 | tf_op jit(solution)/shard_map/all_to_all | solution.py:504
  54.4 3.5 %shard_map.84 = (bf16[32,2,5248]{2,1,0:T(2,128)(2,1)}, bf16[48,5248]{1,0:T(8,128)(2,1)S(1)}) custom-call(bf16[32,2,6272]{2,1,0:T(2,128)(2,1)S(1)} %all-to-all-done.got_ref, bf16[48,5248]{1,0:T(8,128)(2,1)S(1)} %get-tuple-element.32.local_ref, bf16[48,16,1024]{2,1,0:T(8,128)(2,1)S(1)} %copy-done, bf16[48,16,1024]{2,1,0:T(8,128)(2,1)} %v_hbm.1), custom_call_target="tpu_custom_call" | custom-call | flops 1000000000 | bytes 4194304 | tf_op jit(solution)/shard_map/pallas_call | solution.py:401
  57.9 14.4 %all-to-all-start.1 = ((bf16[32,2,5248]{2,1,0:T(2,128)(2,1)}), bf16[32,2,5248]{2,1,0:T(2,128)(2,1)S(1)}, u32[]{:S(2)}, u32[]{:S(2)}) async-start(bf16[32,2,5248]{2,1,0:T(2,128)(2,1)} %get-tuple-element.33), calls=%async_computation.1 | async-start | bytes 1343488 | tf_op jit(solution)/shard_map/all_to_all | solution.py:504
  72.3 0.1 slice.4
  72.4 0.1 reshape.11.mine_a
  72.5 4.6 %collective-permute-start.3 = (bf16[256,256]{1,0:T(8,128)(2,1)S(1)}, bf16[256,256]{1,0:T(8,128)(2,1)S(1)}, u32[]{:S(2)}, u32[]{:S(2)}) collective-permute-start(bf16[256,256]{1,0:T(8,128)(2,1)S(1)} %reshape.11.mine_a), channel_id=1, source_target_pairs={{0,64},{32,96},{64,0},{96,32},{128,192},{160,224},{192,128},{224,1... | collective-permute-start | bytes 393224 | tf_op jit(solution)/shard_map/ppermute | solution.py:501
  77.1 1.9 %collective-permute-start.4 = (bf16[256,256]{1,0:T(8,128)(2,1)S(1)}, bf16[256,256]{1,0:T(8,128)(2,1)S(1)}, u32[]{:S(2)}, u32[]{:S(2)}) collective-permute-start(bf16[256,256]{1,0:T(8,128)(2,1)S(1)} %reshape.11.mine_a), channel_id=1, source_target_pairs={{0,16},{1,17},{2,18},{3,19},{4,20},{5,21},{6,22},{7,23},{8,24},{9,... | collective-permute-start | bytes 393224 | tf_op jit(solution)/shard_map/ppermute | solution.py:520
  79.1 2.4 %collective-permute-start.5 = (bf16[256,256]{1,0:T(8,128)(2,1)S(1)}, bf16[256,256]{1,0:T(8,128)(2,1)S(1)}, u32[]{:S(2)}, u32[]{:S(2)}) collective-permute-start(bf16[256,256]{1,0:T(8,128)(2,1)S(1)} %reshape.11.mine_a), channel_id=1, source_target_pairs={{0,80},{1,81},{2,82},{3,83},{4,84},{5,85},{6,86},{7,87},{8,88},{9,... | collective-permute-start | bytes 393224 | tf_op jit(solution)/shard_map/ppermute | solution.py:520
  81.5 2.3 %collective-permute-done.4 = bf16[256,256]{1,0:T(8,128)(2,1)S(1)} collective-permute-done((bf16[256,256]{1,0:T(8,128)(2,1)S(1)}, bf16[256,256]{1,0:T(8,128)(2,1)S(1)}, u32[]{:S(2)}, u32[]{:S(2)}) %collective-permute-start.4) | collective-permute-done | bytes 131104 | tf_op jit(solution)/shard_map/ppermute | solution.py:520
  83.8 2.2 %collective-permute-done.5 = bf16[256,256]{1,0:T(8,128)(2,1)S(1)} collective-permute-done((bf16[256,256]{1,0:T(8,128)(2,1)S(1)}, bf16[256,256]{1,0:T(8,128)(2,1)S(1)}, u32[]{:S(2)}, u32[]{:S(2)}) %collective-permute-start.5) | collective-permute-done | bytes 131104 | tf_op jit(solution)/shard_map/ppermute | solution.py:520
  86.0 4.5 %collective-permute-start.7 = (bf16[768,256]{1,0:T(8,128)(2,1)S(1)}, bf16[768,256]{1,0:T(8,128)(2,1)S(1)}, u32[]{:S(2)}, u32[]{:S(2)}) collective-permute-start(bf16[768,256]{1,0:T(8,128)(2,1)S(1)} %constant_dynamic-update-slice_fusion.mine_b), channel_id=1, source_target_pairs={{0,32},{32,0},{64,96},{96,64},{128,160},{160,128},{192,224},{224,1... | collective-permute-start | bytes 1179656 | tf_op jit(solution)/shard_map/ppermute | solution.py:501
  90.5 1.9 %collective-permute-start.6 = (bf16[256,256]{1,0:T(8,128)(2,1)S(1)}, bf16[256,256]{1,0:T(8,128)(2,1)S(1)}, u32[]{:S(2)}, u32[]{:S(2)}) collective-permute-start(bf16[256,256]{1,0:T(8,128)(2,1)S(1)} %reshape.11.mine_a), channel_id=1, source_target_pairs={{0,32},{32,0},{64,96},{96,64},{128,160},{160,128},{192,224},{224,1... | collective-permute-start | bytes 393224 | tf_op jit(solution)/shard_map/ppermute | solution.py:501
  92.5 1.3 %collective-permute-done.6.other_a = bf16[256,256]{1,0:T(8,128)(2,1)S(1)} collective-permute-done((bf16[256,256]{1,0:T(8,128)(2,1)S(1)}, bf16[256,256]{1,0:T(8,128)(2,1)S(1)}, u32[]{:S(2)}, u32[]{:S(2)}) %collective-permute-start.6) | collective-permute-done | bytes 131104 | tf_op jit(solution)/shard_map/ppermute | solution.py:501
  93.8 2.1 %shard_map.85 = (bf16[32,1408]{1,0:T(8,128)(2,1)S(1)}, bf16[32,1408]{1,0:T(8,128)(2,1)S(1)}, bf16[32,1408]{1,0:T(8,128)(2,1)S(1)}, bf16[32,1408]{1,0:T(8,128)(2,1)S(1)}) custom-call(bf16[32,1280]{1,0:T(8,128)(2,1)S(1)} %get-tuple-element.36.q0, bf16[32,1280]{1,0:T(8,128)(2,1)S(1)} %copy-done.2, bf16[32,1280]{1,0:T(8,128)(2,1)S(1)} %copy-done.4, ...), custom_call_target="tpu_custom_call" | custom-call | flops 1000000000 | bytes 4194304 | tf_op jit(solution)/shard_map/pallas_call | solution.py:401
  95.9 4.7 %collective-permute-start.10 = (bf16[32,1408]{1,0:T(8,128)(2,1)S(1)}, bf16[32,1408]{1,0:T(8,128)(2,1)S(1)}, u32[]{:S(2)}, u32[]{:S(2)}) collective-permute-start(bf16[32,1408]{1,0:T(8,128)(2,1)S(1)} %get-tuple-element.44), channel_id=1, source_target_pairs={{0,384},{32,416},{64,448},{96,480},{128,256},{160,288},{192,320},{... | collective-permute-start | bytes 270344 | tf_op jit(solution)/shard_map/ppermute | solution.py:501
  100.6 1.9 %collective-permute-start.8 = (bf16[32,1408]{1,0:T(8,128)(2,1)S(1)}, bf16[32,1408]{1,0:T(8,128)(2,1)S(1)}, u32[]{:S(2)}, u32[]{:S(2)}) collective-permute-start(bf16[32,1408]{1,0:T(8,128)(2,1)S(1)} %get-tuple-element.42), channel_id=1, source_target_pairs={{0,128},{32,160},{64,192},{96,224},{128,0},{160,32},{192,64},{224,... | collective-permute-start | bytes 270344 | tf_op jit(solution)/shard_map/ppermute | solution.py:501
  102.5 3.1 %collective-permute-start.9 = (bf16[32,1408]{1,0:T(8,128)(2,1)S(1)}, bf16[32,1408]{1,0:T(8,128)(2,1)S(1)}, u32[]{:S(2)}, u32[]{:S(2)}) collective-permute-start(bf16[32,1408]{1,0:T(8,128)(2,1)S(1)} %get-tuple-element.43), channel_id=1, source_target_pairs={{0,256},{32,288},{64,320},{96,352},{128,384},{160,416},{192,448},{... | collective-permute-start | bytes 270344 | tf_op jit(solution)/shard_map/ppermute | solution.py:501
  105.6 0.7 collective-permute-done.8.refs_1_
  106.3 3.3 %collective-permute-done.9.refs_2_ = bf16[32,1408]{1,0:T(8,128)(2,1)S(1)} collective-permute-done((bf16[32,1408]{1,0:T(8,128)(2,1)S(1)}, bf16[32,1408]{1,0:T(8,128)(2,1)S(1)}, u32[]{:S(2)}, u32[]{:S(2)}) %collective-permute-start.9) | collective-permute-done | bytes 90144 | tf_op jit(solution)/shard_map/ppermute | solution.py:501
  109.6 2.2 %shard_map.86 = bf16[32,5120]{1,0:T(8,128)(2,1)} custom-call(bf16[32,2,5248]{2,1,0:T(2,128)(2,1)S(1)} %all-to-all-done.1.got_ref, bf16[48,5248]{1,0:T(8,128)(2,1)S(1)} %get-tuple-element.35.own_ref, f32[128,128]{1,0:T(8,128)S(1)} %get-tuple-element.26.where_ref, bf16[32,1408]{1,0:T(8,128)(2,1)S(1)} %get-tuple-element.41.refs_0_, ...), custom_call_target="tpu_custom_call" | custom-call | flops 100000000 | bytes 4194304 | tf_op jit(solution)/shard_map/pallas_call | solution.py:401
  (18 shorter events, 0.1 us)
Async XLA Ops:
  0.0 54.4 %copy-start = (bf16[48,16,1024]{2,1,0:T(8,128)(2,1)S(1)}, bf16[48,16,1024]{2,1,0:T(8,128)(2,1)}, u32[]{:S(2)}) copy-start(bf16[48,16,1024]{2,1,0:T(8,128)(2,1)} %k_ref.1) | copy-start | bytes 4718596
  3.2 51.2 %all-to-all-start = ((bf16[32,2,6272]{2,1,0:T(2,128)(2,1)}), bf16[32,2,6272]{2,1,0:T(2,128)(2,1)S(1)}, u32[]{:S(2)}, u32[]{:S(2)}) async-start(bf16[32,2,6272]{2,1,0:T(2,128)(2,1)} %get-tuple-element.25), calls=%async_computation | async-start | bytes 1605632 | tf_op jit(solution)/shard_map/all_to_all | solution.py:504
  21.5 9.7 %collective-permute-start = (bf16[32,1280]{1,0:T(8,128)(2,1)S(1)}, bf16[32,1280]{1,0:T(8,128)(2,1)S(1)}, u32[]{:S(2)}, u32[]{:S(2)}) collective-permute-start(bf16[32,1280]{1,0:T(8,128)(2,1)S(1)} %get-tuple-element.29), channel_id=1, source_target_pairs={{0,128},{32,160},{64,192},{96,224},{128,0},{160,32},{192,64},{224,... | collective-permute-start | bytes 245768 | tf_op jit(solution)/shard_map/ppermute | solution.py:501
  24.8 7.3 %collective-permute-start.1 = (bf16[32,1280]{1,0:T(8,128)(2,1)S(1)}, bf16[32,1280]{1,0:T(8,128)(2,1)S(1)}, u32[]{:S(2)}, u32[]{:S(2)}) collective-permute-start(bf16[32,1280]{1,0:T(8,128)(2,1)S(1)} %get-tuple-element.30), channel_id=1, source_target_pairs={{0,256},{32,288},{64,320},{96,352},{128,384},{160,416},{192,448},{... | collective-permute-start | bytes 245768 | tf_op jit(solution)/shard_map/ppermute | solution.py:501
  29.3 6.4 %collective-permute-start.2 = (bf16[32,1280]{1,0:T(8,128)(2,1)S(1)}, bf16[32,1280]{1,0:T(8,128)(2,1)S(1)}, u32[]{:S(2)}, u32[]{:S(2)}) collective-permute-start(bf16[32,1280]{1,0:T(8,128)(2,1)S(1)} %get-tuple-element.31), channel_id=1, source_target_pairs={{0,384},{32,416},{64,448},{96,480},{128,256},{160,288},{192,320},{... | collective-permute-start | bytes 245768 | tf_op jit(solution)/shard_map/ppermute | solution.py:501
  31.2 0.6 copy-start.1
  32.1 0.6 copy-start.3
  35.7 0.6 copy-start.5
  57.9 35.9 %copy-start.2 = (bf16[32,1280]{1,0:T(8,128)(2,1)S(1)}, bf16[32,1280]{1,0:T(8,128)(2,1)}, u32[]{:S(2)}) copy-start(bf16[32,1280]{1,0:T(8,128)(2,1)} %copy-done.1) | copy-start | bytes 245764
  57.9 35.9 %copy-start.4 = (bf16[32,1280]{1,0:T(8,128)(2,1)S(1)}, bf16[32,1280]{1,0:T(8,128)(2,1)}, u32[]{:S(2)}) copy-start(bf16[32,1280]{1,0:T(8,128)(2,1)} %copy-done.3) | copy-start | bytes 245764
  57.9 35.9 %copy-start.6 = (bf16[32,1280]{1,0:T(8,128)(2,1)S(1)}, bf16[32,1280]{1,0:T(8,128)(2,1)}, u32[]{:S(2)}) copy-start(bf16[32,1280]{1,0:T(8,128)(2,1)} %copy-done.5) | copy-start | bytes 245764
  57.9 51.7 %all-to-all-start.1 = ((bf16[32,2,5248]{2,1,0:T(2,128)(2,1)}), bf16[32,2,5248]{2,1,0:T(2,128)(2,1)S(1)}, u32[]{:S(2)}, u32[]{:S(2)}) async-start(bf16[32,2,5248]{2,1,0:T(2,128)(2,1)} %get-tuple-element.33), calls=%async_computation.1 | async-start | bytes 1343488 | tf_op jit(solution)/shard_map/all_to_all | solution.py:504
  72.5 9.0 %collective-permute-start.3 = (bf16[256,256]{1,0:T(8,128)(2,1)S(1)}, bf16[256,256]{1,0:T(8,128)(2,1)S(1)}, u32[]{:S(2)}, u32[]{:S(2)}) collective-permute-start(bf16[256,256]{1,0:T(8,128)(2,1)S(1)} %reshape.11.mine_a), channel_id=1, source_target_pairs={{0,64},{32,96},{64,0},{96,32},{128,192},{160,224},{192,128},{224,1... | collective-permute-start | bytes 393224 | tf_op jit(solution)/shard_map/ppermute | solution.py:501
  77.1 6.7 %collective-permute-start.4 = (bf16[256,256]{1,0:T(8,128)(2,1)S(1)}, bf16[256,256]{1,0:T(8,128)(2,1)S(1)}, u32[]{:S(2)}, u32[]{:S(2)}) collective-permute-start(bf16[256,256]{1,0:T(8,128)(2,1)S(1)} %reshape.11.mine_a), channel_id=1, source_target_pairs={{0,16},{1,17},{2,18},{3,19},{4,20},{5,21},{6,22},{7,23},{8,24},{9,... | collective-permute-start | bytes 393224 | tf_op jit(solution)/shard_map/ppermute | solution.py:520
  79.1 6.9 %collective-permute-start.5 = (bf16[256,256]{1,0:T(8,128)(2,1)S(1)}, bf16[256,256]{1,0:T(8,128)(2,1)S(1)}, u32[]{:S(2)}, u32[]{:S(2)}) collective-permute-start(bf16[256,256]{1,0:T(8,128)(2,1)S(1)} %reshape.11.mine_a), channel_id=1, source_target_pairs={{0,80},{1,81},{2,82},{3,83},{4,84},{5,85},{6,86},{7,87},{8,88},{9,... | collective-permute-start | bytes 393224 | tf_op jit(solution)/shard_map/ppermute | solution.py:520
  86.0 7.8 %collective-permute-start.7 = (bf16[768,256]{1,0:T(8,128)(2,1)S(1)}, bf16[768,256]{1,0:T(8,128)(2,1)S(1)}, u32[]{:S(2)}, u32[]{:S(2)}) collective-permute-start(bf16[768,256]{1,0:T(8,128)(2,1)S(1)} %constant_dynamic-update-slice_fusion.mine_b), channel_id=1, source_target_pairs={{0,32},{32,0},{64,96},{96,64},{128,160},{160,128},{192,224},{224,1... | collective-permute-start | bytes 1179656 | tf_op jit(solution)/shard_map/ppermute | solution.py:501
  90.5 3.2 %collective-permute-start.6 = (bf16[256,256]{1,0:T(8,128)(2,1)S(1)}, bf16[256,256]{1,0:T(8,128)(2,1)S(1)}, u32[]{:S(2)}, u32[]{:S(2)}) collective-permute-start(bf16[256,256]{1,0:T(8,128)(2,1)S(1)} %reshape.11.mine_a), channel_id=1, source_target_pairs={{0,32},{32,0},{64,96},{96,64},{128,160},{160,128},{192,224},{224,1... | collective-permute-start | bytes 393224 | tf_op jit(solution)/shard_map/ppermute | solution.py:501
  95.9 9.7 %collective-permute-start.10 = (bf16[32,1408]{1,0:T(8,128)(2,1)S(1)}, bf16[32,1408]{1,0:T(8,128)(2,1)S(1)}, u32[]{:S(2)}, u32[]{:S(2)}) collective-permute-start(bf16[32,1408]{1,0:T(8,128)(2,1)S(1)} %get-tuple-element.44), channel_id=1, source_target_pairs={{0,384},{32,416},{64,448},{96,480},{128,256},{160,288},{192,320},{... | collective-permute-start | bytes 270344 | tf_op jit(solution)/shard_map/ppermute | solution.py:501
  100.6 5.7 %collective-permute-start.8 = (bf16[32,1408]{1,0:T(8,128)(2,1)S(1)}, bf16[32,1408]{1,0:T(8,128)(2,1)S(1)}, u32[]{:S(2)}, u32[]{:S(2)}) collective-permute-start(bf16[32,1408]{1,0:T(8,128)(2,1)S(1)} %get-tuple-element.42), channel_id=1, source_target_pairs={{0,128},{32,160},{64,192},{96,224},{128,0},{160,32},{192,64},{224,... | collective-permute-start | bytes 270344 | tf_op jit(solution)/shard_map/ppermute | solution.py:501
  102.5 7.1 %collective-permute-start.9 = (bf16[32,1408]{1,0:T(8,128)(2,1)S(1)}, bf16[32,1408]{1,0:T(8,128)(2,1)S(1)}, u32[]{:S(2)}, u32[]{:S(2)}) collective-permute-start(bf16[32,1408]{1,0:T(8,128)(2,1)S(1)} %get-tuple-element.43), channel_id=1, source_target_pairs={{0,256},{32,288},{64,320},{96,352},{128,384},{160,416},{192,448},{... | collective-permute-start | bytes 270344 | tf_op jit(solution)/shard_map/ppermute | solution.py:501
